TPU v7x, 32 devices: a whole 2x2x4 slice. The times are simulated.
32 devices in a mesh: dp: 8 (over z, core), fsdp: 4 (over y, x).
Axes of the slice: x: 2, y: 2, z: 4, core: 2. Of those that a mesh axis runs over, the one named last changes fastest.
Arguments:
- patches: bfloat16 [6400, 1024], P(('dp', 'fsdp')), may hold values from -6 to 6
- out_grad: bfloat16 [6400, 1024], P(('dp', 'fsdp')), may hold values from -6 to 6
- norm_gain: bfloat16 [2, 2, 1024], P(None, None, ('dp', 'fsdp')), may hold values from 0.099609375 to 1.8984375
- norm_shift: bfloat16 [2, 2, 1024], P(None, None, ('dp', 'fsdp')), may hold values from -4 to 4
- qkv_weight: bfloat16 [2, 1024, 3072], P(None, ('dp', 'fsdp')), may hold values from -0.1875 to 0.1875
- qv_bias: bfloat16 [2, 2048], P(None, ('dp', 'fsdp')), may hold values from -6 to 6
- rel_table: bfloat16 [2, 361, 32], replicated, may hold values from -6 to 6
- proj_weight: bfloat16 [2, 1024, 1024], P(None, ('dp', 'fsdp')), may hold values from -0.75 to 0.75
- proj_bias: bfloat16 [2, 1024], P(None, ('dp', 'fsdp')), may hold values from -4 to 4
- up_weight: bfloat16 [2, 1024, 4096], P(None, ('dp', 'fsdp')), may hold values from -0.1875 to 0.1875
- up_bias: bfloat16 [2, 4096], P(None, ('dp', 'fsdp')), may hold values from -6 to 6
- down_weight: bfloat16 [2, 4096, 1024], P(None, ('dp', 'fsdp')), may hold values from -0.09375 to 0.09375
- down_bias: bfloat16 [2, 1024], P(None, ('dp', 'fsdp')), may hold values from -4 to 4
- tile_perm: int32 [64], replicated, may hold values from 0 to 63, as said below
- window_slot: int32 [64], replicated, may hold values from 0 to 63, as said below
- mask_ids: int32 [64], replicated, may hold values from 0 to 3
- bias_index: int32 [100, 100], replicated, may hold values from 0 to 360, as said below
Outputs:
- block_out: bfloat16 [6400, 1024], P(('dp', 'fsdp'))
- patches_grad: float32 [6400, 1024], P(('dp', 'fsdp'))
- norm_gain_grad: float32 [2, 2, 1024], P(None, None, ('dp', 'fsdp'))
- norm_shift_grad: float32 [2, 2, 1024], P(None, None, ('dp', 'fsdp'))
- qkv_weight_grad: float32 [2, 1024, 3072], P(None, ('dp', 'fsdp'))
- qv_bias_grad: float32 [2, 2048], P(None, ('dp', 'fsdp'))
- rel_table_grad: float32 [2, 361, 32], replicated
- proj_weight_grad: float32 [2, 1024, 1024], P(None, ('dp', 'fsdp'))
- proj_bias_grad: float32 [2, 1024], P(None, ('dp', 'fsdp'))
- up_weight_grad: float32 [2, 1024, 4096], P(None, ('dp', 'fsdp'))
- up_bias_grad: float32 [2, 4096], P(None, ('dp', 'fsdp'))
- down_weight_grad: float32 [2, 4096, 1024], P(None, ('dp', 'fsdp'))
- down_bias_grad: float32 [2, 1024], P(None, ('dp', 'fsdp'))
Inputs may be any that keep to these rules, and one draw needn't show every extreme that they name: A permutation of the 64 windows; slots window_slot[w] and window_slot[tile_perm[w]] lie on devices of the same index along dp; for any two devices, at most 1 windows w held on the second have window tile_perm[w] held on the first, and some pair of devices has exactly 1. `window_slot`: a permutation of the 64 slots. `bias_index`: entry (i, j) depends only on the offset between positions i and j of the window, and different offsets have different entries.
All inputs are finite; a program needn't handle non-finite values.
Results may differ from a plain program's by a relative error of at most 0.015.
Values may be sent and summed in bfloat16 or wider, within the bound.
A program may use at most 320 MiB of HBM per device.

v0:
```python
import jax
import jax.numpy as jnp
from jax import lax
from jax.sharding import PartitionSpec as P

HEADS = 32
SIDE = 10
WIN = 100


epsilon = 1e-05
masked_score = -1000000000.0


def layer_norm(inputs, gain, shift):
    mean_value = jnp.mean(inputs, axis=-1, keepdims=True)
    centered = inputs - mean_value
    inverse = lax.rsqrt(jnp.mean(centered * centered, axis=-1, keepdims=True) + epsilon)
    normal_part = centered * inverse
    return (normal_part * gain + shift, normal_part, inverse)


def norm_back(grad_out, normal_part, inverse, gain):
    scaled = grad_out * gain
    grad_in = inverse * (
        scaled
        - jnp.mean(scaled, axis=-1, keepdims=True)
        - normal_part * jnp.mean(scaled * normal_part, axis=-1, keepdims=True)
    )
    return (grad_in, jnp.sum(grad_out * normal_part, axis=0), jnp.sum(grad_out, axis=0))


def gelu_exact(hidden):
    return jax.nn.gelu(hidden, approximate=False)


def region_mask(region_ids):
    position = jnp.arange(WIN, dtype=jnp.int32)
    cut_point = SIDE - SIDE // 2
    right_half = (position % SIDE >= cut_point).astype(jnp.int32)
    lower_half = (position // SIDE >= cut_point).astype(jnp.int32)
    labels = (
        region_ids[:, None] % 2 * right_half[None]
        + 2 * (region_ids[:, None] // 2) * lower_half[None]
    )
    same_label = labels[:, :, None] == labels[:, None, :]
    return jnp.where(same_label, 0.0, masked_score).astype(jnp.float32)[:, None]


def rank_within(device_of, windows):
    grid_view = device_of.reshape(-1, windows)
    earlier = jnp.arange(windows)[None, :] < jnp.arange(windows)[:, None]
    same_peer = grid_view[:, :, None] == grid_view[:, None, :]
    return jnp.sum(same_peer & earlier[None], axis=2).reshape(-1)


def peer_of(slot_ids, windows, peer_count):
    return slot_ids // windows % peer_count


def attention_scores(qkv_parts, position_bias, mask_add):
    head_scale = qkv_parts.shape[-1] ** (-0.5)
    scores = (
        jnp.einsum(
            "wqhd,wkhd->whqk",
            qkv_parts[:, :, 0],
            qkv_parts[:, :, 1],
            preferred_element_type=jnp.float32,
        )
        * head_scale
        + position_bias[None]
    )
    if mask_add is not None:
        scores = scores + mask_add
    return scores


def block_forward(inputs, weights, position_bias, mask_add, windows):
    norm_gains, norm_shifts, w_qkv, qv_bias, w_proj, b_proj, w_up, b_up, w_down, b_down = weights
    model_width = inputs.shape[1]
    norm_gains = norm_gains.astype(jnp.float32)
    norm_shifts = norm_shifts.astype(jnp.float32)
    normed, normal_one, inverse_one = layer_norm(inputs, norm_gains[0], norm_shifts[0])
    normed_low = normed.astype(jnp.bfloat16)
    qv_float = qv_bias.astype(jnp.float32)
    bias_full = jnp.concatenate(
        [qv_float[:model_width], jnp.zeros((model_width,), jnp.float32), qv_float[model_width:]]
    )
    qkv_low = (jnp.dot(normed_low, w_qkv, preferred_element_type=jnp.float32) + bias_full).astype(
        jnp.bfloat16
    )
    qkv_parts = qkv_low.reshape(windows, WIN, 3, HEADS, -1)
    scores = attention_scores(qkv_parts, position_bias, mask_add)
    row_max = jnp.max(scores, axis=-1, keepdims=True)
    shifted_exp = jnp.exp(scores - row_max)
    row_total = jnp.sum(shifted_exp, axis=-1, keepdims=True)
    soft_low = (shifted_exp / row_total).astype(jnp.bfloat16)
    log_total = row_max + jnp.log(row_total)
    attended = jnp.einsum(
        "whqk,wkhd->wqhd", soft_low, qkv_parts[:, :, 2], preferred_element_type=jnp.float32
    )
    attended_low = attended.reshape(inputs.shape).astype(jnp.bfloat16)
    middle = inputs + (
        jnp.dot(attended_low, w_proj, preferred_element_type=jnp.float32)
        + b_proj.astype(jnp.float32)
    )
    normed_two, normal_two, inverse_two = layer_norm(middle, norm_gains[1], norm_shifts[1])
    normed_two_low = normed_two.astype(jnp.bfloat16)
    hidden = jnp.dot(normed_two_low, w_up, preferred_element_type=jnp.float32) + b_up.astype(
        jnp.float32
    )
    activated_low = gelu_exact(hidden).astype(jnp.bfloat16)
    output = middle + (
        jnp.dot(activated_low, w_down, preferred_element_type=jnp.float32)
        + b_down.astype(jnp.float32)
    )
    kept_state = (
        normal_one,
        inverse_one,
        normed_low,
        qkv_low,
        log_total,
        attended_low,
        normal_two,
        inverse_two,
        normed_two_low,
        hidden,
        activated_low,
    )
    return (output, kept_state)


def block_backward(grad_out, weights, kept_state, position_bias, mask_add, bucket_table, windows):
    norm_gains, norm_shifts, w_qkv, qv_bias, w_proj, b_proj, w_up, b_up, w_down, b_down = weights
    (
        normal_one,
        inverse_one,
        normed_low,
        qkv_low,
        log_total,
        attended_low,
        normal_two,
        inverse_two,
        normed_two_low,
        hidden,
        activated_low,
    ) = kept_state
    model_width = grad_out.shape[1]
    norm_gains = norm_gains.astype(jnp.float32)
    grad_down_low = grad_out.astype(jnp.bfloat16)
    down_grad = jnp.einsum(
        "rf,rd->fd", activated_low, grad_down_low, preferred_element_type=jnp.float32
    )
    down_bias_grad = jnp.sum(grad_down_low, axis=0, dtype=jnp.float32)
    grad_act = jnp.einsum("rd,fd->rf", grad_down_low, w_down, preferred_element_type=jnp.float32)
    gelu_back = jax.vjp(gelu_exact, hidden)[1]
    grad_hidden_low = gelu_back(grad_act)[0].astype(jnp.bfloat16)
    up_grad = jnp.einsum(
        "rd,rf->df", normed_two_low, grad_hidden_low, preferred_element_type=jnp.float32
    )
    up_bias_grad = jnp.sum(grad_hidden_low, axis=0, dtype=jnp.float32)
    grad_normed_two = jnp.einsum(
        "rf,df->rd", grad_hidden_low, w_up, preferred_element_type=jnp.float32
    )
    grad_mid_norm, gain_two_grad, shift_two_grad = norm_back(
        grad_normed_two, normal_two, inverse_two, norm_gains[1]
    )
    grad_middle = grad_out + grad_mid_norm
    grad_branch_low = grad_middle.astype(jnp.bfloat16)
    proj_grad = jnp.einsum(
        "rc,rd->cd", attended_low, grad_branch_low, preferred_element_type=jnp.float32
    )
    proj_bias_grad = jnp.sum(grad_branch_low, axis=0, dtype=jnp.float32)
    grad_attended_low = jnp.einsum(
        "rd,cd->rc", grad_branch_low, w_proj, preferred_element_type=jnp.float32
    ).astype(jnp.bfloat16)
    qkv_parts = qkv_low.reshape(windows, WIN, 3, HEADS, -1)
    scores = attention_scores(qkv_parts, position_bias, mask_add)
    soft = jnp.exp(scores - log_total)
    soft_low = soft.astype(jnp.bfloat16)
    grad_heads = grad_attended_low.reshape(windows, WIN, HEADS, -1)
    grad_value = jnp.einsum(
        "whqk,wqhd->wkhd", soft_low, grad_heads, preferred_element_type=jnp.float32
    )
    grad_soft = jnp.einsum(
        "wqhd,wkhd->whqk", grad_heads, qkv_parts[:, :, 2], preferred_element_type=jnp.float32
    )
    grad_scores_low = (
        soft * (grad_soft - jnp.sum(soft * grad_soft, axis=-1, keepdims=True))
    ).astype(jnp.bfloat16)
    head_scale = qkv_parts.shape[-1] ** (-0.5)
    grad_query = (
        jnp.einsum(
            "whqk,wkhd->wqhd",
            grad_scores_low,
            qkv_parts[:, :, 1],
            preferred_element_type=jnp.float32,
        )
        * head_scale
    )
    grad_key = (
        jnp.einsum(
            "whqk,wqhd->wkhd",
            grad_scores_low,
            qkv_parts[:, :, 0],
            preferred_element_type=jnp.float32,
        )
        * head_scale
    )
    score_sum = jnp.sum(grad_scores_low, axis=0, dtype=jnp.float32).reshape(HEADS, -1)
    table_grad = jnp.einsum("hn,nb->bh", score_sum, bucket_table, precision=lax.Precision.HIGHEST)
    grad_qkv_low = (
        jnp.stack([grad_query, grad_key, grad_value], axis=2)
        .reshape(qkv_low.shape)
        .astype(jnp.bfloat16)
    )
    weight_qkv_grad = jnp.einsum(
        "rd,re->de", normed_low, grad_qkv_low, preferred_element_type=jnp.float32
    )
    column_sums = jnp.sum(grad_qkv_low, axis=0, dtype=jnp.float32)
    qv_grad = jnp.concatenate([column_sums[:model_width], column_sums[2 * model_width :]])
    grad_normed = jnp.einsum("re,de->rd", grad_qkv_low, w_qkv, preferred_element_type=jnp.float32)
    grad_in_norm, gain_one_grad, shift_one_grad = norm_back(
        grad_normed, normal_one, inverse_one, norm_gains[0]
    )
    grad_input = grad_middle + grad_in_norm
    grads = (
        jnp.stack([gain_one_grad, gain_two_grad]),
        jnp.stack([shift_one_grad, shift_two_grad]),
        weight_qkv_grad,
        qv_grad,
        proj_grad,
        proj_bias_grad,
        up_grad,
        up_bias_grad,
        down_grad,
        down_bias_grad,
    )
    return (grad_input, grads, table_grad)


def shards(
    patches,
    out_grad,
    norm_gain,
    norm_shift,
    qkv_weight,
    qv_bias,
    rel_table,
    proj_weight,
    proj_bias,
    up_weight,
    up_bias,
    down_weight,
    down_bias,
    tile_perm,
    window_slot,
    mask_ids,
    bias_index,
):
    windows = patches.shape[0] // WIN
    model_width = patches.shape[1]
    peer_count = lax.axis_size("fsdp")
    capacity = (windows + peer_count - 1) // peer_count
    device_index = lax.axis_index(("dp", "fsdp"))
    total_windows = tile_perm.shape[0]
    slot_ids = jnp.arange(total_windows, dtype=jnp.int32)
    source_of = jnp.zeros((total_windows,), jnp.int32).at[window_slot].set(window_slot[tile_perm])
    target_of = jnp.zeros((total_windows,), jnp.int32).at[source_of].set(slot_ids)
    region_slot = jnp.zeros((total_windows,), jnp.int32).at[window_slot].set(mask_ids)
    own_slots = device_index * windows + jnp.arange(windows, dtype=jnp.int32)
    forward_rank = rank_within(target_of // windows, windows)
    backward_rank = rank_within(source_of // windows, windows)
    own_source = source_of[own_slots]
    own_target = target_of[own_slots]
    forward_send = peer_of(own_target, windows, peer_count) * capacity + forward_rank[own_slots]
    forward_take = peer_of(own_source, windows, peer_count) * capacity + forward_rank[own_source]
    backward_send = peer_of(own_source, windows, peer_count) * capacity + backward_rank[own_slots]
    backward_take = peer_of(own_target, windows, peer_count) * capacity + backward_rank[own_target]
    mask_add = region_mask(region_slot[own_slots])
    bucket_table = (
        bias_index.reshape(-1)[:, None] == jnp.arange(rel_table.shape[1], dtype=jnp.int32)[None, :]
    ).astype(jnp.float32)
    tables = rel_table.astype(jnp.float32)
    bias_one = jnp.einsum(
        "nb,bh->hn", bucket_table, tables[0], precision=lax.Precision.HIGHEST
    ).reshape(HEADS, WIN, WIN)
    bias_two = jnp.einsum(
        "nb,bh->hn", bucket_table, tables[1], precision=lax.Precision.HIGHEST
    ).reshape(HEADS, WIN, WIN)

    def to_shifted(rows_low):
        sectioning = (
            jnp.zeros((peer_count * capacity, WIN, model_width), rows_low.dtype)
            .at[forward_send]
            .set(rows_low.reshape(windows, WIN, model_width))
        )
        arrived = lax.all_to_all(sectioning, "fsdp", split_axis=0, concat_axis=0, tiled=True)
        return arrived[forward_take].reshape(rows_low.shape)

    def from_shifted(rows_low):
        sectioning = (
            jnp.zeros((peer_count * capacity, WIN, model_width), rows_low.dtype)
            .at[backward_send]
            .set(rows_low.reshape(windows, WIN, model_width))
        )
        arrived = lax.all_to_all(sectioning, "fsdp", split_axis=0, concat_axis=0, tiled=True)
        return arrived[backward_take].reshape(rows_low.shape)

    def fetch_forward(layer_index):
        return (
            lax.all_gather(norm_gain[layer_index], ("dp", "fsdp"), axis=1, tiled=True),
            lax.all_gather(norm_shift[layer_index], ("dp", "fsdp"), axis=1, tiled=True),
            lax.all_gather(qkv_weight[layer_index], ("dp", "fsdp"), axis=0, tiled=True),
            lax.all_gather(qv_bias[layer_index], ("dp", "fsdp"), axis=0, tiled=True),
            lax.all_gather(proj_weight[layer_index], ("dp", "fsdp"), axis=0, tiled=True),
            lax.all_gather(proj_bias[layer_index], ("dp", "fsdp"), axis=0, tiled=True),
            lax.all_gather(up_weight[layer_index], ("dp", "fsdp"), axis=0, tiled=True),
            lax.all_gather(up_bias[layer_index], ("dp", "fsdp"), axis=0, tiled=True),
            lax.all_gather(down_weight[layer_index], ("dp", "fsdp"), axis=0, tiled=True),
            lax.all_gather(down_bias[layer_index], ("dp", "fsdp"), axis=0, tiled=True),
        )

    def fetch_backward(layer_index):
        return (
            lax.all_gather(norm_gain[layer_index], ("dp", "fsdp"), axis=1, tiled=True),
            lax.all_gather(norm_shift[layer_index], ("dp", "fsdp"), axis=1, tiled=True),
            lax.all_gather(qkv_weight[layer_index], ("dp", "fsdp"), axis=0, tiled=True),
            lax.all_gather(qv_bias[layer_index], ("dp", "fsdp"), axis=0, tiled=True),
            lax.all_gather(proj_weight[layer_index], ("dp", "fsdp"), axis=0, tiled=True),
            lax.all_gather(proj_bias[layer_index], ("dp", "fsdp"), axis=0, tiled=True),
            lax.all_gather(up_weight[layer_index], ("dp", "fsdp"), axis=0, tiled=True),
            lax.all_gather(up_bias[layer_index], ("dp", "fsdp"), axis=0, tiled=True),
            lax.all_gather(down_weight[layer_index], ("dp", "fsdp"), axis=0, tiled=True),
            lax.all_gather(down_bias[layer_index], ("dp", "fsdp"), axis=0, tiled=True),
        )

    def reduce_grads(grads):
        return (
            lax.psum_scatter(grads[0], ("dp", "fsdp"), scatter_dimension=1, tiled=True),
            lax.psum_scatter(grads[1], ("dp", "fsdp"), scatter_dimension=1, tiled=True),
            lax.psum_scatter(grads[2], ("dp", "fsdp"), scatter_dimension=0, tiled=True),
            lax.psum_scatter(grads[3], ("dp", "fsdp"), scatter_dimension=0, tiled=True),
            lax.psum_scatter(grads[4], ("dp", "fsdp"), scatter_dimension=0, tiled=True),
            lax.psum_scatter(grads[5], ("dp", "fsdp"), scatter_dimension=0, tiled=True),
            lax.psum_scatter(grads[6], ("dp", "fsdp"), scatter_dimension=0, tiled=True),
            lax.psum_scatter(grads[7], ("dp", "fsdp"), scatter_dimension=0, tiled=True),
            lax.psum_scatter(grads[8], ("dp", "fsdp"), scatter_dimension=0, tiled=True),
            lax.psum_scatter(grads[9], ("dp", "fsdp"), scatter_dimension=0, tiled=True),
        )

    first_weights = fetch_forward(0)
    output_one, state_one = block_forward(
        patches.astype(jnp.float32), first_weights, bias_one, None, windows
    )
    second_input = to_shifted(output_one.astype(jnp.bfloat16))
    second_weights = fetch_forward(1)
    output_two, state_two = block_forward(
        second_input.astype(jnp.float32), second_weights, bias_two, mask_add, windows
    )
    block_out = from_shifted(output_two.astype(jnp.bfloat16))
    grad_two = to_shifted(out_grad)
    back_two = fetch_backward(1)
    grad_input_two, grads_two, table_two = block_backward(
        grad_two.astype(jnp.float32), back_two, state_two, bias_two, mask_add, bucket_table, windows
    )
    shards_two = reduce_grads(grads_two)
    grad_one = from_shifted(grad_input_two.astype(jnp.bfloat16))
    back_one = fetch_backward(0)
    grad_patches, grads_one, table_one = block_backward(
        grad_one.astype(jnp.float32), back_one, state_one, bias_one, None, bucket_table, windows
    )
    shards_one = reduce_grads(grads_one)
    stacked = [jnp.stack([shards_one[member], shards_two[member]]) for member in range(10)]
    table_total = lax.psum(jnp.stack([table_one, table_two]), ("dp", "fsdp"))
    return (
        block_out,
        grad_patches,
        stacked[0],
        stacked[1],
        stacked[2],
        stacked[3],
        table_total,
        stacked[4],
        stacked[5],
        stacked[6],
        stacked[7],
        stacked[8],
        stacked[9],
    )


def solution(mesh):
    placed = (
        P(("dp", "fsdp"), None),
        P(("dp", "fsdp"), None),
        P(None, None, ("dp", "fsdp")),
        P(None, None, ("dp", "fsdp")),
        P(None, ("dp", "fsdp"), None),
        P(None, ("dp", "fsdp")),
        P(),
        P(None, ("dp", "fsdp"), None),
        P(None, ("dp", "fsdp")),
        P(None, ("dp", "fsdp"), None),
        P(None, ("dp", "fsdp")),
        P(None, ("dp", "fsdp"), None),
        P(None, ("dp", "fsdp")),
        P(),
        P(),
        P(),
        P(),
    )
    return jax.shard_map(
        shards,
        mesh=mesh,
        in_specs=placed,
        out_specs=(
            P(("dp", "fsdp"), None),
            P(("dp", "fsdp"), None),
            P(None, None, ("dp", "fsdp")),
            P(None, None, ("dp", "fsdp")),
            P(None, ("dp", "fsdp"), None),
            P(None, ("dp", "fsdp")),
            P(),
            P(None, ("dp", "fsdp"), None),
            P(None, ("dp", "fsdp")),
            P(None, ("dp", "fsdp"), None),
            P(None, ("dp", "fsdp")),
            P(None, ("dp", "fsdp"), None),
            P(None, ("dp", "fsdp")),
        ),
        check_vma=False,
    )
```

profile of v0, /device:TPU:0, one launch (start us, length us, event | category | flops | bytes accessed | tf_op | source)
XLA Modules:
  0.0 3558.2 jit_solution(9657178917296029269)
XLA Ops:
  34.0 46.7 %all-reduce.15 = (bf16[2048]{0:T(1024)(128)(2,1)S(1)}, bf16[1024]{0:T(1024)(128)(2,1)S(1)}, bf16[1024]{0:T(1024)(128)(2,1)S(1)}, bf16[2048]{0:T(1024)(128)(2,1)S...) all-reduce(bf16[2048]{0:T(1024)(128)(2,1)S(1)} %dynamic-update-slic, ...), channel_id=5, replica_groups=mesh['dp'=8,'fsdp'=4] {'dp','fsdp'}, use_global_device_ids=true, to_apply=%add | all-reduce | flops 8192 | bytes 32768
  80.8 69.4 %all-gather = bf16[1,2,1024]{1,0,2:T(2,128)(2,1)S(1)} all-gather(bf16[1,2,32]{1,0,2:T(2,128)(2,1)S(1)} %copy.202), channel_id=2, replica_groups=mesh['dp'=8,'fsdp'=4] {'dp','fsdp'}, dimensions={2}, use_global_device_ids=true | all-gather | bytes 4224 | tf_op jit(solution)/shard_map/all_gather | solution.py:312
  151.4 68.8 %all-gather.1 = bf16[1,2,1024]{1,0,2:T(2,128)(2,1)S(1)} all-gather(bf16[1,2,32]{1,0,2:T(2,128)(2,1)S(1)} %copy.203), channel_id=3, replica_groups=mesh['dp'=8,'fsdp'=4] {'dp','fsdp'}, dimensions={2}, use_global_device_ids=true | all-gather | bytes 4224 | tf_op jit(solution)/shard_map/all_gather | solution.py:313
  232.0 65.4 %all-gather.7 = bf16[1,4096]{1,0:T(2,128)(2,1)S(1)} all-gather(bf16[1,128]{1,0:T(2,128)(2,1)S(1)} %get-tuple-element.100), channel_id=9, replica_groups=mesh['dp'=8,'fsdp'=4] {'dp','fsdp'}, dimensions={1}, use_global_device_ids=true | all-gather | bytes 8448 | tf_op jit(solution)/shard_map/all_gather | solution.py:319
  298.2 68.0 %all-gather.10 = bf16[1,2,1024]{1,0,2:T(2,128)(2,1)S(1)} all-gather(bf16[1,2,32]{1,0,2:T(2,128)(2,1)S(1)} %copy.207), channel_id=12, replica_groups=mesh['dp'=8,'fsdp'=4] {'dp','fsdp'}, dimensions={2}, use_global_device_ids=true | all-gather | bytes 4224 | tf_op jit(solution)/shard_map/all_gather | solution.py:312
  383.8 7.2 slice_reduce_fusion.1
  417.1 13.6 multiply_convert_fusion.3
  447.7 73.4 %all-gather.11 = bf16[1,2,1024]{1,0,2:T(2,128)(2,1)S(1)} all-gather(bf16[1,2,32]{1,0,2:T(2,128)(2,1)S(1)} %copy.208), channel_id=13, replica_groups=mesh['dp'=8,'fsdp'=4] {'dp','fsdp'}, dimensions={2}, use_global_device_ids=true | all-gather | bytes 4224 | tf_op jit(solution)/shard_map/all_gather | solution.py:313
  528.8 63.9 %all-gather.17 = bf16[1,4096]{1,0:T(2,128)(2,1)S(1)} all-gather(bf16[1,128]{1,0:T(2,128)(2,1)S(1)} %copy-done.93), channel_id=19, replica_groups=mesh['dp'=8,'fsdp'=4] {'dp','fsdp'}, dimensions={1}, use_global_device_ids=true | all-gather | bytes 8448 | tf_op jit(solution)/shard_map/all_gather | solution.py:319
  593.3 8.0 slice_reduce_fusion
  645.0 13.6 multiply_convert_fusion.2
  658.6 9.8 convert_reduce_fusion.2
  727.4 9.7 convert_reduce_fusion.3
  738.3 7.1 multiply_reduce_fusion.5
  786.0 7.8 fusion.218
  802.9 9.7 fusion.198
  813.8 9.7 fusion.197
  824.5 9.6 fusion.220
  835.1 9.6 fusion.219
  871.4 110.8 %reduce-scatter.39.cloned.1.call-done = f32[32,2]{1,0:T(8,128)} async-done(((f32[1024,2]{1,0:T(8,128)}), f32[32,2]{1,0:T(8,128)}) %reduce-scatter.39.cloned.1.call-update) | async-done | bytes 272
  998.9 115.4 %reduce-scatter.41.cloned.1.call-done = f32[32,2]{1,0:T(8,128)} async-done(((f32[1024,2]{1,0:T(8,128)}), f32[32,2]{1,0:T(8,128)}) %reduce-scatter.41.cloned.1.call-update) | async-done | bytes 272
  1115.1 131.7 %reduce-scatter.37.cloned.1.call-done = f32[32,2]{1,0:T(8,128)} async-done(((f32[1024,2]{1,0:T(8,128)}), f32[32,2]{1,0:T(8,128)}) %reduce-scatter.37.cloned.1.call-update) | async-done | bytes 272
  1248.7 121.4 %all-reduce.21.cloned.1.call-done = (f32[2048]{0:T(1024)}, f32[2048]{0:T(1024)}, f32[1024]{0:T(1024)}, f32[1024]{0:T(1024)}, f32[4096]{0:T(1024)}, /*index=5*/f32[4096]{0:T(1024)}, f32[1024]{0:T(1024)}, f32[1024]{0:T(1024)}) async-done(((f32[2048]{0:T(1024)}, f32[2048]{0:T(1024)}, f32[1024]{0:T(1024)}, f32[1024]{0:T(1024)}, f32[4096]{0:T(1024)}, /*index=5*/f32[4096]{0:T(1024)}, f32[1024]{0:T(1024)}, ...) | async-done | bytes 65552
  1378.4 136.7 %reduce-scatter.27.cloned.1.call-done = f32[32,1024]{1,0:T(8,128)} async-done(((f32[1024,1024]{1,0:T(8,128)}), f32[32,1024]{1,0:T(8,128)}) %reduce-scatter.27.cloned.1.call-update) | async-done | bytes 131088 | tf_op jit(solution)/shard_map/reduce_scatter | solution.py:344
  1515.1 141.6 %reduce-scatter.25.cloned.1.call-done = f32[32,1024]{1,0:T(8,128)} async-done(((f32[1024,1024]{1,0:T(8,128)}), f32[32,1024]{1,0:T(8,128)}) %reduce-scatter.25.cloned.1.call-update) | async-done | bytes 131088 | tf_op jit(solution)/shard_map/reduce_scatter | solution.py:344
  1658.4 158.0 %reduce-scatter.23.cloned.1.call-done = f32[32,3072]{1,0:T(8,128)} async-done(((f32[1024,3072]{1,0:T(8,128)}), f32[32,3072]{1,0:T(8,128)}) %reduce-scatter.23.cloned.1.call-update) | async-done | bytes 393232 | tf_op jit(solution)/shard_map/reduce_scatter | solution.py:342
  1816.4 161.7 %reduce-scatter.21.cloned.1.call-done = f32[32,3072]{1,0:T(8,128)} async-done(((f32[1024,3072]{1,0:T(8,128)}), f32[32,3072]{1,0:T(8,128)}) %reduce-scatter.21.cloned.1.call-update) | async-done | bytes 393232 | tf_op jit(solution)/shard_map/reduce_scatter | solution.py:342
  1980.2 356.8 %reduce-scatter.31.cloned.1.call-done = f32[32,4096]{1,0:T(8,128)} async-done(((f32[1024,4096]{1,0:T(8,128)}), f32[32,4096]{1,0:T(8,128)}) %reduce-scatter.31.cloned.1.call-update) | async-done | bytes 524304 | tf_op jit(solution)/shard_map/reduce_scatter | solution.py:346
  2337.0 361.4 %reduce-scatter.29.cloned.1.call-done = f32[32,4096]{1,0:T(8,128)} async-done(((f32[1024,4096]{1,0:T(8,128)}), f32[32,4096]{1,0:T(8,128)}) %reduce-scatter.29.cloned.1.call-update) | async-done | bytes 524304 | tf_op jit(solution)/shard_map/reduce_scatter | solution.py:346
  2700.7 359.0 %reduce-scatter.35.cloned.1.call-done = f32[128,1024]{1,0:T(8,128)} async-done(((f32[4096,1024]{1,0:T(8,128)}), f32[128,1024]{1,0:T(8,128)}) %reduce-scatter.35.cloned.1.call-update) | async-done | bytes 524304 | tf_op jit(solution)/shard_map/reduce_scatter | solution.py:348
  3059.7 361.4 %reduce-scatter.33.cloned.1.call-done = f32[128,1024]{1,0:T(8,128)} async-done(((f32[4096,1024]{1,0:T(8,128)}), f32[128,1024]{1,0:T(8,128)}) %reduce-scatter.33.cloned.1.call-update) | async-done | bytes 524304 | tf_op jit(solution)/shard_map/reduce_scatter | solution.py:348
  3423.4 125.9 %all-reduce.19.cloned.1.call-done = f32[2,361,32]{1,2,0:T(8,128)} async-done(((f32[2,361,32]{1,2,0:T(8,128)}), f32[2,361,32]{1,2,0:T(8,128)}) %all-reduce.19.cloned.1.call-update) | async-done | bytes 92432 | tf_op jit(solution)/shard_map/psum | solution.py:375
  (501 shorter events, 329.1 us)
Async XLA Ops:
  7.2 390.4 %all-gather.29.cloned.1.call-start = ((), (), s32[]{:S(2)}) async-start(), calls=%async_computation.25 | async-start | bytes 6488064 | tf_op jit(solution)/shard_map/all_gather | solution.py:314
  9.1 404.2 %all-gather.31.cloned.1.call-start = ((), (), s32[]{:S(2)}) async-start(), calls=%async_computation.26 | async-start | bytes 2162688 | tf_op jit(solution)/shard_map/all_gather | solution.py:316
  10.7 406.3 %all-gather.33.cloned.1.call-start = ((), (), s32[]{:S(2)}) async-start(), calls=%async_computation.27 | async-start | bytes 8650752 | tf_op jit(solution)/shard_map/all_gather | solution.py:318
  12.6 418.1 %all-gather.35.cloned.1.call-start = ((), (), s32[]{:S(2)}) async-start(), calls=%async_computation.28 | async-start | bytes 8650752 | tf_op jit(solution)/shard_map/all_gather | solution.py:320
  14.6 604.5 %all-gather.37.cloned.1.call-start = ((), (), s32[]{:S(2)}) async-start(), calls=%async_computation.29 | async-start | bytes 6488064 | tf_op jit(solution)/shard_map/all_gather | solution.py:314
  15.2 625.4 %all-gather.39.cloned.1.call-start = ((), (), s32[]{:S(2)}) async-start(), calls=%async_computation.30 | async-start | bytes 2162688 | tf_op jit(solution)/shard_map/all_gather | solution.py:316
  15.7 629.2 %all-gather.41.cloned.1.call-start = ((), (), s32[]{:S(2)}) async-start(), calls=%async_computation.31 | async-start | bytes 8650752 | tf_op jit(solution)/shard_map/all_gather | solution.py:318
  21.1 59.6 %copy-start.94 = (bf16[2,2,32]{2,1,0:T(2,128)(2,1)S(1)}, bf16[2,2,32]{2,1,0:T(2,128)(2,1)}, u32[]{:S(2)}) copy-start(bf16[2,2,32]{2,1,0:T(2,128)(2,1)} %param.19) | copy-start | bytes 772
  21.9 128.8 %copy-start.95 = (bf16[2,2,32]{2,1,0:T(2,128)(2,1)S(1)}, bf16[2,2,32]{2,1,0:T(2,128)(2,1)}, u32[]{:S(2)}) copy-start(bf16[2,2,32]{2,1,0:T(2,128)(2,1)} %param.20) | copy-start | bytes 772
  25.3 195.4 %copy-start.58 = (s32[100,100]{1,0:T(8,128)S(1)}, s32[100,100]{1,0:T(8,128)}, u32[]{:S(2)}) copy-start(s32[100,100]{1,0:T(8,128)} %param.33) | copy-start | bytes 120004
  25.3 195.5 %copy-start.97 = (bf16[2,361,32]{1,2,0:T(8,128)(2,1)S(1)}, bf16[2,361,32]{1,2,0:T(8,128)(2,1)}, u32[]{:S(2)}) copy-start(bf16[2,361,32]{1,2,0:T(8,128)(2,1)} %param.23) | copy-start | bytes 138628
  25.3 417.5 %all-to-all-start.2 = ((bf16[4,100,1024]{2,1,0:T(8,128)(2,1)}), bf16[4,100,1024]{2,1,0:T(8,128)(2,1)}, u32[]{:S(2)}, u32[]{:S(2)}) async-start(bf16[4,100,1024]{2,1,0:T(8,128)(2,1)} %scatter_fusion.2), calls=%async_computation.2 | async-start | bytes 1703936 | tf_op jit(solution)/shard_map/all_to_all | solution.py:298
  30.6 628.0 %all-gather.43.cloned.1.call-start = ((), (), s32[]{:S(2)}) async-start(), calls=%async_computation.32 | async-start | bytes 8650752 | tf_op jit(solution)/shard_map/all_gather | solution.py:320
  220.8 170.1 %copy-start.59 = (s32[10000]{0:T(1024)}, s32[10000]{0:T(1024)S(1)}, u32[]{:S(2)}) copy-start(s32[10000]{0:T(1024)S(1)} %eq.79) | copy-start | bytes 120004
  229.8 140.5 %copy-start.14 = (bf16[200,1024]{1,0:T(8,128)(2,1)S(1)}, bf16[200,1024]{1,0:T(8,128)(2,1)}, u32[]{:S(2)}) copy-start(bf16[200,1024]{1,0:T(8,128)(2,1)} %param.17) | copy-start | bytes 1228804
  442.8 165.5 %all-to-all-start = ((bf16[4,100,1024]{2,1,0:T(8,128)(2,1)}), bf16[4,100,1024]{2,1,0:T(8,128)(2,1)}, u32[]{:S(2)}, u32[]{:S(2)}) async-start(bf16[4,100,1024]{2,1,0:T(8,128)(2,1)} %scatter_fusion), calls=%async_computation | async-start | bytes 1703936 | tf_op jit(solution)/shard_map/all_to_all | solution.py:298
  710.2 12.7 all-to-all-start.3
  714.5 156.1 %reduce-scatter.43.cloned.1.call-start = ((), (), s32[]{:S(2)}) async-start(), calls=%async_computation.36 | async-start | bytes 540672
  715.6 266.5 %reduce-scatter.39.cloned.1.call-start = ((), (), s32[]{:S(2)}) async-start(), calls=%async_computation.34 | async-start | bytes 540672
  717.6 396.7 %reduce-scatter.41.cloned.1.call-start = ((), (), s32[]{:S(2)}) async-start(), calls=%async_computation.35 | async-start | bytes 540672
  775.7 471.0 %reduce-scatter.37.cloned.1.call-start = ((), (), s32[]{:S(2)}) async-start(), calls=%async_computation.33 | async-start | bytes 540672
  777.0 593.1 %all-reduce.21.cloned.1.call-start = ((), (), s32[]{:S(2)}) async-start(), calls=%async_computation.37 | async-start | bytes 131072
  777.8 737.4 %reduce-scatter.27.cloned.1.call-start = ((), (), s32[]{:S(2)}) async-start(), calls=%async_computation.20 | async-start | bytes 4325376 | tf_op jit(solution)/shard_map/reduce_scatter | solution.py:344
  780.5 876.2 %reduce-scatter.25.cloned.1.call-start = ((), (), s32[]{:S(2)}) async-start(), calls=%async_computation.19 | async-start | bytes 4325376 | tf_op jit(solution)/shard_map/reduce_scatter | solution.py:344
  784.6 1031.8 %reduce-scatter.23.cloned.1.call-start = ((), (), s32[]{:S(2)}) async-start(), calls=%async_computation.17 | async-start | bytes 12976128 | tf_op jit(solution)/shard_map/reduce_scatter | solution.py:342
  793.8 1184.4 %reduce-scatter.21.cloned.1.call-start = ((), (), s32[]{:S(2)}) async-start(), calls=%async_computation.16 | async-start | bytes 12976128 | tf_op jit(solution)/shard_map/reduce_scatter | solution.py:342
  801.8 1535.3 %reduce-scatter.31.cloned.1.call-start = ((), (), s32[]{:S(2)}) async-start(), calls=%async_computation.22 | async-start | bytes 17301504 | tf_op jit(solution)/shard_map/reduce_scatter | solution.py:346
  812.7 1885.8 %reduce-scatter.29.cloned.1.call-start = ((), (), s32[]{:S(2)}) async-start(), calls=%async_computation.21 | async-start | bytes 17301504 | tf_op jit(solution)/shard_map/reduce_scatter | solution.py:346
  823.6 2236.1 %reduce-scatter.35.cloned.1.call-start = ((), (), s32[]{:S(2)}) async-start(), calls=%async_computation.24 | async-start | bytes 17301504 | tf_op jit(solution)/shard_map/reduce_scatter | solution.py:348
  834.1 2587.0 %reduce-scatter.33.cloned.1.call-start = ((), (), s32[]{:S(2)}) async-start(), calls=%async_computation.23 | async-start | bytes 17301504 | tf_op jit(solution)/shard_map/reduce_scatter | solution.py:348
  854.6 134.3 %all-to-all-start.1 = ((bf16[4,100,1024]{2,1,0:T(8,128)(2,1)}), bf16[4,100,1024]{2,1,0:T(8,128)(2,1)S(1)}, u32[]{:S(2)}, u32[]{:S(2)}) async-start(bf16[4,100,1024]{2,1,0:T(8,128)(2,1)} %scatter_fusion.1), calls=%async_computation.1 | async-start | bytes 1703936 | tf_op jit(solution)/shard_map/all_to_all | solution.py:307
  858.3 2691.0 %all-reduce.19.cloned.1.call-start = ((), (), s32[]{:S(2)}) async-start(), calls=%async_computation.18 | async-start | bytes 196608 | tf_op jit(solution)/shard_map/psum | solution.py:375
  (93 other events, 572.3 us)
Sparse Core Ops, SparseCore 0:
  11.5 73.8 all-gather.28
  88.8 55.9 all-gather.30
  148.3 78.3 all-gather.32
  230.0 80.8 all-gather.34
  313.6 69.0 all-gather.36
  386.0 55.2 all-gather.38
  444.7 78.6 all-gather.40
  526.2 77.7 all-gather.42
  717.5 132.6 reduce-scatter.42
  852.4 129.7 reduce-scatter.38
  984.4 129.8 reduce-scatter.40
  1117.1 129.6 reduce-scatter.36
  1253.8 116.3 all-reduce.20
  1372.3 142.8 reduce-scatter.26
  1517.3 139.4 reduce-scatter.24
  1662.6 153.7 reduce-scatter.22
  1823.3 154.7 reduce-scatter.20
  1980.3 356.6 reduce-scatter.30
  2339.3 359.0 reduce-scatter.28
  2700.6 359.0 reduce-scatter.34
  3062.0 359.0 reduce-scatter.32
  3427.2 122.0 all-reduce.18
where the time goes:
time: 3570 us; the launch traced here: 3560 us
  waiting for transfers between devices  2650 us (74%)
  blocking collectives  456 us (13%)
  matrix products  201 us (6%)
  local copies, waits for them, and re-layouts  175 us (5%)
  other arithmetic  42 us (1%)
    reduce_scatter x2, waiting for transfers between devices, reduce_grads(): lax.psum_scatter(grads[8], ('dp', 'fsdp'), scatter_dimension=0, tiled=True)  720 us
    reduce_scatter x2, waiting for transfers between devices, reduce_grads(): lax.psum_scatter(grads[6], ('dp', 'fsdp'), scatter_dimension=0, tiled=True)  718 us
    unnamed x27, waiting for transfers between devices  482 us
    reduce_scatter x2, waiting for transfers between devices, reduce_grads(): lax.psum_scatter(grads[2], ('dp', 'fsdp'), scatter_dimension=0, tiled=True)  320 us
    reduce_scatter x2, waiting for transfers between devices, reduce_grads(): lax.psum_scatter(grads[4], ('dp', 'fsdp'), scatter_dimension=0, tiled=True)  278 us
    all_gather x2, blocking collectives, fetch_forward(): lax.all_gather(norm_shift[layer_index], ('dp', 'fsdp'), axis=1, tiled=True)  142 us
    all_gather x2, blocking collectives, fetch_forward(): lax.all_gather(norm_gain[layer_index], ('dp', 'fsdp'), axis=1, tiled=True)  137 us
    all_gather x2, blocking collectives, fetch_forward(): lax.all_gather(up_bias[layer_index], ('dp', 'fsdp'), axis=0, tiled=True)  129 us
  transfers between devices with their start and end apart: 26, of which 14 were waited for; matrix products, arithmetic and copies ran while one was open for 10% of the time, Pallas kernels for 0%

commit v1 on v0

v1 whole, which is shorter than its diff:
```python
import functools

import jax
import jax.numpy as jnp
from jax import lax
from jax.experimental import pallas as pl
from jax.experimental.pallas import tpu as pltpu
from jax.sharding import PartitionSpec as P

HEADS = 32
SIDE = 10
WIN = 100


epsilon = 1e-05
masked_score = -1000000000.0


def layer_norm(inputs, gain, shift):
    mean_value = jnp.mean(inputs, axis=-1, keepdims=True)
    centered = inputs - mean_value
    inverse = lax.rsqrt(jnp.mean(centered * centered, axis=-1, keepdims=True) + epsilon)
    normal_part = centered * inverse
    return (normal_part * gain + shift, normal_part, inverse)


def norm_back(grad_out, normal_part, inverse, gain):
    scaled = grad_out * gain
    grad_in = inverse * (
        scaled
        - jnp.mean(scaled, axis=-1, keepdims=True)
        - normal_part * jnp.mean(scaled * normal_part, axis=-1, keepdims=True)
    )
    return (grad_in, jnp.sum(grad_out * normal_part, axis=0), jnp.sum(grad_out, axis=0))


def gelu_exact(hidden):
    return jax.nn.gelu(hidden, approximate=False)


def region_mask(region_ids):
    position = jnp.arange(WIN, dtype=jnp.int32)
    cut_point = SIDE - SIDE // 2
    right_half = (position % SIDE >= cut_point).astype(jnp.int32)
    lower_half = (position // SIDE >= cut_point).astype(jnp.int32)
    labels = (
        region_ids[:, None] % 2 * right_half[None]
        + 2 * (region_ids[:, None] // 2) * lower_half[None]
    )
    same_label = labels[:, :, None] == labels[:, None, :]
    return jnp.where(same_label, 0.0, masked_score).astype(jnp.float32)[:, None]


MESH = pl.DeviceIdType.MESH
ANY = pl.BlockSpec(memory_space=pl.ANY)
VMEM = pl.BlockSpec(memory_space=pltpu.VMEM)
WIDE = 1024
LOOK = 2


def ring_position(peer, peers):
    column, row = lax.rem(peer, 2), lax.div(peer, 2)
    return column * (peers - 1 - row) + (1 - column) * row


def ring_member(place, peers):
    place = lax.rem(place + peers, peers)
    far = lax.div(place, peers // 2)
    return (1 - far) * 2 * place + far * (2 * (peers - 1 - place) + 1)


class Place:
    def __init__(self, depths, peers):
        self.depths, self.peers, self.half = depths, peers, peers // 2
        outer = lax.axis_index("dp")
        self.depth, self.core = lax.div(outer, 2), lax.rem(outer, 2)
        self.peer = lax.axis_index("fsdp")
        self.spot = ring_position(self.peer, peers)
        self.index = outer * peers + self.peer
        self.total = depths * 2 * peers

    def sibling(self):
        return (self.depth * 2 + 1 - self.core, self.peer)

    def around(self, step):
        return ring_member(self.spot + step, self.peers)

    def neighbour(self, step):
        return (self.depth * 2 + self.core, self.around(step))

    def at_depth(self, step):
        return lax.rem(self.depth + step + self.depths, self.depths)

    def deep(self, step):
        return (self.at_depth(step) * 2 + self.core, self.peer)

    def other(self, step):
        index = lax.rem(self.index + step, self.total)
        return (lax.div(index, self.peers), lax.rem(index, self.peers))

    def greet(self):
        barrier = pltpu.get_barrier_semaphore()

        def signal(step, carry):
            pl.semaphore_signal(barrier, inc=1, device_id=self.other(step), device_id_type=MESH)
            return carry

        lax.fori_loop(1, self.total, signal, 0)
        pl.semaphore_wait(barrier, self.total - 1)

    def greet_near(self):
        barrier = pltpu.get_barrier_semaphore()
        near = [self.sibling(), self.neighbour(1), self.neighbour(-1)]
        near += [self.deep(step) for step in range(1, self.depths)]
        for device in near:
            pl.semaphore_signal(barrier, inc=1, device_id=device, device_id_type=MESH)
        pl.semaphore_wait(barrier, len(near))


def remote(source, target, send, receive, device):
    return pltpu.make_async_remote_copy(
        src_ref=source,
        dst_ref=target,
        send_sem=send,
        recv_sem=receive,
        device_id=device,
        device_id_type=MESH,
    )


class Spread:
    def __init__(self, place, source, target, send, receive, local):
        self.place, self.source, self.target = place, source, target
        self.send, self.receive, self.local = send, receive, local

    def own(self):
        return pltpu.make_async_copy(self.source, self.target.at[self.place.index], self.local)

    def start(self):
        def copy(step, carry):
            remote(
                self.source,
                self.target.at[self.place.index],
                self.send,
                self.receive,
                self.place.other(step),
            ).start()
            return carry

        lax.fori_loop(1, self.place.total, copy, 0)
        self.own().start()

    def wait(self):
        rest = self.target.at[pl.ds(0, self.place.total - 1)]
        both = remote(rest, rest, self.send, self.receive, self.place.other(1))
        both.wait_send()
        both.wait_recv()
        self.own().wait()


def gather_kernel(chunks, depths, peers, count, *refs):
    blocks, small = refs[:count], refs[count]
    fulls, small_full = refs[count + 1 : 2 * count + 1], refs[2 * count + 1]
    (z_send, z_recv, r_send, r_recv, c_send, c_recv, own_sem, s_send, s_recv, s_own) = refs[
        2 * count + 2 :
    ]
    place = Place(depths, peers)
    half = place.half
    core, cut = place.core, depths // 2

    def view(i, depth, peer):
        array, layer, rows, columns = chunks[i]
        return fulls[array].at[depth, core, peer, rows, columns]

    def block(i):
        array, layer, rows, columns = chunks[i]
        return blocks[array].at[layer, rows, columns]

    def own(i):
        return pltpu.make_async_copy(block(i), view(i, place.depth, place.peer), own_sem.at[i])

    def deep(i, step):
        return remote(
            block(i),
            view(i, place.depth, place.peer),
            z_send.at[i, step - 1],
            z_recv.at[i, step - 1],
            place.deep(step),
        )

    def part(step, way):
        if step < half:
            return slice(None)
        return slice(0, cut) if way == 0 else slice(cut, depths)

    def ring(i, step, way):
        turn = 1 if way == 0 else -1
        here = view(i, part(step, way), place.around(-turn * (step - 1)))
        return remote(
            here,
            here,
            r_send.at[i, step - 1, way],
            r_recv.at[i, step - 1, way],
            place.neighbour(turn),
        )

    def across(i, slot):
        step = (slot + 1) // 2
        turn = 1 if slot % 2 else -1
        here = view(i, slice(None), place.around(-turn * step))
        return remote(here, here, c_send.at[i, slot], c_recv.at[i, slot], place.sibling())

    slots = 2 * half
    total = len(chunks)

    def begin(i):
        for step in range(1, depths):
            deep(i, step).start()
        own(i).start()

    def first(i):
        own(i).wait()
        for step in range(1, depths):
            deep(i, step).wait_recv()
        ring(i, 1, 0).start()
        ring(i, 1, 1).start()
        across(i, 0).start()

    def later(i, step):
        ring(i, step, 0).wait_recv()
        ring(i, step, 1).wait_recv()
        if step < half:
            ring(i, step + 1, 0).start()
            ring(i, step + 1, 1).start()
            across(i, 2 * step - 1).start()
            across(i, 2 * step).start()
        else:
            across(i, 2 * step - 1).start()

    place.greet()
    begin(0)
    spread = Spread(place, small, small_full, s_send, s_recv, s_own)
    spread.start()
    for i in range(1, min(LOOK, total)):
        begin(i)
    for tick in range(total + half):
        if tick + LOOK < total:
            begin(tick + LOOK)
        if tick < total:
            first(tick)
        for step in range(1, half + 1):
            if 0 <= tick - step < total:
                later(tick - step, step)
    spread.wait()
    for i in range(total):
        for slot in range(slots):
            across(i, slot).wait()
        for step in range(1, depths):
            deep(i, step).wait_send()
        for step in range(1, half + 1):
            for way in range(2):
                ring(i, step, way).wait_send()


def chunk_list(shapes, layers):
    chunks = []
    for layer in layers:
        for which, (rows, columns) in enumerate(shapes):
            array = layer * len(shapes) + which
            if columns > WIDE:
                for start in range(0, columns, WIDE):
                    chunks.append((which, array, layer, slice(None), slice(start, start + WIDE)))
            else:
                size = rows // 4 if rows % 64 == 0 and rows > 64 else rows
                for start in range(0, rows, size):
                    chunks.append((which, array, layer, slice(start, start + size), slice(None)))
    return chunks


def gather_all(blocks, small, depths, peers):
    shapes = [b.shape[1:] for b in blocks]
    half = peers // 2
    count = 2 * len(blocks)
    plan = [(array, layer, rows, cols) for _, array, layer, rows, cols in chunk_list(shapes, (0, 1))]
    total = len(plan)

    outs = [
        jax.ShapeDtypeStruct((depths, 2, peers) + shape, jnp.bfloat16)
        for _ in range(2)
        for shape in shapes
    ]
    outs.append(jax.ShapeDtypeStruct((depths * 2 * peers,) + small.shape, small.dtype))
    dma = pltpu.SemaphoreType.DMA
    doubled = list(blocks) + list(blocks)
    return pl.pallas_call(
        functools.partial(gather_kernel, plan, depths, peers, count),
        out_shape=outs,
        in_specs=[ANY] * (count + 1),
        out_specs=[ANY] * (count + 1),
        scratch_shapes=[
            dma((total, depths - 1)),
            dma((total, depths - 1)),
            dma((total, half, 2)),
            dma((total, half, 2)),
            dma((total, 2 * half)),
            dma((total, 2 * half)),
            dma((total,)),
            dma(()),
            dma(()),
            dma(()),
        ],
        compiler_params=pltpu.CompilerParams(
            collective_id=0, has_side_effects=True, vmem_limit_bytes=60 * 2**20
        ),
    )(*doubled, small)


def sum_kernel(plan, depths, peers, count, with_small, *refs):
    lefts, rights, rest = refs[:count], refs[count : 2 * count], refs[2 * count :]
    if with_small:
        small, rest = rest[0], rest[1:]
    outs, rest = rest[:count], rest[count:]
    if with_small:
        small_all, rest = rest[0], rest[1:]
    left_bufs, right_bufs, rest = rest[:count], rest[count : 2 * count], rest[2 * count :]
    (half_send, half_recv, full_send, full_recv, z_out, z_in, own_part, x_send, x_recv, x_own) = rest[:10]
    (r_send, r_recv, z_send, z_recv) = rest[10:14]
    if with_small:
        small_in, small_sum, a_send, a_recv, a_own, b_send, b_recv, b_own = rest[14:]
    place = Place(depths, peers)
    half, core = place.half, place.core
    rows = z_out.shape[2]
    tall = depths * rows
    cut = tall // 2

    def swap(k):
        array = k // 2
        if k % 2 == 0:
            mine, theirs = lefts[array].at[core], lefts[array].at[1 - core]
            buf = left_bufs[array]
        else:
            mine = theirs = rights[array]
            buf = right_bufs[array]
        return (
            pltpu.make_async_copy(mine, buf.at[0], x_own.at[k]),
            remote(theirs, buf.at[1], x_send.at[k], x_recv.at[k], place.sibling()),
        )

    def product(i, peer):
        array, row_part, start, _ = plan[i]
        columns = pl.ds(start, WIDE)
        return jnp.dot(
            left_bufs[array][0, row_part, peer],
            right_bufs[array][0, :, columns],
            preferred_element_type=jnp.float32,
        ) + jnp.dot(
            left_bufs[array][1, row_part, peer],
            right_bufs[array][1, :, columns],
            preferred_element_type=jnp.float32,
        )

    def ring(i, step, way):
        if step == 1:
            source, target = half_send.at[i, way], half_recv.at[i, way]
        else:
            source, target = full_send.at[i, step - 2, way], full_recv.at[i, step - 2, way]
        return remote(
            source,
            target,
            r_send.at[i, step - 1, way],
            r_recv.at[i, step - 1, way],
            place.neighbour(1 if way == 0 else -1),
        )

    def deep(i, step):
        return remote(
            z_out.at[i, place.at_depth(step)],
            z_in.at[i, step - 1],
            z_send.at[i, step - 1],
            z_recv.at[i, step - 1],
            place.deep(step),
        )

    def first(i):
        found = product(i, place.around(half)).astype(jnp.bfloat16)
        half_send[i, 0] = found[:cut]
        half_send[i, 1] = found[cut:]
        ring(i, 1, 0).start()
        ring(i, 1, 1).start()

    def next_step(i, step):
        for way in range(2):
            turn = 1 if way == 0 else -1
            found = product(i, place.around(turn * (half - step + 1)))
            ring(i, step - 1, way).wait_recv()
            if step == 2:
                came = half_recv[i, way].astype(jnp.float32)
                low = found[:cut] + came if way == 0 else found[:cut]
                high = found[cut:] if way == 0 else found[cut:] + came
                full_send[i, 0, way, :cut] = low.astype(jnp.bfloat16)
                full_send[i, 0, way, cut:] = high.astype(jnp.bfloat16)
            else:
                came = full_recv[i, step - 3, way].astype(jnp.float32)
                full_send[i, step - 2, way] = (found + came).astype(jnp.bfloat16)
            ring(i, step, way).start()

    def plane(i):
        found = product(i, place.peer)
        for way in range(2):
            ring(i, half, way).wait_recv()
            found += full_recv[i, half - 2, way].astype(jnp.float32)
        for depth in range(depths):
            piece = found[depth * rows : (depth + 1) * rows]
            z_out[i, depth] = piece.astype(jnp.bfloat16)

            @pl.when(depth == place.depth)
            def _():
                own_part[i] = piece

        for step in range(1, depths):
            deep(i, step).start()

    def finish(i):
        array, _, start, out_rows = plan[i]
        found = own_part[i]
        for step in range(1, depths):
            deep(i, step).wait_recv()
            found += z_in[i, step - 1].astype(jnp.float32)
        outs[array][out_rows, pl.ds(start, WIDE)] = found

    if with_small:
        place.greet()
    else:
        place.greet_near()
    for k in reversed(range(2 * count)):
        for copy in swap(k):
            copy.start()
    if with_small:

        def send_small(step, carry):
            outer, peer = place.other(step)
            remote(
                small.at[outer * peers + peer],
                small_in.at[place.index],
                a_send,
                a_recv,
                (outer, peer),
            ).start()
            return carry

        lax.fori_loop(1, place.total, send_small, 0)
        own_small = pltpu.make_async_copy(small.at[place.index], small_in.at[place.index], a_own)
        own_small.start()
        spread = Spread(place, small_sum, small_all, b_send, b_recv, b_own)

    total = len(plan)
    ready = set()
    for tick in range(total + half + 1):
        if tick < total:
            array = plan[tick][0]
            if array not in ready:
                ready.add(array)
                for k in (2 * array + 1, 2 * array):
                    kept, sent = swap(k)
                    kept.wait()
                    sent.wait_recv()
            first(tick)
        for step in range(2, half + 1):
            if 0 <= tick - step + 1 < total:
                next_step(tick - step + 1, step)
        if 0 <= tick - half < total:
            plane(tick - half)
        if 0 <= tick - half - 1 < total:
            finish(tick - half - 1)
        if with_small and tick == 4:
            rest_in = small_in.at[pl.ds(0, place.total - 1)]
            both = remote(rest_in, rest_in, a_send, a_recv, place.other(1))
            both.wait_send()
            both.wait_recv()
            own_small.wait()
            small_sum[...] = jnp.sum(small_in[...], axis=0)
            spread.start()
    if with_small:
        spread.wait()
    for k in range(2 * count):
        swap(k)[1].wait_send()
    for i in range(total):
        for step in range(1, half + 1):
            for way in range(2):
                ring(i, step, way).wait_send()
        for step in range(1, depths):
            deep(i, step).wait_send()


def sum_all(pairs, shapes, depths, peers, call, small=None):
    half, count = peers // 2, len(pairs)
    tokens = pairs[0][0].shape[0]
    padded = -(-tokens // 128) * 128
    unit = min(shape[0] for shape in shapes)
    lefts, rights, plan = [], [], []
    for array, ((left, right), shape) in enumerate(zip(pairs, shapes)):
        parts = shape[0] // unit
        turned = jnp.pad(left, ((0, padded - tokens), (0, 0))).T
        turned = turned.reshape(depths, 2, peers, parts, unit, padded)
        lefts.append(
            turned.transpose(1, 3, 2, 0, 4, 5).reshape(2, parts, peers, depths * unit, padded)
        )
        rights.append(jnp.pad(right, ((0, padded - tokens), (0, 0))))
        for part in range(parts):
            for start in range(0, shape[1], WIDE):
                plan.append((array, part, start, pl.ds(part * unit, unit)))
    plan = plan[::-1]
    total, tall = len(plan), depths * unit
    dma = pltpu.SemaphoreType.DMA
    low = jnp.bfloat16
    scratch = [pltpu.VMEM((2,) + a.shape[1:], low) for a in lefts]
    scratch += [pltpu.VMEM((2,) + a.shape, low) for a in rights]
    scratch += [
        pltpu.VMEM((total, 2, tall // 2, WIDE), low),
        pltpu.VMEM((total, 2, tall // 2, WIDE), low),
        pltpu.VMEM((total, half - 1, 2, tall, WIDE), low),
        pltpu.VMEM((total, half - 1, 2, tall, WIDE), low),
        pltpu.VMEM((total, depths, unit, WIDE), low),
        pltpu.VMEM((total, depths - 1, unit, WIDE), low),
        pltpu.VMEM((total, unit, WIDE), jnp.float32),
        dma((2 * count,)),
        dma((2 * count,)),
        dma((2 * count,)),
        dma((total, half, 2)),
        dma((total, half, 2)),
        dma((total, depths - 1)),
        dma((total, depths - 1)),
    ]
    args = [*lefts, *rights]
    in_specs = [ANY] * (2 * count)
    out_shape = [jax.ShapeDtypeStruct(shape, jnp.float32) for shape in shapes]
    out_specs = [VMEM] * count
    if small is not None:
        args.append(small)
        in_specs.append(ANY)
        out_shape.append(jax.ShapeDtypeStruct(small.shape, jnp.float32))
        out_specs.append(VMEM)
        scratch += [
            pltpu.VMEM(small.shape, jnp.float32),
            pltpu.VMEM(small.shape[1:], jnp.float32),
        ] + [dma(())] * 6
    return pl.pallas_call(
        functools.partial(sum_kernel, plan, depths, peers, count, small is not None),
        out_shape=out_shape,
        in_specs=in_specs,
        out_specs=out_specs,
        scratch_shapes=scratch,
        compiler_params=pltpu.CompilerParams(
            collective_id=call, has_side_effects=True, vmem_limit_bytes=60 * 2**20
        ),
    )(*args)


def attention_scores(qkv_parts, position_bias, mask_add):
    head_scale = qkv_parts.shape[-1] ** (-0.5)
    scores = (
        jnp.einsum(
            "wqhd,wkhd->whqk",
            qkv_parts[:, :, 0],
            qkv_parts[:, :, 1],
            preferred_element_type=jnp.float32,
        )
        * head_scale
        + position_bias[None]
    )
    if mask_add is not None:
        scores = scores + mask_add
    return scores


def block_forward(inputs, weights, position_bias, mask_add, windows):
    norm_gains, norm_shifts, w_qkv, qv_bias, w_proj, b_proj, w_up, b_up, w_down, b_down = weights
    model_width = inputs.shape[1]
    norm_gains = norm_gains.astype(jnp.float32)
    norm_shifts = norm_shifts.astype(jnp.float32)
    normed, normal_one, inverse_one = layer_norm(inputs, norm_gains[0], norm_shifts[0])
    normed_low = normed.astype(jnp.bfloat16)
    qv_float = qv_bias.astype(jnp.float32)
    bias_full = jnp.concatenate(
        [qv_float[:model_width], jnp.zeros((model_width,), jnp.float32), qv_float[model_width:]]
    )
    qkv_low = (jnp.dot(normed_low, w_qkv, preferred_element_type=jnp.float32) + bias_full).astype(
        jnp.bfloat16
    )
    qkv_parts = qkv_low.reshape(windows, WIN, 3, HEADS, -1)
    scores = attention_scores(qkv_parts, position_bias, mask_add)
    row_max = jnp.max(scores, axis=-1, keepdims=True)
    shifted_exp = jnp.exp(scores - row_max)
    row_total = jnp.sum(shifted_exp, axis=-1, keepdims=True)
    soft_low = (shifted_exp / row_total).astype(jnp.bfloat16)
    log_total = row_max + jnp.log(row_total)
    attended = jnp.einsum(
        "whqk,wkhd->wqhd", soft_low, qkv_parts[:, :, 2], preferred_element_type=jnp.float32
    )
    attended_low = attended.reshape(inputs.shape).astype(jnp.bfloat16)
    middle = inputs + (
        jnp.dot(attended_low, w_proj, preferred_element_type=jnp.float32)
        + b_proj.astype(jnp.float32)
    )
    normed_two, normal_two, inverse_two = layer_norm(middle, norm_gains[1], norm_shifts[1])
    normed_two_low = normed_two.astype(jnp.bfloat16)
    hidden = jnp.dot(normed_two_low, w_up, preferred_element_type=jnp.float32) + b_up.astype(
        jnp.float32
    )
    activated_low = gelu_exact(hidden).astype(jnp.bfloat16)
    output = middle + (
        jnp.dot(activated_low, w_down, preferred_element_type=jnp.float32)
        + b_down.astype(jnp.float32)
    )
    kept_state = (
        normal_one,
        inverse_one,
        normed_low,
        qkv_low,
        log_total,
        attended_low,
        normal_two,
        inverse_two,
        normed_two_low,
        hidden,
        activated_low,
    )
    return (output, kept_state)


def block_backward(grad_out, weights, kept_state, position_bias, mask_add, bucket_table, windows):
    norm_gains, norm_shifts, w_qkv, qv_bias, w_proj, b_proj, w_up, b_up, w_down, b_down = weights
    (
        normal_one,
        inverse_one,
        normed_low,
        qkv_low,
        log_total,
        attended_low,
        normal_two,
        inverse_two,
        normed_two_low,
        hidden,
        activated_low,
    ) = kept_state
    model_width = grad_out.shape[1]
    norm_gains = norm_gains.astype(jnp.float32)
    grad_down_low = grad_out.astype(jnp.bfloat16)
    down_bias_grad = jnp.sum(grad_down_low, axis=0, dtype=jnp.float32)
    grad_act = jnp.einsum("rd,fd->rf", grad_down_low, w_down, preferred_element_type=jnp.float32)
    gelu_back = jax.vjp(gelu_exact, hidden)[1]
    grad_hidden_low = gelu_back(grad_act)[0].astype(jnp.bfloat16)
    up_bias_grad = jnp.sum(grad_hidden_low, axis=0, dtype=jnp.float32)
    grad_normed_two = jnp.einsum(
        "rf,df->rd", grad_hidden_low, w_up, preferred_element_type=jnp.float32
    )
    grad_mid_norm, gain_two_grad, shift_two_grad = norm_back(
        grad_normed_two, normal_two, inverse_two, norm_gains[1]
    )
    grad_middle = grad_out + grad_mid_norm
    grad_branch_low = grad_middle.astype(jnp.bfloat16)
    proj_bias_grad = jnp.sum(grad_branch_low, axis=0, dtype=jnp.float32)
    grad_attended_low = jnp.einsum(
        "rd,cd->rc", grad_branch_low, w_proj, preferred_element_type=jnp.float32
    ).astype(jnp.bfloat16)
    qkv_parts = qkv_low.reshape(windows, WIN, 3, HEADS, -1)
    scores = attention_scores(qkv_parts, position_bias, mask_add)
    soft = jnp.exp(scores - log_total)
    soft_low = soft.astype(jnp.bfloat16)
    grad_heads = grad_attended_low.reshape(windows, WIN, HEADS, -1)
    grad_value = jnp.einsum(
        "whqk,wqhd->wkhd", soft_low, grad_heads, preferred_element_type=jnp.float32
    )
    grad_soft = jnp.einsum(
        "wqhd,wkhd->whqk", grad_heads, qkv_parts[:, :, 2], preferred_element_type=jnp.float32
    )
    grad_scores_low = (
        soft * (grad_soft - jnp.sum(soft * grad_soft, axis=-1, keepdims=True))
    ).astype(jnp.bfloat16)
    head_scale = qkv_parts.shape[-1] ** (-0.5)
    grad_query = (
        jnp.einsum(
            "whqk,wkhd->wqhd",
            grad_scores_low,
            qkv_parts[:, :, 1],
            preferred_element_type=jnp.float32,
        )
        * head_scale
    )
    grad_key = (
        jnp.einsum(
            "whqk,wqhd->wkhd",
            grad_scores_low,
            qkv_parts[:, :, 0],
            preferred_element_type=jnp.float32,
        )
        * head_scale
    )
    score_sum = jnp.sum(grad_scores_low, axis=0, dtype=jnp.float32).reshape(HEADS, -1)
    table_grad = jnp.einsum("hn,nb->bh", score_sum, bucket_table, precision=lax.Precision.HIGHEST)
    grad_qkv_low = (
        jnp.stack([grad_query, grad_key, grad_value], axis=2)
        .reshape(qkv_low.shape)
        .astype(jnp.bfloat16)
    )
    column_sums = jnp.sum(grad_qkv_low, axis=0, dtype=jnp.float32)
    qv_grad = jnp.concatenate([column_sums[:model_width], column_sums[2 * model_width :]])
    grad_normed = jnp.einsum("re,de->rd", grad_qkv_low, w_qkv, preferred_element_type=jnp.float32)
    grad_in_norm, gain_one_grad, shift_one_grad = norm_back(
        grad_normed, normal_one, inverse_one, norm_gains[0]
    )
    grad_input = grad_middle + grad_in_norm
    grads = (
        jnp.stack([gain_one_grad, gain_two_grad]),
        jnp.stack([shift_one_grad, shift_two_grad]),
        qv_grad,
        proj_bias_grad,
        up_bias_grad,
        down_bias_grad,
    )
    pairs = (
        (normed_low, grad_qkv_low),
        (attended_low, grad_branch_low),
        (normed_two_low, grad_hidden_low),
        (activated_low, grad_down_low),
    )
    return (grad_input, grads, table_grad, pairs)


def shards(
    outer_count,
    peer_count,
    patches,
    out_grad,
    norm_gain,
    norm_shift,
    qkv_weight,
    qv_bias,
    rel_table,
    proj_weight,
    proj_bias,
    up_weight,
    up_bias,
    down_weight,
    down_bias,
    tile_perm,
    window_slot,
    mask_ids,
    bias_index,
):
    windows = patches.shape[0] // WIN
    model_width = patches.shape[1]
    depths = outer_count // 2
    devices = outer_count * peer_count
    capacity = (windows + peer_count - 1) // peer_count
    device_index = lax.axis_index(("dp", "fsdp"))
    total_windows = tile_perm.shape[0]
    slot_ids = jnp.arange(total_windows, dtype=jnp.int32)

    def one_hot_pick(keys, values):
        return jnp.sum(jnp.where(keys[None, :] == slot_ids[:, None], values[None, :], 0), axis=1)

    def look_up(values, at):
        hit = at[:, None] == jnp.arange(values.shape[0], dtype=jnp.int32)[None, :]
        return jnp.sum(jnp.where(hit, values[None, :], 0), axis=1)

    source_of = one_hot_pick(window_slot, look_up(window_slot, tile_perm))
    target_of = one_hot_pick(source_of, slot_ids)
    region_slot = one_hot_pick(window_slot, mask_ids)
    own_slots = device_index * windows + jnp.arange(windows, dtype=jnp.int32)

    def rank_of(slots, device_of):
        grid_view = device_of.reshape(-1, windows)
        earlier = jnp.arange(windows)[None, :] < jnp.arange(windows)[:, None]
        same_peer = grid_view[:, :, None] == grid_view[:, None, :]
        ranks = jnp.sum(same_peer & earlier[None], axis=2).reshape(-1)
        return look_up(ranks, slots)

    def peer_of(slots):
        return slots // windows % peer_count

    own_source = look_up(source_of, own_slots)
    own_target = look_up(target_of, own_slots)
    forward_send = peer_of(own_target) * capacity + rank_of(own_slots, target_of // windows)
    forward_take = peer_of(own_source) * capacity + rank_of(own_source, target_of // windows)
    backward_send = peer_of(own_source) * capacity + rank_of(own_slots, source_of // windows)
    backward_take = peer_of(own_target) * capacity + rank_of(own_target, source_of // windows)
    mask_add = region_mask(look_up(region_slot, own_slots))
    bucket_table = (
        bias_index.reshape(-1)[:, None] == jnp.arange(rel_table.shape[1], dtype=jnp.int32)[None, :]
    ).astype(jnp.float32)
    tables = rel_table.astype(jnp.float32)
    bias_one = jnp.einsum(
        "nb,bh->hn", bucket_table, tables[0], precision=lax.Precision.HIGHEST
    ).reshape(HEADS, WIN, WIN)
    bias_two = jnp.einsum(
        "nb,bh->hn", bucket_table, tables[1], precision=lax.Precision.HIGHEST
    ).reshape(HEADS, WIN, WIN)

    def choose(rows, at, count):
        spots = jnp.arange(count, dtype=jnp.int32)
        hit = spots[:, None] == at[None, :]
        return sum(
            jnp.where(hit[:, w][:, None, None], rows[w][None], jnp.zeros((), rows.dtype))
            for w in range(rows.shape[0])
        )

    def take(rows, at):
        hit = at[:, None] == jnp.arange(rows.shape[0], dtype=jnp.int32)[None, :]
        return sum(
            jnp.where(hit[:, w][:, None, None], rows[w][None], jnp.zeros((), rows.dtype))
            for w in range(rows.shape[0])
        )

    def move(rows_low, send, fetch):
        parts = rows_low.reshape(windows, WIN, model_width)
        sectioning = choose(parts, send, peer_count * capacity)
        arrived = lax.all_to_all(sectioning, "fsdp", split_axis=0, concat_axis=0, tiled=True)
        return take(arrived, fetch).reshape(rows_low.shape)

    def to_shifted(rows_low):
        return move(rows_low, forward_send, forward_take)

    def from_shifted(rows_low):
        return move(rows_low, backward_send, backward_take)

    vectors = (norm_gain, norm_shift, qv_bias, proj_bias, up_bias, down_bias)
    flat = jnp.concatenate([v.reshape(-1) for v in vectors])
    small = jnp.pad(flat, (0, -flat.shape[0] % 2048)).reshape(-1, 128)
    matrices = (qkv_weight, proj_weight, up_weight, down_weight)
    *fulls, small_full = gather_all(matrices, small, depths, peer_count)
    small_full = small_full.reshape(devices, -1)
    whole, offset = [], 0
    for v in vectors:
        size = v.size
        piece = small_full[:, offset : offset + size].reshape((devices,) + v.shape)
        offset += size
        piece = jnp.moveaxis(piece, 0, -2)
        whole.append(piece.reshape(v.shape[:-1] + (-1,)))

    def weights_of(layer):
        gains, shifts, qv, proj_b, up_b, down_b = [v[layer] for v in whole]
        w_qkv, w_proj, w_up, w_down = [
            fulls[4 * layer + k].reshape(-1, matrices[k].shape[-1]) for k in range(4)
        ]
        return (gains, shifts, w_qkv, qv, w_proj, proj_b, w_up, up_b, w_down, down_b)

    first_weights, second_weights = weights_of(0), weights_of(1)
    grad_two = to_shifted(out_grad)
    output_one, state_one = block_forward(
        patches.astype(jnp.float32), first_weights, bias_one, None, windows
    )
    second_input = to_shifted(output_one.astype(jnp.bfloat16))
    output_two, state_two = block_forward(
        second_input.astype(jnp.float32), second_weights, bias_two, mask_add, windows
    )
    block_out = from_shifted(output_two.astype(jnp.bfloat16))
    shapes = [m.shape[1:] for m in matrices]
    grad_input_two, grads_two, table_two, pairs_two = block_backward(
        grad_two.astype(jnp.float32), second_weights, state_two, bias_two, mask_add, bucket_table, windows
    )
    sums_two = sum_all(pairs_two, shapes, depths, peer_count, 1)
    grad_one = from_shifted(grad_input_two.astype(jnp.bfloat16))
    grad_patches, grads_one, table_one, pairs_one = block_backward(
        grad_one.astype(jnp.float32), first_weights, state_one, bias_one, None, bucket_table, windows
    )
    small_grads = []
    for one, two, v in zip(grads_one, grads_two, vectors):
        both = jnp.stack([one, two]).reshape(v.shape[:-1] + (devices, v.shape[-1]))
        small_grads.append(jnp.moveaxis(both, -2, 0).reshape(devices, -1))
    table = jnp.stack([table_one, table_two]).reshape(-1)
    table = jnp.pad(table, (0, -table.shape[0] % devices)).reshape(devices, -1)
    packed = jnp.concatenate(small_grads + [table], axis=1)
    width = packed.shape[1]
    packed = jnp.pad(packed, ((0, 0), (0, -width % 1024))).reshape(devices, -1, 128)
    *sums_one, small_all = sum_all(pairs_one, shapes, depths, peer_count, 2, packed)
    small_all = small_all.reshape(devices, -1)
    mine = lax.dynamic_index_in_dim(small_all, device_index, 0, keepdims=False)
    vector_grads, offset = [], 0
    for v in vectors:
        vector_grads.append(mine[offset : offset + v.size].reshape(v.shape))
        offset += v.size
    table_total = small_all[:, offset:width].reshape(-1)[: rel_table.size].reshape(rel_table.shape)
    grad_qkv, grad_proj, grad_up, grad_down = [
        jnp.stack([one, two]) for one, two in zip(sums_one, sums_two)
    ]
    return (
        block_out,
        grad_patches,
        vector_grads[0],
        vector_grads[1],
        grad_qkv,
        vector_grads[2],
        table_total,
        grad_proj,
        vector_grads[3],
        grad_up,
        vector_grads[4],
        grad_down,
        vector_grads[5],
    )


def solution(mesh):
    placed = (
        P(("dp", "fsdp"), None),
        P(("dp", "fsdp"), None),
        P(None, None, ("dp", "fsdp")),
        P(None, None, ("dp", "fsdp")),
        P(None, ("dp", "fsdp"), None),
        P(None, ("dp", "fsdp")),
        P(),
        P(None, ("dp", "fsdp"), None),
        P(None, ("dp", "fsdp")),
        P(None, ("dp", "fsdp"), None),
        P(None, ("dp", "fsdp")),
        P(None, ("dp", "fsdp"), None),
        P(None, ("dp", "fsdp")),
        P(),
        P(),
        P(),
        P(),
    )
    return jax.shard_map(
        functools.partial(shards, mesh.shape["dp"], mesh.shape["fsdp"]),
        mesh=mesh,
        in_specs=placed,
        out_specs=(
            P(("dp", "fsdp"), None),
            P(("dp", "fsdp"), None),
            P(None, None, ("dp", "fsdp")),
            P(None, None, ("dp", "fsdp")),
            P(None, ("dp", "fsdp"), None),
            P(None, ("dp", "fsdp")),
            P(),
            P(None, ("dp", "fsdp"), None),
            P(None, ("dp", "fsdp")),
            P(None, ("dp", "fsdp"), None),
            P(None, ("dp", "fsdp")),
            P(None, ("dp", "fsdp"), None),
            P(None, ("dp", "fsdp")),
        ),
        check_vma=False,
    )
```

time: 3570 us -> 897 us (0.25)
  waiting for transfers between devices: 2650 us -> 10.5 us
  Pallas kernels: 0 us -> 476 us
  blocking collectives: 456 us -> 0 us
  matrix products: 201 us -> 135 us
    reduce_scatter x8 -> x0, waiting for transfers between devices: 2040 us -> none  [the longest x2 720 us: reduce_grads(): lax.psum_scatter(grads[8], ('dp', 'fsdp'), scatter_dimension=0, tiled=True)]
    unnamed x27 -> x0, waiting for transfers between devices: 482 us -> none
    pallas_call x0 -> x3, Pallas kernels: none -> 476 us  [the longest x2 245 us: sum_all(): pl.pallas_call(functools.partial(sum_kernel, plan, depths, peers, count,...]
    all_gather x6 -> x0, blocking collectives: 409 us -> none  [the longest x2 142 us: fetch_forward(): lax.all_gather(norm_shift[layer_index], ('dp', 'fsdp'), axis=1, tiled=True)]
    psum x1 -> x0, waiting for transfers between devices: 126 us -> none  [shards(): table_total = lax.psum(jnp.stack([table_one, table_two]), ('dp', 'fsdp'))]
    dot_general x8 -> x0, matrix products: 58.4 us -> none  [the longest x2 19.5 us: block_backward(): jnp.einsum('rd,rf->df', normed_two_low, grad_hidden_low, preferred_elemen...]
    broadcast_in_dim x0 -> x58, local copies, waits for them, and re-layouts: none -> 49 us  [the longest x54 47.6 us: take(): jnp.where(hit[:, w][:, None, None], rows[w][None], jnp.zeros((), rows.dty...]
    unnamed x1 -> x0, blocking collectives: 46.7 us -> none
  transfers between devices with their start and end apart: 26 -> 4, of which waited for: 14 -> 1; matrix products, arithmetic and copies ran while one was open for 10% -> 14% of each run, Pallas kernels for 0% -> 13%
where the time goes in v1:
time: 897 us; the launch traced here: 885 us
  Pallas kernels  476 us (53%)
  local copies, waits for them, and re-layouts  181 us (20%)
  matrix products  135 us (15%)
  other arithmetic  54.2 us (6%)
  starting transfers between devices  24.8 us (3%)
  waiting for transfers between devices  10.5 us (1%)
    pallas_call x2, Pallas kernels, sum_all(): pl.pallas_call(functools.partial(sum_kernel, plan, depths, peers, count,...  245 us
    pallas_call x1, Pallas kernels, gather_all(): pl.pallas_call(functools.partial(gather_kernel, plan, depths, peers, coun...  232 us
    broadcast_in_dim x54, local copies, waits for them, and re-layouts, take(): jnp.where(hit[:, w][:, None, None], rows[w][None], jnp.zeros((), rows.dty...  47.6 us
    dot_general x2, matrix products, block_backward(): jnp.einsum('rd,fd->rf', grad_down_low, w_down, preferred_element_type=jnp...  25.2 us
    all_to_all x4, starting transfers between devices, move(): lax.all_to_all(sectioning, 'fsdp', split_axis=0, concat_axis=0, tiled=True)  24.8 us
    dot_general x2, matrix products, block_forward(): jnp.dot(normed_two_low, w_up, preferred_element_type=jnp.float32)  18.1 us
  transfers between devices with their start and end apart: 4, of which 1 were waited for; matrix products, arithmetic and copies ran while one was open for 14% of the time, Pallas kernels for 13%

profile of v1, /device:TPU:0, one launch (start us, length us, event | category | flops | bytes accessed | tf_op | source)
XLA Modules:
  0.0 884.5 jit_solution(1995239709316230011)
XLA Ops:
  7.7 231.8 %shard_map.264 = (bf16[4,2,4,32,3072]{4,3,2,1,0:T(8,128)(2,1)}, bf16[4,2,4,32,1024]{4,3,2,1,0:T(8,128)(2,1)}, bf16[4,2,4,32,4096]{4,3,2,1,0:T(8,128)(2,1)}, bf16...) custom-call(bf16[2,32,3072]{2,1,0:T(8,128)(2,1)} %refs_4_.1, ...), custom_call_target="tpu_custom_call" | custom-call | tf_op jit(solution)/shard_map/pallas_call | solution.py:295
  246.7 3.5 fusion.4
  258.5 4.2 fusion.10
  264.3 4.0 reshape.1537
  280.3 12.6 %multiply_convert_fusion.3 = (bf16[200,4096]{1,0:T(8,128)(2,1)S(1)}, f32[200,4096]{1,0:T(8,128)}, f32[200,4096]{1,0:T(8,128)}) fusion(f32[4096]{0:T(1024)} %bitcast.345, bf16[200,1024]{1,0:T(8,128)(2,1)S(1)} %add_convert_fusion.3, bf16[1024,4096]{1,0:T(8,128)(2,1)} %bitcast.348), kind=kOutput, calls=%fused_computation.52 | convolution fusion | flops 1731788800 | bytes 17006592 | tf_op jit(solution)/shard_map/dot_general | solution.py:607
  293.1 5.9 fusion.53
  300.6 3.6 all-to-all-start.2
  304.2 6.7 fusion.5
  316.2 3.1 add.619
  343.3 3.2 copy.192
  347.3 12.6 %all-to-all-start = ((bf16[4,100,1024]{2,1,0:T(8,128)(2,1)}), bf16[4,100,1024]{2,1,0:T(8,128)(2,1)S(1)}, u32[]{:S(2)}, u32[]{:S(2)}) async-start(bf16[4,100,1024]{2,1,0:T(8,128)(2,1)} %get-tuple-element.225), calls=%async_computation | async-start | bytes 1703936 | tf_op jit(solution)/shard_map/all_to_all | solution.py:818
  361.2 10.5 %all-to-all-done = bf16[4,100,1024]{2,1,0:T(8,128)(2,1)S(1)} async-done(((bf16[4,100,1024]{2,1,0:T(8,128)(2,1)}), bf16[4,100,1024]{2,1,0:T(8,128)(2,1)S(1)}, u32[]{:S(2)}, u32[]{:S(2)}) %all-to-all-start) | async-done | bytes 819232 | tf_op jit(solution)/shard_map/all_to_all | solution.py:818
  375.5 5.3 fusion.11
  414.6 5.4 convolution_add_fusion
  420.1 15.6 %convert_reduce_fusion.2 = (f32[4096]{0:T(1024)}, bf16[200,4096]{1,0:T(8,128)(2,1)S(1)}, f32[200,4096]{1,0:T(8,128)}) fusion(f32[200,4096]{1,0:T(8,128)S(1)} %convolution_add_fusion, bf16[200,1024]{1,0:T(8,128)(2,1)S(1)} %copy-done.80, bf16[4096,1024]{1,0:T(8,128)(2,1)} %bitcast.352), kind=kOutput, calls=%fused_computation.35 | convolution fusion | flops 1738338304 | bytes 17006592 | tf_op jit(solution)/shard_map/rd,fd->rf/dot_general | solution.py:650
  435.7 4.4 multiply_reduce_fusion.2
  453.6 4.3 convert_reduce_fusion.10
  478.2 6.6 fusion.88
  487.2 3.1 pad.75.refs_6_
  492.6 5.9 fusion.52
  500.2 4.2 all-to-all-start.3
  519.9 3.3 copy.203
  525.3 117.7 %shard_map.266 = (f32[32,3072]{1,0:T(8,128)}, f32[32,1024]{1,0:T(8,128)}, f32[32,4096]{1,0:T(8,128)}, f32[128,1024]{1,0:T(8,128)}) custom-call(bf16[2,1,4,128,256]{4,3,2,1,0:T(8,128)(2,1)} %bitcast.307, bf16[2,1,4,128,256]{4,3,2,1,0:T(8,128)(2,1)} %bitcast.308, bf16[2,1,4,128,256]{4,3,2,1,0:T(8,128)(2,1)} %bitcast.309, ...), custom_call_target="tpu_custom_call" | custom-call | tf_op jit(solution)/shard_map/pallas_call | solution.py:547
  643.1 5.9 fusion.57
  649.1 4.4 all-to-all-start.1
  655.9 9.6 %convert_reduce_fusion.3 = (f32[4096]{0:T(1024)}, bf16[200,4096]{1,0:T(8,128)(2,1)S(1)}) fusion(f32[200,4096]{1,0:T(8,128)} %get-tuple-element.168, f32[200,4096]{1,0:T(8,128)} %get-tuple-element.244, bf16[200,1024]{1,0:T(8,128)(2,1)S(1)} %add.661, bf16[4096,1024]{1,0:T(8,128)(2,1)} %bitcast.351), kind=kOutput, calls=%fused_computation.36 | convolution fusion | flops 1690824704 | bytes 17006592 | tf_op jit(solution)/shard_map/rd,fd->rf/dot_general | solution.py:650
  665.5 8.4 multiply_reduce_fusion.3
  674.6 3.4 convert_reduce_fusion.11
  678.8 3.6 convolution_convert_fusion
  702.5 6.6 fusion.76
  735.1 5.3 fusion.56
  741.7 127.0 %shard_map.265 = (f32[32,3072]{1,0:T(8,128)}, f32[32,1024]{1,0:T(8,128)}, f32[32,4096]{1,0:T(8,128)}, f32[128,1024]{1,0:T(8,128)}, f32[32,16,128]{2,1,0:T(8,128)}) custom-call(bf16[2,1,4,128,256]{4,3,2,1,0:T(8,128)(2,1)} %bitcast.304, bf16[2,1,4,128,256]{4,3,2,1,0:T(8,128)(2,1)} %bitcast.305, bf16[2,1,4,128,256]{4,3,2,1,0:T(8,128)(2,1)} %bitcast.306, ...), custom_call_target="tpu_custom_call" | custom-call | tf_op jit(solution)/shard_map/pallas_call | solution.py:547
  (640 shorter events, 229.7 us)
Async XLA Ops:
  0.6 241.7 %copy-start.97 = (s32[100,100]{1,0:T(8,128)S(1)}, s32[100,100]{1,0:T(8,128)}, u32[]{:S(2)}) copy-start(s32[100,100]{1,0:T(8,128)} %param.33) | copy-start | bytes 120004
  0.7 243.8 %copy-start.78 = (bf16[200,1024]{1,0:T(8,128)(2,1)S(1)}, bf16[200,1024]{1,0:T(8,128)(2,1)}, u32[]{:S(2)}) copy-start(bf16[200,1024]{1,0:T(8,128)(2,1)} %param.18) | copy-start | bytes 1228804
  0.7 246.0 %copy-start.162 = (bf16[2,361,32]{1,2,0:T(8,128)(2,1)S(1)}, bf16[2,361,32]{1,2,0:T(8,128)(2,1)}, u32[]{:S(2)}) copy-start(bf16[2,361,32]{1,2,0:T(8,128)(2,1)} %param.23) | copy-start | bytes 138628
  277.3 15.7 %copy-start.107 = (f32[1024]{0:T(1024)}, f32[1024]{0:T(1024)S(1)}, u32[]{:S(2)}) copy-start(f32[1024]{0:T(1024)S(1)} %mul.381) | copy-start | bytes 12292
  300.6 46.7 %all-to-all-start.2 = ((bf16[4,100,1024]{2,1,0:T(8,128)(2,1)}), bf16[4,100,1024]{2,1,0:T(8,128)(2,1)S(1)}, u32[]{:S(2)}, u32[]{:S(2)}) async-start(bf16[4,100,1024]{2,1,0:T(8,128)(2,1)} %get-tuple-element.224), calls=%async_computation.2 | async-start | bytes 1703936 | tf_op jit(solution)/shard_map/all_to_all | solution.py:818
  315.4 17.8 %copy-start.129 = (pred[2]{0:T(512)(128)(4,1)}, pred[2]{0:T(512)(128)(4,1)S(1)}, u32[]{:S(2)}) copy-start(pred[2]{0:T(512)(128)(4,1)S(1)} %get-tuple-element.226) | copy-start | bytes 10
  319.3 18.6 %copy-start.20 = (bf16[200,1024]{0,1:T(8,128)(2,1)S(1)}, bf16[200,1024]{0,1:T(8,128)(2,1)}, u32[]{:S(2)}) copy-start(bf16[200,1024]{0,1:T(8,128)(2,1)} %convert_element_type.333) | copy-start | bytes 1228804
  322.9 52.2 %copy-start.105 = (f32[1024]{0:T(1024)}, f32[1024]{0:T(1024)S(1)}, u32[]{:S(2)}) copy-start(f32[1024]{0:T(1024)S(1)} %add.614) | copy-start | bytes 12292
  322.9 82.6 %copy-start.89 = (f32[1024]{0:T(1024)}, f32[1024]{0:T(1024)S(1)}, u32[]{:S(2)}) copy-start(f32[1024]{0:T(1024)S(1)} %mul.390) | copy-start | bytes 12292
  343.3 16.5 %copy-start.138 = (pred[4,2]{0,1:T(4,128)(4,1)S(1)}, pred[4,2]{0,1:T(4,128)(4,1)}, u32[]{:S(2)}) copy-start(pred[4,2]{0,1:T(4,128)(4,1)} %iota_compare_fusion.19) | copy-start | bytes 28
  346.5 26.0 %copy-start.139 = (pred[2]{0:T(512)(128)(4,1)S(1)}, pred[2]{0:T(512)(128)(4,1)}, u32[]{:S(2)}) copy-start(pred[2]{0:T(512)(128)(4,1)} %get-tuple-element.230) | copy-start | bytes 10
  346.5 26.0 %copy-start.140 = (pred[2]{0:T(512)(128)(4,1)S(1)}, pred[2]{0:T(512)(128)(4,1)}, u32[]{:S(2)}) copy-start(pred[2]{0:T(512)(128)(4,1)} %get-tuple-element.231) | copy-start | bytes 10
  346.5 26.0 %copy-start.141 = (pred[2]{0:T(512)(128)(4,1)S(1)}, pred[2]{0:T(512)(128)(4,1)}, u32[]{:S(2)}) copy-start(pred[2]{0:T(512)(128)(4,1)} %get-tuple-element.232) | copy-start | bytes 10
  346.5 26.0 %copy-start.142 = (pred[2]{0:T(512)(128)(4,1)S(1)}, pred[2]{0:T(512)(128)(4,1)}, u32[]{:S(2)}) copy-start(pred[2]{0:T(512)(128)(4,1)} %get-tuple-element.233) | copy-start | bytes 10
  347.3 24.4 %all-to-all-start = ((bf16[4,100,1024]{2,1,0:T(8,128)(2,1)}), bf16[4,100,1024]{2,1,0:T(8,128)(2,1)S(1)}, u32[]{:S(2)}, u32[]{:S(2)}) async-start(bf16[4,100,1024]{2,1,0:T(8,128)(2,1)} %get-tuple-element.225), calls=%async_computation | async-start | bytes 1703936 | tf_op jit(solution)/shard_map/all_to_all | solution.py:818
  361.2 19.6 %copy-start.49 = (bf16[100,1024]{1,0:T(8,128)(2,1)}, bf16[100,1024]{1,0:T(8,128)(2,1)S(1)}, u32[]{:S(2)}) copy-start(bf16[100,1024]{1,0:T(8,128)(2,1)S(1)} %get-tuple-element.185) | copy-start | bytes 614404
  361.2 19.6 %copy-start.50 = (bf16[100,1024]{1,0:T(8,128)(2,1)}, bf16[100,1024]{1,0:T(8,128)(2,1)S(1)}, u32[]{:S(2)}) copy-start(bf16[100,1024]{1,0:T(8,128)(2,1)S(1)} %get-tuple-element.188) | copy-start | bytes 614404
  361.2 19.6 %copy-start.51 = (bf16[100,1024]{1,0:T(8,128)(2,1)}, bf16[100,1024]{1,0:T(8,128)(2,1)S(1)}, u32[]{:S(2)}) copy-start(bf16[100,1024]{1,0:T(8,128)(2,1)S(1)} %get-tuple-element.187) | copy-start | bytes 614404
  374.7 30.9 %copy-start.116 = (f32[200]{0:T(256)}, f32[200]{0:T(256)S(1)}, u32[]{:S(2)}) copy-start(f32[200]{0:T(256)S(1)} %div.161) | copy-start | bytes 2404
  375.0 30.5 %copy-start.118 = (f32[200]{0:T(256)}, f32[200]{0:T(256)S(1)}, u32[]{:S(2)}) copy-start(f32[200]{0:T(256)S(1)} %rsqrt.40) | copy-start | bytes 2404
  389.1 16.5 %copy-start.106 = (f32[1024]{0:T(1024)S(1)}, f32[1024]{0:T(1024)}, u32[]{:S(2)}) copy-start(f32[1024]{0:T(1024)} %copy-done.105) | copy-start | bytes 12292
  389.1 16.5 %copy-start.151 = (pred[200]{0:T(512)(128)(4,1)S(1)}, pred[200]{0:T(512)(128)(4,1)}, u32[]{:S(2)}) copy-start(pred[200]{0:T(512)(128)(4,1)} %broadcast_in_dim.619) | copy-start | bytes 604
  389.1 16.5 %copy-start.152 = (pred[200]{0:T(512)(128)(4,1)S(1)}, pred[200]{0:T(512)(128)(4,1)}, u32[]{:S(2)}) copy-start(pred[200]{0:T(512)(128)(4,1)} %broadcast_in_dim.612) | copy-start | bytes 604
  389.1 16.5 %copy-start.153 = (pred[200]{0:T(512)(128)(4,1)S(1)}, pred[200]{0:T(512)(128)(4,1)}, u32[]{:S(2)}) copy-start(pred[200]{0:T(512)(128)(4,1)} %broadcast_in_dim.605) | copy-start | bytes 604
  389.1 16.5 %copy-start.154 = (pred[200]{0:T(512)(128)(4,1)S(1)}, pred[200]{0:T(512)(128)(4,1)}, u32[]{:S(2)}) copy-start(pred[200]{0:T(512)(128)(4,1)} %broadcast_in_dim.590) | copy-start | bytes 604
  414.6 21.1 %slice-start = ((s8[8388608]{0:T(1024)(128)(4,1)}), s8[4194304]{0:T(1024)(128)(4,1)S(1)}, s32[]{:S(2)}) async-start(s8[8388608]{0:T(1024)(128)(4,1)} %bitcast.293), calls=%async_computation.4 | async-start | bytes 8388608
  420.1 15.6 %copy-start.7 = (f32[200,4096]{1,0:T(8,128)}, f32[200,4096]{1,0:T(8,128)S(1)}, u32[]{:S(2)}) copy-start(f32[200,4096]{1,0:T(8,128)S(1)} %convolution_add_fusion) | copy-start | bytes 9830404
  500.2 148.9 %all-to-all-start.3 = ((bf16[4,100,1024]{2,1,0:T(8,128)(2,1)}), bf16[4,100,1024]{2,1,0:T(8,128)(2,1)}, u32[]{:S(2)}, u32[]{:S(2)}) async-start(bf16[4,100,1024]{2,1,0:T(8,128)(2,1)} %get-tuple-element.222), calls=%async_computation.3 | async-start | bytes 1703936 | tf_op jit(solution)/shard_map/all_to_all | solution.py:818
  525.3 117.7 %copy-start.70 = (f32[32,10000]{1,0:T(8,128)S(1)}, f32[32,10000]{1,0:T(8,128)}, u32[]{:S(2)}) copy-start(f32[32,10000]{1,0:T(8,128)} %reshape.1566) | copy-start | bytes 3840004
  525.3 117.7 %copy-start.101 = (s32[10000]{0:T(1024)S(1)}, s32[10000]{0:T(1024)}, u32[]{:S(2)}) copy-start(s32[10000]{0:T(1024)} %copy-done.99) | copy-start | bytes 120004
  649.1 60.0 %all-to-all-start.1 = ((bf16[4,100,1024]{2,1,0:T(8,128)(2,1)}), bf16[4,100,1024]{2,1,0:T(8,128)(2,1)}, u32[]{:S(2)}, u32[]{:S(2)}) async-start(bf16[4,100,1024]{2,1,0:T(8,128)(2,1)} %get-tuple-element.223), calls=%async_computation.1 | async-start | bytes 1703936 | tf_op jit(solution)/shard_map/all_to_all | solution.py:818
  713.1 17.9 %copy-start.14 = (f32[32,100,100]{1,2,0:T(8,128)S(1)}, f32[32,100,100]{1,2,0:T(8,128)}, u32[]{:S(2)}) copy-start(f32[32,100,100]{1,2,0:T(8,128)} %get-tuple-element.138) | copy-start | bytes 3840004
  (138 other events, 769.6 us)

commit v2 on v1

--- a/solution.py
+++ b/solution.py
@@ -1,4 +1,5 @@
 import functools
+import types
 
 import jax
 import jax.numpy as jnp
@@ -901,7 +902,1369 @@
     )
 
 
+ROWS = 112
+GAP = 2
+AHEAD = 4
+F_BUDGET, B_BUDGET = 5.0, 5.0
+KEYS = 128
+GROUP = 4
+SCALE = 32**-0.5
+LOW = jnp.bfloat16
+WHOLE = jnp.float32
+NEVER = -1e30
+
+
+def names(words, refs):
+    return types.SimpleNamespace(**dict(zip(words, refs, strict=True)))
+
+
+class Queue:
+    def __init__(self, budget):
+        self.pieces, self.budget = [], budget
+
+    def add(self, tick, cost, work, *arguments):
+        self.pieces.append((tick, cost, work, arguments))
+
+    def run(self, tick, after, all_of_it=False):
+        left = self.budget
+        while self.pieces and self.pieces[0][0] <= tick and (left > 0 or all_of_it):
+            left -= self.step(after)
+
+    def step(self, after):
+        _, cost, work, arguments = self.pieces.pop(0)
+        work(*arguments)
+        after()
+        return cost
+
+
+def row_loop(count, size, body):
+    def step(i, carry):
+        body(pl.multiple_of(i * size, size))
+        return carry
+
+    lax.fori_loop(0, count // size, step, 0)
+
+
+def lane_mask(rows, head):
+    lane = lax.broadcasted_iota(jnp.int32, (rows, 128), 1)
+    return lane // 32 == head
+
+
+def per_head(value):
+    tall = jnp.concatenate([value, jnp.zeros((KEYS - ROWS, 128), value.dtype)], axis=0)
+    zero = jnp.zeros((), value.dtype)
+    return jnp.concatenate(
+        [jnp.where(lane_mask(KEYS, head), tall, zero) for head in range(GROUP)], axis=0
+    )
+
+
+def dot(a, b, over=(1, 0)):
+    return lax.dot_general(
+        a, b, (((over[0],), (over[1],)), ((), ())), preferred_element_type=jnp.float32
+    )
+
+
+def normal_parts(block):
+    mean = jnp.mean(block, axis=1, keepdims=True)
+    centered = block - mean
+    inverse = lax.rsqrt(jnp.mean(centered * centered, axis=1, keepdims=True) + epsilon)
+    return centered * inverse, inverse
+
+
+class Exchange:
+    def __init__(self, place, out, into, send, receive, parts):
+        self.place, self.out, self.into = place, out, into
+        self.send, self.receive = send, receive
+        self.width = out.shape[-1] // parts
+
+    def columns(self, part):
+        return slice(part * self.width, (part + 1) * self.width)
+
+    def copy(self, part, step):
+        place = self.place
+        peer = lax.rem(place.peer + step, place.peers)
+        return remote(
+            self.out.at[peer, :, self.columns(part)],
+            self.into.at[place.peer, :, self.columns(part)],
+            self.send.at[part, step - 1],
+            self.receive.at[part, step - 1],
+            (place.depth * 2 + place.core, peer),
+        )
+
+    def give(self, part, tiles, chosen):
+        columns = self.columns(part)
+        for peer in range(self.place.peers):
+            self.out[peer, :, columns] = tiles[chosen[peer], :, columns]
+        self.into[self.place.peer, :, columns] = self.out[self.place.peer, :, columns]
+        for step in range(1, self.place.peers):
+            self.copy(part, step).start()
+
+    def await_part(self, part):
+        for step in range(1, self.place.peers):
+            self.copy(part, step).wait_recv()
+
+    def finish(self, parts):
+        for part in range(parts):
+            for step in range(1, self.place.peers):
+                self.copy(part, step).wait_send()
+
+
+class Gather:
+    def __init__(self, place, chunks, blocks, fulls, sems):
+        self.place, self.chunks, self.blocks, self.fulls = place, chunks, blocks, fulls
+        (self.z_send, self.z_recv, self.r_send, self.r_recv, self.c_send, self.c_recv, self.own_sem) = sems
+        self.half, self.cut = place.half, place.depths // 2
+
+    def view(self, i, depth, peer):
+        array, layer, columns = self.chunks[i]
+        return self.fulls[layer * len(self.blocks) + array].at[
+            depth, self.place.core, peer, :, columns
+        ]
+
+    def block(self, i):
+        array, layer, columns = self.chunks[i]
+        return self.blocks[array].at[layer, :, columns]
+
+    def own(self, i):
+        place = self.place
+        return pltpu.make_async_copy(
+            self.block(i), self.view(i, place.depth, place.peer), self.own_sem.at[i]
+        )
+
+    def deep(self, i, step):
+        place = self.place
+        return remote(
+            self.block(i),
+            self.view(i, place.depth, place.peer),
+            self.z_send.at[i, step - 1],
+            self.z_recv.at[i, step - 1],
+            place.deep(step),
+        )
+
+    def part(self, step, way):
+        if step < self.half:
+            return slice(None)
+        return slice(0, self.cut) if way == 0 else slice(self.cut, self.place.depths)
+
+    def ring(self, i, step, way):
+        turn = 1 if way == 0 else -1
+        here = self.view(i, self.part(step, way), self.place.around(-turn * (step - 1)))
+        return remote(
+            here,
+            here,
+            self.r_send.at[i, step - 1, way],
+            self.r_recv.at[i, step - 1, way],
+            self.place.neighbour(turn),
+        )
+
+    def across(self, i, slot):
+        step = (slot + 1) // 2
+        turn = 1 if slot % 2 else -1
+        here = self.view(i, slice(None), self.place.around(-turn * step))
+        return remote(
+            here, here, self.c_send.at[i, slot], self.c_recv.at[i, slot], self.place.sibling()
+        )
+
+    def begin(self, i):
+        for step in range(1, self.place.depths):
+            self.deep(i, step).start()
+        self.own(i).start()
+
+    def first(self, i):
+        self.own(i).wait()
+        for step in range(1, self.place.depths):
+            self.deep(i, step).wait_recv()
+        self.ring(i, 1, 0).start()
+        self.ring(i, 1, 1).start()
+        self.across(i, 0).start()
+
+    def later(self, i, step):
+        self.ring(i, step, 0).wait_recv()
+        self.ring(i, step, 1).wait_recv()
+        if step < self.half:
+            self.ring(i, step + 1, 0).start()
+            self.ring(i, step + 1, 1).start()
+            self.across(i, 2 * step - 1).start()
+            self.across(i, 2 * step).start()
+        else:
+            self.across(i, 2 * step - 1).start()
+
+    def tick(self, tick):
+        total = len(self.chunks)
+        if tick + AHEAD < total:
+            self.begin(tick + AHEAD)
+        if tick < total:
+            self.first(tick)
+        for step in range(1, self.half + 1):
+            if 0 <= tick - step * GAP < total:
+                self.later(tick - step * GAP, step)
+
+    def await_across(self, i):
+        for slot in range(2 * self.half):
+            self.across(i, slot).wait_recv()
+
+    def finish(self):
+        for i in range(len(self.chunks)):
+            for slot in range(2 * self.half):
+                self.across(i, slot).wait_send()
+            for step in range(1, self.place.depths):
+                self.deep(i, step).wait_send()
+            for step in range(1, self.half + 1):
+                for way in range(2):
+                    self.ring(i, step, way).wait_send()
+
+
+F_IN = (
+    "w0", "w1", "w2", "w3", "small", "x0", "grads", "tables", "index", "mask", "forward_send", "forward_take",
+    "backward_send", "backward_take",
+)
+F_OUT = (
+    "f0", "f1", "f2", "f3", "f4", "f5", "f6", "f7", "moved_grad", "result", "left0", "left1", "left2",
+    "left3", "low_x", "middle", "qkv", "probs", "slope", "vec32",
+)
+F_SCRATCH = (
+    "small_full", "bias", "x", "x0w", "normed", "att", "normed_two", "act", "mid", "q_s", "p_s", "slope_s", "wide_a",
+    "wide_b", "total", "sib_a", "sib_b", "turned", "left_a", "left_b", "g_out", "g_in", "x_out", "x_in",
+    "y_out", "y_in", "vec64", "vec128", "z_send", "z_recv", "r_send", "r_recv", "c_send", "c_recv", "own_sem",
+    "s_send", "s_recv", "s_own", "load", "save", "swap_send", "swap_recv", "eg_send", "eg_recv", "ex_send",
+    "ex_recv", "ey_send", "ey_recv",
+)
+
+
+def forward_kernel(chunks, depths, peers, *refs):
+    r = names(F_IN + F_OUT + F_SCRATCH, refs)
+    place = Place(depths, peers)
+    gather = Gather(
+        place,
+        chunks,
+        (r.w0, r.w1, r.w2, r.w3),
+        (r.f0, r.f1, r.f2, r.f3, r.f4, r.f5, r.f6, r.f7),
+        (r.z_send, r.z_recv, r.r_send, r.r_recv, r.c_send, r.c_recv, r.own_sem),
+    )
+    spread = Spread(place, r.small, r.small_full, r.s_send, r.s_recv, r.s_own)
+    eg = Exchange(place, r.g_out, r.g_in, r.eg_send, r.eg_recv, 1)
+    ex = Exchange(place, r.x_out, r.x_in, r.ex_send, r.ex_recv, 4)
+    ey = Exchange(place, r.y_out, r.y_in, r.ey_send, r.ey_recv, 4)
+    windows = 2
+    tall = windows * ROWS
+    per_layer = len(chunks) // 2
+    total = len(chunks)
+    queue = Queue(F_BUDGET)
+    saved, loaded, used = [], [], set()
+
+    def spill(source, target):
+        copy = pltpu.make_async_copy(source, target, r.save.at[len(saved)])
+        copy.start()
+        saved.append(copy)
+
+    def staged(i):
+        array, layer, columns = chunks[i]
+        count = sum(1 for c in chunks[:i] if (c[0] == 3) == (array == 3))
+        return (r.wide_b if array == 3 else r.wide_a).at[count % 2]
+
+    def load(i):
+        array, layer, columns = chunks[i]
+        source = gather.fulls[layer * 4 + array].at[:, :, :, :, columns]
+        return pltpu.make_async_copy(source, staged(i), r.load.at[i])
+
+    def weight(i):
+        assert i in loaded
+        used.add(i)
+        load(i).wait()
+        value = staged(i)[...]
+        return value.reshape(-1, value.shape[-1])
+
+    def fetch(i):
+        gather.await_across(i)
+        load(i).start()
+
+    def unpack():
+        spread.wait()
+        count = place.total
+        row = lax.broadcasted_iota(jnp.int32, (count, 128), 0)
+        lane = lax.broadcasted_iota(jnp.int32, (count, 128), 1)
+
+        def spread_lanes(line, member, size):
+            each = 128 // size
+            found = jnp.zeros((count, 128), WHOLE)
+            for turn in range(each):
+                spot = (member + turn) % each
+                rolled = line if turn == 0 else pltpu.roll(line, turn * size, 1)
+                found += jnp.where((lane // size == spot) & (row % each == spot), rolled, 0.0)
+            blocks = [
+                jnp.sum(found[each * b : each * (b + 1)], axis=0, keepdims=True)
+                for b in range(count // each)
+            ]
+            return jnp.concatenate(blocks, axis=1)
+
+        for k in range(3):
+            line = r.small_full[:, k, :].astype(WHOLE)
+            for member in range(4):
+                r.vec32[4 * k + member : 4 * k + member + 1, :] = spread_lanes(line, member, 32)
+        line = r.small_full[:, 3, :].astype(WHOLE)
+        for member in range(2):
+            r.vec64[member : member + 1, :] = spread_lanes(line, member, 64)
+        for member in range(2):
+            line = r.small_full[:, 4 + member, :].astype(WHOLE)
+            r.vec128[member : member + 1, :] = jnp.concatenate(
+                [line[d : d + 1] for d in range(count)], axis=1
+            )
+
+    def bias_rows(start, stop):
+        buckets = lax.broadcasted_iota(jnp.int32, (384, KEYS), 0)
+
+        def step(i, carry):
+            rows = pl.ds(pl.multiple_of(i * 8, 8), 8)
+            lines = r.index[rows, :]
+            found = []
+            for row in range(8):
+                hot = jnp.where(buckets == lines[row : row + 1], 1.0, 0.0).astype(LOW)
+                found.append(dot(r.tables[...], hot))
+            for k in range(2 * HEADS):
+                layer, head, g = k // HEADS, k // 8 % GROUP, k % 8
+                block = jnp.concatenate([one[k : k + 1] for one in found], axis=0)
+                r.bias[layer, g, rows, head * KEYS : (head + 1) * KEYS] = block
+            return carry
+
+        lax.fori_loop(start, stop, step, 0)
+
+    def vec(k):
+        return r.vec32[k : k + 1, :]
+
+    def norm(source, target, layer, k):
+        gain, shift = vec(2 * layer + k), vec(4 + 2 * layer + k)
+
+        def body(start):
+            rows = pl.ds(start, 32)
+            parts, _ = normal_parts(source[rows, :].astype(WHOLE))
+            target[rows, :] = (parts * gain + shift).astype(LOW)
+
+        row_loop(tall, 32, body)
+
+    def enter(layer):
+        x = r.x.at[layer]
+        if layer == 0:
+            x[...] = r.x0[...]
+        else:
+            for part in range(4):
+                ex.await_part(part)
+            for w in range(windows):
+                x[w * ROWS : (w + 1) * ROWS, :] = r.x_in[r.forward_take[w]]
+        spill(x, r.low_x.at[layer])
+        norm(x, r.normed.at[layer], layer, 0)
+        swap(layer, 0).start()
+
+    def project(layer, i):
+        part = i % per_layer
+        found = dot(r.normed[layer], weight(i))
+        if part != 1:
+            half = part // 2
+            found = found + r.vec64[layer : layer + 1, half * 1024 : (half + 1) * 1024]
+        r.q_s[layer, :, part * 1024 : (part + 1) * 1024] = found.astype(LOW)
+
+    def attend(layer, w):
+        def step(g, carry):
+            rows = slice(w * ROWS, (w + 1) * ROWS)
+            start = pl.multiple_of(g * 128, 128)
+            q = r.q_s[layer, rows, pl.ds(start, 128)]
+            k = r.q_s[layer, rows, pl.ds(start + 1024, 128)]
+            v = r.q_s[layer, rows, pl.ds(start + 2048, 128)]
+            scores = dot(q, per_head(k), (1, 1)) * SCALE + r.bias[layer, g]
+            heads = []
+            for head in range(GROUP):
+                one = scores[:, head * KEYS : (head + 1) * KEYS]
+                if layer == 1:
+                    one = one + r.mask[w]
+                shifted = jnp.exp(one - jnp.max(one, axis=1, keepdims=True))
+                heads.append(
+                    (shifted * (1.0 / jnp.sum(shifted, axis=1, keepdims=True))).astype(LOW)
+                )
+            found = jnp.concatenate(heads, axis=1)
+            r.p_s[layer, w * 8 + g] = found
+            r.att[layer, rows, pl.ds(start, 128)] = dot(found, per_head(v)).astype(LOW)
+            return carry
+
+        lax.fori_loop(0, 8, step, 0)
+
+    def branch(layer, i):
+        spill(r.q_s.at[layer], r.qkv.at[layer])
+        spill(r.p_s.at[layer], r.probs.at[layer])
+        swap(layer, 1).start()
+        found = dot(r.att[layer], weight(i)) + vec(8 + layer)
+        r.mid[layer] = r.x[layer].astype(WHOLE) + found
+        spill(r.mid.at[layer], r.middle.at[layer])
+
+    def second_norm(layer):
+        norm(r.mid.at[layer], r.normed_two.at[layer], layer, 1)
+        swap(layer, 2).start()
+
+    def widen(layer, i):
+        part = i % per_layer - 4
+        columns = slice(part * 1024, (part + 1) * 1024)
+        r.total[...] = dot(r.normed_two[layer], weight(i)) + r.vec128[layer : layer + 1, columns]
+
+        def body(start):
+            rows = pl.ds(start, 16)
+            v = r.total[rows, :]
+            spread_half = 0.5 * (1.0 + lax.erf(v * (2.0**-0.5)))
+            density = jnp.exp(-0.5 * v * v) * 0.3989422804014327
+            r.act[layer, rows, columns] = (v * spread_half).astype(LOW)
+            r.slope_s[layer, rows, columns] = (spread_half + v * density).astype(LOW)
+
+        row_loop(tall, 16, body)
+        if part == 3:
+            spill(r.slope_s.at[layer], r.slope.at[layer])
+            swap(layer, 3).start()
+
+    def narrow(layer, i):
+        part = i % per_layer - 8
+        columns = slice(part * 256, (part + 1) * 256)
+        found = dot(r.act[layer], weight(i)) + vec(10 + layer)[:, columns]
+        found = (r.mid[layer, :, columns] + found).astype(LOW)
+        for w in range(windows):
+            r.x0w[w, :, columns] = found[w * ROWS : (w + 1) * ROWS]
+        if layer == 0:
+            ex.give(part, r.x0w, r.forward_send)
+        else:
+            ey.give(part, r.x0w, r.backward_send)
+
+    sources = (r.normed, r.att, r.normed_two, r.act)
+
+    def swap(layer, array):
+        target = (r.sib_b if array == 3 else r.sib_a.at[array]).at[layer]
+        return remote(
+            sources[array].at[layer],
+            target,
+            r.swap_send.at[layer, array],
+            r.swap_recv.at[layer, array],
+            place.sibling(),
+        )
+
+    def turn(layer, array):
+        swap(layer, array).wait_recv()
+        mine = sources[array].at[layer]
+        theirs = (r.sib_b if array == 3 else r.sib_a.at[array]).at[layer]
+        unit = r.left0.shape[-2] // depths
+        pad = jnp.zeros((256 - tall, 128), WHOLE)
+        rounds = peers if array == 3 else 1
+        for f in range(rounds):
+            for depth in range(depths):
+                start = (depth * 2 + place.core) * rounds * 128 + f * 128
+                columns = pl.ds(pl.multiple_of(start, 128), 128)
+                for side, ref in enumerate((mine, theirs)):
+                    block = jnp.concatenate([ref[:, columns].astype(WHOLE), pad], axis=0)
+                    r.turned[depth, :, side * 256 : (side + 1) * 256] = block.T
+            for part in range(4):
+                found = jnp.concatenate(
+                    [r.turned[depth, part * unit : (part + 1) * unit] for depth in range(depths)],
+                    axis=0,
+                ).astype(LOW)
+                if array == 3:
+                    r.left_b[layer, part, f] = found
+                else:
+                    r.left_a[layer, array, part] = found
+        if array == 3:
+            spill(r.left_b.at[layer], r.left3.at[layer])
+        else:
+            spill(r.left_a.at[layer, array], (r.left0, r.left1, r.left2)[array].at[layer])
+
+    place.greet()
+    gather.begin(0)
+    spread.start()
+    eg.give(0, r.grads, r.forward_send)
+    for i in range(1, AHEAD):
+        gather.begin(i)
+
+    whole_at = GAP * place.half + 1
+    lag = whole_at + 1
+    queue.add(0, 5, bias_rows, 0, 7)
+    queue.add(0, 5, bias_rows, 7, ROWS // 8)
+    queue.add(2, 1, unpack)
+    for layer in range(2):
+        base = layer * per_layer
+        late = base + lag
+        queue.add(2 if layer == 0 else late + 1, 2, enter, layer)
+        for part in range(3):
+            queue.add(late + part, 1.5, project, layer, base + part)
+        for w in range(windows):
+            queue.add(late + 2, 5, attend, layer, w)
+        queue.add(late + 3, 1.5, branch, layer, base + 3)
+        queue.add(late + 3, 1.5, second_norm, layer)
+        for part in range(4):
+            queue.add(late + 4 + part, 3.5, widen, layer, base + 4 + part)
+            if part < 3:
+                queue.add(late + 4 + part, 1, turn, layer, part)
+        for part in range(4):
+            queue.add(late + 8 + part, 1.5, narrow, layer, base + 8 + part)
+        queue.add(late + 12, 4, turn, layer, 3)
+
+    last = total - 1 + lag
+    state = types.SimpleNamespace(tick=0)
+
+    def pump():
+        while len(loaded) < total and len(loaded) <= state.tick - whole_at:
+            i = len(loaded)
+            same = [j for j in range(i) if (chunks[j][0] == 3) == (chunks[i][0] == 3)]
+            if len(same) > 1 and same[-2] not in used:
+                break
+            fetch(i)
+            loaded.append(i)
+
+    for tick in range(last + 1):
+        state.tick = tick
+        gather.tick(tick)
+        pump()
+        queue.run(tick, pump)
+        if tick == 3:
+            eg.await_part(0)
+            for w in range(windows):
+                r.moved_grad[w] = r.g_in[r.forward_take[w]]
+    queue.run(last + total, pump, True)
+    for part in range(4):
+        ey.await_part(part)
+    for w in range(windows):
+        r.result[w] = r.y_in[r.backward_take[w]]
+    eg.finish(1)
+    ex.finish(4)
+    ey.finish(4)
+    gather.finish()
+    for layer in range(2):
+        for array in range(4):
+            swap(layer, array).wait_send()
+    for copy in saved:
+        copy.wait()
+
+
+def forward_all(blocks, small, x0, grads, tables, index, mask, moves, depths, peers):
+    count = depths * 2 * peers
+    width = x0.shape[-1]
+    hidden = blocks[2].shape[-1]
+    tall = x0.shape[0]
+    half = peers // 2
+    chunks = []
+    for layer in range(2):
+        for array, block in enumerate(blocks):
+            size = 256 if array == 3 else 1024
+            for start in range(0, block.shape[-1], size):
+                chunks.append((array, layer, slice(start, start + size)))
+    total = len(chunks)
+    unit = blocks[0].shape[1]
+    dma = pltpu.SemaphoreType.DMA
+    vmem = pltpu.VMEM
+    smem = pl.BlockSpec(memory_space=pltpu.SMEM)
+    shape = jax.ShapeDtypeStruct
+    tiles = (2, ROWS, width)
+    left = (2, peers, depths * unit, 512)
+    outs = [shape((depths, 2, peers) + b.shape[1:], LOW) for _ in range(2) for b in blocks]
+    outs += [shape(tiles, LOW), shape(tiles, LOW)]
+    outs += [shape(left, LOW)] * 3 + [shape((2, 4) + left[1:], LOW)]
+    outs += [
+        shape((2, tall, width), LOW),
+        shape((2, tall, width), WHOLE),
+        shape((2, tall, 3 * width), LOW),
+        shape((2, 16, ROWS, GROUP * KEYS), LOW),
+        shape((2, tall, hidden), LOW),
+        shape((12, width), WHOLE),
+    ]
+    exchange = (peers,) + tiles[1:]
+    scratch = [
+        vmem((count,) + small.shape, WHOLE),
+        vmem((2, 8, ROWS, GROUP * KEYS), WHOLE),
+        vmem((2, tall, width), LOW),
+        vmem(tiles, LOW),
+        vmem((2, tall, width), LOW),
+        vmem((2, tall, width), LOW),
+        vmem((2, tall, width), LOW),
+        vmem((2, tall, hidden), LOW),
+        vmem((2, tall, width), WHOLE),
+        vmem((2, tall, 3 * width), LOW),
+        vmem((2, 16, ROWS, GROUP * KEYS), LOW),
+        vmem((2, tall, hidden), LOW),
+        vmem((2, depths, 2, peers, unit, 1024), LOW),
+        vmem((2, depths, 2, peers, 4 * unit, 256), LOW),
+        vmem((tall, 1024), WHOLE),
+        vmem((3, 2, tall, width), LOW),
+        vmem((2, tall, hidden), LOW),
+        vmem((depths, 128, 512), WHOLE),
+        vmem((2, 3) + left[1:], LOW),
+        vmem((2, 4) + left[1:], LOW),
+        *[vmem(exchange, LOW)] * 6,
+        vmem((2, 2 * width), WHOLE),
+        vmem((2, hidden), WHOLE),
+        dma((total, depths - 1)),
+        dma((total, depths - 1)),
+        dma((total, half, 2)),
+        dma((total, half, 2)),
+        dma((total, 2 * half)),
+        dma((total, 2 * half)),
+        dma((total,)),
+        dma(()),
+        dma(()),
+        dma(()),
+        dma((total,)),
+        dma((32,)),
+        dma((2, 4)),
+        dma((2, 4)),
+        dma((1, peers - 1)),
+        dma((1, peers - 1)),
+        *[dma((4, peers - 1))] * 4,
+    ]
+    return pl.pallas_call(
+        functools.partial(forward_kernel, chunks, depths, peers),
+        out_shape=outs,
+        in_specs=[ANY] * 4 + [VMEM] * 6 + [smem] * 4,
+        out_specs=[ANY] * 8 + [VMEM] * 2 + [ANY] * 9 + [VMEM],
+        scratch_shapes=scratch,
+        compiler_params=pltpu.CompilerParams(
+            collective_id=3, has_side_effects=True, vmem_limit_bytes=63 * 2**20
+        ),
+    )(*blocks, small, x0, grads, tables, index, mask, *moves)
+
+
+SLOTS = 6
+
+
+class Reduce:
+    def __init__(self, place, plan, product, keep, bufs, sems):
+        self.place, self.plan, self.product, self.keep = place, plan, product, keep
+        (self.half_send, self.half_recv, self.full_send, self.full_recv, self.z_out, self.z_in, self.own_part) = bufs
+        self.r_send, self.r_recv, self.z_send, self.z_recv = sems
+        self.half = place.half
+        self.rows = self.z_out.shape[2]
+        self.cut = place.depths * self.rows // 2
+
+    def ring(self, i, step, way):
+        slot = i % SLOTS
+        if step == 1:
+            source, target = self.half_send.at[slot, way], self.half_recv.at[slot, way]
+        else:
+            source = self.full_send.at[slot, step - 2, way]
+            target = self.full_recv.at[slot, step - 2, way]
+        return remote(
+            source,
+            target,
+            self.r_send.at[slot, step - 1, way],
+            self.r_recv.at[slot, step - 1, way],
+            self.place.neighbour(1 if way == 0 else -1),
+        )
+
+    def deep(self, i, step):
+        slot = i % SLOTS
+        return remote(
+            self.z_out.at[slot, self.place.at_depth(step)],
+            self.z_in.at[slot, step - 1],
+            self.z_send.at[slot, step - 1],
+            self.z_recv.at[slot, step - 1],
+            self.place.deep(step),
+        )
+
+    def sent(self, i):
+        for way in range(2):
+            for step in range(1, self.half + 1):
+                self.ring(i, step, way).wait_send()
+        for step in range(1, self.place.depths):
+            self.deep(i, step).wait_send()
+
+    def first(self, i):
+        if i >= SLOTS:
+            self.sent(i - SLOTS)
+        slot = i % SLOTS
+        found = self.product(i, self.place.around(self.half)).astype(LOW)
+        for way in range(2):
+            self.half_send[slot, way] = found[: self.cut] if way == 0 else found[self.cut :]
+            self.ring(i, 1, way).start()
+
+    def next_step(self, i, step):
+        slot = i % SLOTS
+        cut = self.cut
+        for way in range(2):
+            turn = 1 if way == 0 else -1
+            found = self.product(i, self.place.around(turn * (self.half - step + 1)))
+            self.ring(i, step - 1, way).wait_recv()
+            target = self.full_send.at[slot, step - 2, way]
+            if step == 2:
+                came = self.half_recv[slot, way].astype(WHOLE)
+                low = found[:cut] + came if way == 0 else found[:cut]
+                high = found[cut:] if way == 0 else found[cut:] + came
+                target[:cut] = low.astype(LOW)
+                target[cut:] = high.astype(LOW)
+            else:
+                came = self.full_recv[slot, step - 3, way].astype(WHOLE)
+                target[...] = (found + came).astype(LOW)
+            self.ring(i, step, way).start()
+
+    def plane(self, i):
+        slot, rows = i % SLOTS, self.rows
+        found = self.product(i, self.place.peer)
+        for way in range(2):
+            self.ring(i, self.half, way).wait_recv()
+            found += self.full_recv[slot, self.half - 2, way].astype(WHOLE)
+        for depth in range(self.place.depths):
+            piece = found[depth * rows : (depth + 1) * rows]
+            self.z_out[slot, depth] = piece.astype(LOW)
+
+            @pl.when(depth == self.place.depth)
+            def _():
+                self.own_part[slot] = piece
+
+        for step in range(1, self.place.depths):
+            self.deep(i, step).start()
+
+    def finish(self, i):
+        slot = i % SLOTS
+        found = self.own_part[slot]
+        for step in range(1, self.place.depths):
+            self.deep(i, step).wait_recv()
+            found += self.z_in[slot, step - 1].astype(WHOLE)
+        self.keep(i, found)
+
+
+B_IN = (
+    "f0", "f1", "f2", "f3", "f4", "f5", "f6", "f7", "moved_grad", "left0", "left1", "left2", "left3", "low_x",
+    "middle", "qkv", "probs", "slope", "vec32", "index", "backward_send", "backward_take",
+)
+B_OUT = (
+    "patches_grad", "g_qkv", "g_proj", "g_up", "g_down", "small_all", "own",
+)
+B_SCRATCH = (
+    "half_send", "half_recv", "full_send", "full_recv", "z_out", "z_in", "own_part", "left_a", "left_b",
+    "right0", "right1", "right2", "right3", "wide_a", "wide_b", "slope_s", "p_s", "q_s", "mid", "x", "grad",
+    "att_grad", "total", "g_mid", "score_sum", "tiles", "e_out", "e_in", "small_mine", "small_in",
+    "small_sum", "r_send", "r_recv", "z_send", "z_recv", "swap_send", "swap_recv", "credit", "load", "state",
+    "e_send", "e_recv", "a_send", "a_recv", "a_own", "b_send", "b_recv", "b_own",
+)
+SMALL_ROWS = 96
+
+
+def backward_kernel(plan, depths, peers, *refs):
+    r = names(B_IN + B_OUT + B_SCRATCH, refs)
+    place = Place(depths, peers)
+    fulls = (r.f0, r.f1, r.f2, r.f3, r.f4, r.f5, r.f6, r.f7)
+    rights = (r.right0, r.right1, r.right2, r.right3)
+    outs = (r.g_qkv, r.g_proj, r.g_up, r.g_down)
+    windows, tall = 2, 2 * ROWS
+    total = len(plan)
+    queue = Queue(B_BUDGET)
+    done, used, loaded = set(), set(), []
+    unit = r.z_out.shape[2]
+
+    def product(i, peer):
+        layer, array, part, start = plan[i]
+        left = r.left_b[layer, part, peer] if array == 3 else r.left_a[layer, array, peer]
+        return dot(left, rights[array][:, start : start + WIDE])
+
+    def keep(i, found):
+        layer, array, part, start = plan[i]
+        outs[array][layer, part * unit : (part + 1) * unit, start : start + WIDE] = found
+
+    reduce = Reduce(
+        place,
+        plan,
+        product,
+        keep,
+        (r.half_send, r.half_recv, r.full_send, r.full_recv, r.z_out, r.z_in, r.own_part),
+        (r.r_send, r.r_recv, r.z_send, r.z_recv),
+    )
+    exchange = Exchange(place, r.e_out, r.e_in, r.e_send, r.e_recv, 1)
+
+    order = [(layer, array, part) for layer in (1, 0) for array, parts in ((3, 4), (2, 4), (1, 1), (0, 3)) for part in range(parts)]
+
+    def slot_of(k):
+        down = order[k][1] == 3
+        return sum(1 for o in order[:k] if (o[1] == 3) == down) % 2
+
+    def load(k):
+        layer, array, part = order[k]
+        full = fulls[layer * 4 + array]
+        if array == 3:
+            return pltpu.make_async_copy(full.at[part], r.wide_b.at[slot_of(k)], r.load.at[k])
+        source = full.at[:, :, :, :, part * 1024 : (part + 1) * 1024]
+        return pltpu.make_async_copy(source, r.wide_a.at[slot_of(k)], r.load.at[k])
+
+    def pump():
+        while len(loaded) < len(order):
+            k = len(loaded)
+            same = [j for j in range(k) if (order[j][1] == 3) == (order[k][1] == 3)]
+            if len(same) > 1 and same[-2] not in used:
+                break
+            load(k).start()
+            loaded.append(k)
+
+    def weight(layer, array, part):
+        k = order.index((layer, array, part))
+        assert k in loaded
+        used.add(k)
+        load(k).wait()
+        value = (r.wide_b if array == 3 else r.wide_a)[slot_of(k)]
+        return value.reshape(-1, value.shape[-1])
+
+    def swap(layer, array, part):
+        columns = slice(part * 1024, (part + 1) * 1024)
+        right = rights[array]
+        return remote(
+            right.at[0:tall, columns],
+            right.at[256 : 256 + tall, columns],
+            r.swap_send.at[array, part],
+            r.swap_recv.at[array, part],
+            place.sibling(),
+        )
+
+    def free(array):
+        pl.semaphore_signal(r.credit.at[array], inc=1, device_id=place.sibling(), device_id_type=MESH)
+
+    def hand_over(layer, array, part):
+        if layer == 0 and part == 0:
+            pl.semaphore_wait(r.credit.at[array], 1)
+        swap(layer, array, part).start()
+
+    def ready(layer, array, part):
+        if layer == 0:
+            assert (array, "freed") in done
+            swap(1, array, part).wait_send()
+
+    def put(layer, row, vector):
+        for k in range(vector.shape[1] // 128):
+            line = layer * SMALL_ROWS + row + k
+            r.small_mine[line : line + 1, :] = vector[:, k * 128 : (k + 1) * 128]
+
+    def column_sums(layer, row, value):
+        ones = jnp.ones((8, tall), LOW)
+        put(layer, row, dot(ones, value)[:1])
+
+    states = (("slope_s", "slope"), ("p_s", "probs"), ("q_s", "qkv"), ("mid", "middle"), ("x", "low_x"))
+
+    def state_copy(layer, k):
+        here, there = states[k]
+        return pltpu.make_async_copy(
+            getattr(r, there).at[layer], getattr(r, here), r.state.at[layer, k]
+        )
+
+    def left_copies(layer):
+        sources = (r.left0, r.left1, r.left2)
+        found = [
+            pltpu.make_async_copy(
+                sources[k].at[layer], r.left_a.at[layer, k], r.state.at[layer, 5 + k]
+            )
+            for k in range(3)
+        ]
+        return found + [
+            pltpu.make_async_copy(r.left3.at[layer], r.left_b.at[layer], r.state.at[layer, 8])
+        ]
+
+    def vec(k):
+        return r.vec32[k : k + 1, :]
+
+    def take_grad(layer):
+        if layer == 1:
+            for w in range(windows):
+                r.grad[w * ROWS : (w + 1) * ROWS, :] = r.moved_grad[w]
+        else:
+            exchange.await_part(0)
+            for w in range(windows):
+                r.grad[w * ROWS : (w + 1) * ROWS, :] = r.e_in[r.backward_take[w]]
+        ready(layer, 3, 0)
+        value = r.grad[...]
+        r.right3[0:tall, :] = value
+        hand_over(layer, 3, 0)
+        column_sums(layer, 88, value)
+
+    def hidden_grad(layer, part):
+        if part == 0:
+            state_copy(layer, 0).wait()
+        columns = slice(part * 1024, (part + 1) * 1024)
+        ready(layer, 2, part)
+        found = dot(r.grad[...], weight(layer, 3, part), (1, 1))
+        low = (found * r.slope_s[:, columns].astype(WHOLE)).astype(LOW)
+        r.right2[0:tall, columns] = low
+        hand_over(layer, 2, part)
+        column_sums(layer, 56 + 8 * part, low)
+        if part == 3 and layer == 1:
+            state_copy(0, 0).start()
+
+    def add_back(layer, array, part, columns):
+        found = dot(rights[array][0:tall, columns], weight(layer, array, part), (1, 1))
+        if part == 0:
+            r.total[...] = found
+        else:
+            r.total[...] += found
+
+    def up_back(layer, part):
+        add_back(layer, 2, part, slice(part * 1024, (part + 1) * 1024))
+
+    def norm_loop(source, layer, k, finish):
+        gain = vec(2 * layer + k)
+
+        def body(i, carry):
+            start = pl.multiple_of(i * 16, 16)
+            rows = pl.ds(start, 16)
+            parts, inverse = normal_parts(source[rows, :].astype(WHOLE))
+            g = r.total[rows, :]
+            e = g * gain
+            mean = jnp.mean(e, axis=1, keepdims=True)
+            along = jnp.mean(e * parts, axis=1, keepdims=True)
+            finish(rows, inverse * (e - mean - parts * along))
+            by_gain, by_shift = carry
+            return (
+                by_gain + jnp.sum(g * parts, axis=0, keepdims=True),
+                by_shift + jnp.sum(g, axis=0, keepdims=True),
+            )
+
+        zero = jnp.zeros((1, source.shape[-1]), WHOLE)
+        by_gain, by_shift = lax.fori_loop(0, tall // 16, body, (zero, zero))
+        put(layer, 8 * k, by_gain)
+        put(layer, 16 + 8 * k, by_shift)
+
+    def middle_grad(layer):
+        state_copy(layer, 3).wait()
+        ready(layer, 1, 0)
+
+        def finish(rows, found):
+            whole = r.grad[rows, :].astype(WHOLE) + found
+            r.g_mid[rows, :] = whole
+            r.right1[rows, :] = whole.astype(LOW)
+
+        norm_loop(r.mid, layer, 1, finish)
+        hand_over(layer, 1, 0)
+        column_sums(layer, 48, r.right1[0:tall, :])
+        if layer == 1:
+            state_copy(0, 3).start()
+
+    def attended_grad(layer):
+        r.att_grad[...] = dot(r.right1[0:tall, :], weight(layer, 1, 0), (1, 1)).astype(LOW)
+
+    def fold(value):
+        return sum(
+            jnp.where(lane_mask(KEYS, head), value[head * KEYS : (head + 1) * KEYS], 0.0)
+            for head in range(GROUP)
+        )[:ROWS]
+
+    def attend_back(layer, w):
+        if w == 0:
+            state_copy(layer, 1).wait()
+            state_copy(layer, 2).wait()
+            for part in range(3):
+                ready(layer, 0, part)
+
+        def step(g, carry):
+            rows = slice(w * ROWS, (w + 1) * ROWS)
+            start = pl.multiple_of(g * 128, 128)
+            q = r.q_s[rows, pl.ds(start, 128)]
+            k = r.q_s[rows, pl.ds(start + 1024, 128)]
+            v = r.q_s[rows, pl.ds(start + 2048, 128)]
+            out_grad = r.att_grad[rows, pl.ds(start, 128)]
+            low = r.p_s[w * 8 + g]
+            prob_grad = dot(out_grad, per_head(v), (1, 1))
+            pieces = []
+            for head in range(GROUP):
+                one = slice(head * KEYS, (head + 1) * KEYS)
+                probs = low[:, one].astype(WHOLE)
+                weighed = probs * prob_grad[:, one]
+                pieces.append(weighed - probs * jnp.sum(weighed, axis=1, keepdims=True))
+            score_grad = jnp.concatenate(pieces, axis=1).astype(LOW)
+            if w == 0:
+                r.score_sum[g] = score_grad.astype(WHOLE)
+            else:
+                r.score_sum[g] += score_grad.astype(WHOLE)
+            by_query = dot(score_grad, per_head(k)) * SCALE
+            by_key = fold(dot(score_grad, q, (0, 0))) * SCALE
+            by_value = fold(dot(low, out_grad, (0, 0)))
+            for part, found in enumerate((by_query, by_key, by_value)):
+                r.right0[rows, pl.ds(start + part * 1024, 128)] = found.astype(LOW)
+            return carry
+
+        lax.fori_loop(0, 8, step, 0)
+        if w == windows - 1:
+            for part in range(3):
+                hand_over(layer, 0, part)
+            column_sums(layer, 32, r.right0[0:tall, 0:1024])
+            column_sums(layer, 40, r.right0[0:tall, 2048:3072])
+            if layer == 1:
+                state_copy(0, 1).start()
+                state_copy(0, 2).start()
+
+    def qkv_back(layer, part):
+        add_back(layer, 0, part, slice(part * 1024, (part + 1) * 1024))
+
+    def input_grad(layer):
+        state_copy(layer, 4).wait()
+
+        def finish(rows, found):
+            r.g_mid[rows, :] = r.g_mid[rows, :] + found
+
+        norm_loop(r.x, layer, 0, finish)
+        if layer == 1:
+            state_copy(0, 4).start()
+            for w in range(windows):
+                r.tiles[w] = r.g_mid[w * ROWS : (w + 1) * ROWS, :].astype(LOW)
+            exchange.give(0, r.tiles, r.backward_send)
+        else:
+            for w in range(windows):
+                r.patches_grad[w * WIN : (w + 1) * WIN, :] = r.g_mid[w * ROWS : w * ROWS + WIN, :]
+
+    def table_grad(layer):
+        buckets = lax.broadcasted_iota(jnp.int32, (384, KEYS), 0)
+
+        def step(i, found):
+            line = r.index[pl.ds(i, 1), :]
+            hot = jnp.where(buckets == line, 1.0, 0.0).astype(LOW)
+            value = r.score_sum[:, pl.ds(i, 1), :].reshape(8, GROUP * KEYS)
+            value = jnp.concatenate(
+                [value[:, head * KEYS : (head + 1) * KEYS] for head in range(GROUP)], axis=0
+            )
+            high = value.astype(LOW)
+            rest = (value - high.astype(WHOLE)).astype(LOW)
+            return found + dot(jnp.concatenate([high, rest], axis=0), hot, (1, 1))
+
+        found = lax.fori_loop(0, 100, step, jnp.zeros((64, 384), WHOLE))
+        found = found[:32] + found[32:]
+        base = 2 * SMALL_ROWS + layer * SMALL_ROWS
+        for k in range(3):
+            r.small_mine[base + 32 * k : base + 32 * (k + 1), :] = found[:, 128 * k : 128 * (k + 1)]
+
+    def send_small():
+        def step(k, carry):
+            outer, peer = place.other(k)
+            remote(
+                r.small_mine.at[pl.ds(pl.multiple_of((outer * peers + peer) * 16, 16), 16)],
+                r.small_in.at[place.index],
+                r.a_send,
+                r.a_recv,
+                (outer, peer),
+            ).start()
+            return carry
+
+        lax.fori_loop(1, place.total, step, 0)
+        own_small().start()
+
+    def own_small():
+        mine = r.small_mine.at[pl.ds(pl.multiple_of(place.index * 16, 16), 16)]
+        return pltpu.make_async_copy(mine, r.small_in.at[place.index], r.a_own)
+
+    spread = Spread(place, r.small_sum, r.small_all, r.b_send, r.b_recv, r.b_own)
+
+    def sum_small():
+        rest = r.small_in.at[pl.ds(0, place.total - 1)]
+        both = remote(rest, rest, r.a_send, r.a_recv, place.other(1))
+        both.wait_send()
+        both.wait_recv()
+        own_small().wait()
+        r.small_sum[...] = jnp.sum(r.small_in[...], axis=0)
+        spread.start()
+
+    def own_vectors():
+        starts = ((0, 4), (8, 4), (16, 4), (24, 4), (32, 2), (48, 4), (56, 1), (88, 4))
+        for layer in range(2):
+            for k, (row, each) in enumerate(starts):
+                line = layer * SMALL_ROWS + row + lax.div(place.index, each)
+                found = r.small_all[lax.div(line, 16), pl.ds(lax.rem(line, 16), 1), :]
+                back = lax.rem(each - lax.rem(place.index, each), each) * (128 // each)
+                r.own[8 * layer + k : 8 * layer + k + 1, :] = pltpu.roll(found, back, 1)
+
+    def note(work, *what):
+        work(*what)
+        done.add((work.__name__, *what))
+
+    def add(tick, cost, work, *what):
+        queue.add(tick, cost, note, work, *what)
+
+    for k in range(5):
+        state_copy(1, k).start()
+    for layer in (1, 0):
+        for copy in left_copies(layer):
+            copy.start()
+    for right in rights:
+        zero = jnp.zeros((256 - tall, right.shape[1]), LOW)
+        right[tall:256, :] = zero
+        right[256 + tall : 512, :] = zero
+    r.small_mine[...] = jnp.zeros(r.small_mine.shape, WHOLE)
+    pump()
+    place.greet()
+
+    add(0, 1, take_grad, 1)
+    last_use = {
+        array: max(i for i, p in enumerate(plan) if p[0] == 1 and p[1] == array) for array in range(4)
+    }
+    after = {array: last_use[array] + GAP * place.half for array in range(4)}
+    for layer in (1, 0):
+        late = 9 if layer == 0 else 0
+        if layer == 0:
+            add(0, 5, table_grad, 1)
+            add(late, 1, take_grad, 0)
+        for part in range(4):
+            add(late and after[2], 2, hidden_grad, layer, part)
+        for part in range(4):
+            add(late, 2, up_back, layer, part)
+        add(late and after[1], 3, middle_grad, layer)
+        add(late, 1.5, attended_grad, layer)
+        for w in range(windows):
+            add(late and after[0], 7, attend_back, layer, w)
+        for part in range(3):
+            add(late, 1.5, qkv_back, layer, part)
+        add(late, 3, input_grad, layer)
+    add(0, 5, table_grad, 0)
+    add(0, 1, send_small)
+
+    needs = {3: ("take_grad",), 2: ("hidden_grad",), 1: ("middle_grad",), 0: ("attend_back",)}
+
+    def wanted(i):
+        layer, array, part, start = plan[i]
+        what = needs[array] + (layer,)
+        if array == 2:
+            what += (start // 1024,)
+        if array == 0:
+            what += (windows - 1,)
+        return what
+
+    received, lefts_in = set(), set()
+    half = place.half
+    for tick in range(total + GAP * (half + 1)):
+        if tick < total:
+            layer, array, part, start = plan[tick]
+            while wanted(tick) not in done:
+                queue.step(pump)
+            if layer not in lefts_in:
+                lefts_in.add(layer)
+                for copy in left_copies(layer):
+                    copy.wait()
+            key = (layer, array, start // 1024)
+            if key not in received:
+                received.add(key)
+                swap(*key).wait_recv()
+            reduce.first(tick)
+        for step in range(2, half + 1):
+            i = tick - GAP * (step - 1)
+            if 0 <= i < total:
+                reduce.next_step(i, step)
+        i = tick - GAP * half
+        if 0 <= i < total:
+            reduce.plane(i)
+            for array, last in last_use.items():
+                if i == last:
+                    free(array)
+                    done.add((array, "freed"))
+        i = tick - GAP * (half + 1)
+        if 0 <= i < total:
+            reduce.finish(i)
+        queue.run(tick, pump)
+        if ("send_small",) in done and ("sum_small",) not in done and tick >= total - 1:
+            note(sum_small)
+    assert not queue.pieces
+    if ("sum_small",) not in done:
+        sum_small()
+    spread.wait()
+    own_vectors()
+    exchange.finish(1)
+    for array, parts in ((3, 1), (2, 4), (1, 1), (0, 3)):
+        for part in range(parts):
+            swap(0, array, part).wait_send()
+    for i in range(total - SLOTS, total):
+        reduce.sent(i)
+
+
+def backward_all(fulls, state, index, moves, depths, peers):
+    moved_grad, left0, left1, left2, left3, low_x, middle, qkv, probs, slope, vec32 = state
+    count = depths * 2 * peers
+    tall, width = low_x.shape[1:]
+    hidden = slope.shape[-1]
+    unit = width // count
+    half = peers // 2
+    plan = []
+    for layer in (1, 0):
+        plan += [(layer, 3, part, 0) for part in range(4)]
+        plan += [(layer, 2, 0, start) for start in range(0, hidden, WIDE)]
+        plan += [(layer, 1, 0, 0)]
+        plan += [(layer, 0, 0, start) for start in range(0, 3 * width, WIDE)]
+    dma = pltpu.SemaphoreType.DMA
+    vmem = pltpu.VMEM
+    smem = pl.BlockSpec(memory_space=pltpu.SMEM)
+    shape = jax.ShapeDtypeStruct
+    flat = depths * unit
+    outs = [
+        shape((2 * WIN, width), WHOLE),
+        shape((2, unit, 3 * width), WHOLE),
+        shape((2, unit, width), WHOLE),
+        shape((2, unit, hidden), WHOLE),
+        shape((2, 4 * unit, width), WHOLE),
+        shape((count, 16, 128), WHOLE),
+        shape((16, 128), WHOLE),
+    ]
+    scratch = [
+        vmem((SLOTS, 2, flat // 2, WIDE), LOW),
+        vmem((SLOTS, 2, flat // 2, WIDE), LOW),
+        vmem((SLOTS, half - 1, 2, flat, WIDE), LOW),
+        vmem((SLOTS, half - 1, 2, flat, WIDE), LOW),
+        vmem((SLOTS, depths, unit, WIDE), LOW),
+        vmem((SLOTS, depths - 1, unit, WIDE), LOW),
+        vmem((SLOTS, unit, WIDE), WHOLE),
+        vmem((2, 3) + left0.shape[1:], LOW),
+        vmem(left3.shape, LOW),
+        vmem((512, 3 * width), LOW),
+        vmem((512, width), LOW),
+        vmem((512, hidden), LOW),
+        vmem((512, width), LOW),
+        vmem((2, depths, 2, peers, unit, 1024), LOW),
+        vmem((2, 2, peers, 4 * unit, width), LOW),
+        vmem((tall, hidden), LOW),
+        vmem(probs.shape[1:], LOW),
+        vmem((tall, 3 * width), LOW),
+        vmem((tall, width), WHOLE),
+        vmem((tall, width), LOW),
+        vmem((tall, width), LOW),
+        vmem((tall, width), LOW),
+        vmem((tall, width), WHOLE),
+        vmem((tall, width), WHOLE),
+        vmem((8, ROWS, GROUP * KEYS), WHOLE),
+        vmem((2, ROWS, width), LOW),
+        vmem((peers, ROWS, width), LOW),
+        vmem((peers, ROWS, width), LOW),
+        vmem((count * 16, 128), WHOLE),
+        vmem((count, 16, 128), WHOLE),
+        vmem((16, 128), WHOLE),
+        dma((SLOTS, half, 2)),
+        dma((SLOTS, half, 2)),
+        dma((SLOTS, depths - 1)),
+        dma((SLOTS, depths - 1)),
+        dma((4, 4)),
+        dma((4, 4)),
+        pltpu.SemaphoreType.REGULAR((4,)),
+        dma((24,)),
+        dma((2, 9)),
+        dma((1, peers - 1)),
+        dma((1, peers - 1)),
+        *[dma(())] * 6,
+    ]
+    return pl.pallas_call(
+        functools.partial(backward_kernel, plan, depths, peers),
+        out_shape=outs,
+        in_specs=[ANY] * 8 + [VMEM] + [ANY] * 9 + [VMEM] * 2 + [smem] * 2,
+        out_specs=[VMEM] * 7,
+        scratch_shapes=scratch,
+        compiler_params=pltpu.CompilerParams(
+            collective_id=4, has_side_effects=True, vmem_limit_bytes=63 * 2**20
+        ),
+    )(*fulls, *state, index, *moves)
+
+
+def whole_shards(
+    outer_count,
+    peer_count,
+    patches,
+    out_grad,
+    norm_gain,
+    norm_shift,
+    qkv_weight,
+    qv_bias,
+    rel_table,
+    proj_weight,
+    proj_bias,
+    up_weight,
+    up_bias,
+    down_weight,
+    down_bias,
+    tile_perm,
+    window_slot,
+    mask_ids,
+    bias_index,
+):
+    windows = patches.shape[0] // WIN
+    width = patches.shape[1]
+    depths = outer_count // 2
+    device_index = lax.axis_index(("dp", "fsdp"))
+    slot_ids = jnp.arange(tile_perm.shape[0], dtype=jnp.int32)
+
+    def one_hot_pick(keys, values):
+        return jnp.sum(jnp.where(keys[None, :] == slot_ids[:, None], values[None, :], 0), axis=1)
+
+    def look_up(values, at):
+        hit = at[:, None] == jnp.arange(values.shape[0], dtype=jnp.int32)[None, :]
+        return jnp.sum(jnp.where(hit, values[None, :], 0), axis=1)
+
+    source_of = one_hot_pick(window_slot, look_up(window_slot, tile_perm))
+    target_of = one_hot_pick(source_of, slot_ids)
+    region_slot = one_hot_pick(window_slot, mask_ids)
+    own_slots = device_index * windows + jnp.arange(windows, dtype=jnp.int32)
+    forward_take = look_up(source_of, own_slots) // windows % peer_count
+    backward_take = look_up(target_of, own_slots) // windows % peer_count
+    spots = jnp.arange(peer_count, dtype=jnp.int32)
+    numbers = jnp.arange(windows, dtype=jnp.int32)
+
+    def window_for(peers):
+        return jnp.sum(jnp.where(peers[None, :] == spots[:, None], numbers[None, :], 0), axis=1)
+
+    moves = (window_for(backward_take), forward_take, window_for(forward_take), backward_take)
+    mask = region_mask(look_up(region_slot, own_slots))[:, 0]
+    mask = jnp.pad(mask, ((0, 0), (0, ROWS - WIN), (0, KEYS - WIN)))
+    index = jnp.pad(
+        bias_index, ((0, ROWS - WIN), (0, KEYS - WIN)), constant_values=rel_table.shape[1]
+    )
+    tables = rel_table.reshape(2, -1, HEADS // GROUP, GROUP).transpose(0, 3, 2, 1)
+    tables = tables.reshape(2 * HEADS, -1)
+    tables = jnp.pad(tables, ((0, 0), (0, 384 - tables.shape[1])), constant_values=NEVER)
+
+    each = width // (outer_count * peer_count)
+    small = jnp.concatenate(
+        [
+            norm_gain.reshape(1, 4 * each),
+            norm_shift.reshape(1, 4 * each),
+            jnp.concatenate([proj_bias, down_bias], axis=0).reshape(1, 4 * each),
+            qv_bias.reshape(1, 4 * each),
+            up_bias,
+            jnp.zeros((2, 4 * each), LOW),
+        ],
+        axis=0,
+    ).astype(jnp.float32)
+
+    def padded(rows):
+        return jnp.pad(rows.reshape(windows, WIN, width), ((0, 0), (0, ROWS - WIN), (0, 0)))
+
+    found = forward_all(
+        (qkv_weight, proj_weight, up_weight, down_weight),
+        small,
+        padded(patches).reshape(windows * ROWS, width),
+        padded(out_grad),
+        tables,
+        index,
+        mask,
+        moves,
+        depths,
+        peer_count,
+    )
+    fulls, moved_grad, result, state = found[:8], found[8], found[9], found[10:]
+    grad_patches, grad_qkv, grad_proj, grad_up, grad_down, small_all, own = backward_all(
+        fulls, (moved_grad, *state), index, moves[2:], depths, peer_count
+    )
+
+    def trimmed(rows):
+        return rows.reshape(windows, ROWS, width)[:, :WIN].reshape(windows * WIN, width)
+
+    flat = small_all.reshape(-1)
+    per_layer = SMALL_ROWS * 128
+    own = own.reshape(2, 8, 128)
+    gain_grad, shift_grad = own[:, 0:2, :each], own[:, 2:4, :each]
+    qv_grad, proj_b_grad = own[:, 4, : 2 * each], own[:, 5, :each]
+    up_b_grad, down_b_grad = own[:, 6], own[:, 7, :each]
+    table = flat[2 * per_layer : 4 * per_layer].reshape(2, 3, GROUP, HEADS // GROUP, 128)
+    table = table.transpose(0, 1, 4, 3, 2).reshape(2, 3 * 128, HEADS)[:, : rel_table.shape[1]]
+    return (
+        trimmed(result),
+        grad_patches,
+        gain_grad,
+        shift_grad,
+        grad_qkv,
+        qv_grad,
+        table,
+        grad_proj,
+        proj_b_grad,
+        grad_up,
+        up_b_grad,
+        grad_down,
+        down_b_grad,
+    )
+
+
 def solution(mesh):
+    outer_count, peer_count = mesh.shape["dp"], mesh.shape["fsdp"]
+    fused = outer_count == 8 and peer_count == 4
     placed = (
         P(("dp", "fsdp"), None),
         P(("dp", "fsdp"), None),
@@ -922,7 +2285,7 @@
         P(),
     )
     return jax.shard_map(
-        functools.partial(shards, mesh.shape["dp"], mesh.shape["fsdp"]),
+        functools.partial(whole_shards if fused else shards, outer_count, peer_count),
         mesh=mesh,
         in_specs=placed,
         out_specs=(

time: 897 us -> 541 us (0.60)
  local copies, waits for them, and re-layouts: 181 us -> 27.1 us
  matrix products: 135 us -> 0 us
  other arithmetic: 54.2 us -> 4.65 us
  Pallas kernels: 476 us -> 501 us
  starting transfers between devices: 24.8 us -> 0 us
  waiting for transfers between devices: 10.5 us -> 0 us
    dot_general x32 -> x0, matrix products: 135 us -> none  [the longest x2 25.2 us: block_backward(): jnp.einsum('rd,fd->rf', grad_down_low, w_down, preferred_element_type=jnp...]
    broadcast_in_dim x58 -> x1, local copies, waits for them, and re-layouts: 49 us -> 0.01 us  [whole_shards(): jnp.zeros((2, 4 * each), LOW)]
    transpose x20 -> x0, local copies, waits for them, and re-layouts: 26.6 us -> none  [the longest x12 14.2 us: sum_all(): turned = jnp.pad(left, ((0, padded - tokens), (0, 0))).T]
    all_to_all x4 -> x0, starting transfers between devices: 24.8 us -> none  [move(): lax.all_to_all(sectioning, 'fsdp', split_axis=0, concat_axis=0, tiled=True)]
    pallas_call x3 -> x2, Pallas kernels: 476 us -> 501 us  [the longest x1 258 us: forward_all(): pl.pallas_call(functools.partial(forward_kernel, chunks, depths, peers),...]
    convert_element_type x19 -> x0, local copies, waits for them, and re-layouts: 24.2 us -> none  [the longest x6 9.55 us: block_backward(): grad_qkv_low = jnp.stack([grad_query, grad_key, grad_value], axis=2).resh...]
    reduce_sum x16 -> x2, other arithmetic: 20.9 us -> 1.19 us  [window_for(): jnp.sum(jnp.where(peers[None, :] == spots[:, None], numbers[None, :], 0),...]
    reshape x29 -> x11, local copies, waits for them, and re-layouts: 21.8 us -> 6.95 us  [the longest x2 2.17 us: padded(): rows.reshape(windows, WIN, width)]
  transfers between devices with their start and end apart: 4 -> 0, of which waited for: 1 -> 0; matrix products, arithmetic and copies ran while one was open for 14% -> 0% of each run, Pallas kernels for 13% -> 0%
where the time goes in v2:
time: 541 us; the launch traced here: 534 us
  Pallas kernels  501 us (93%)
  local copies, waits for them, and re-layouts  27.1 us (5%)
    pallas_call x1, Pallas kernels, forward_all(): pl.pallas_call(functools.partial(forward_kernel, chunks, depths, peers),...  258 us
    pallas_call x1, Pallas kernels, backward_all(): pl.pallas_call(functools.partial(backward_kernel, plan, depths, peers), o...  243 us

profile of v2, /device:TPU:0, one launch (start us, length us, event | category | flops | bytes accessed | tf_op | source)
XLA Modules:
  0.0 533.7 jit_solution(17042319956786095186)
XLA Ops:
  0.7 0.8 reshape.317
  1.4 0.8 reshape.318
  2.2 0.7 reshape.320
  2.9 0.8 select_reduce_fusion.2
  3.8 0.8 select_reduce_fusion.1
  5.0 0.6 fusion.1.refs_12_.refs_20_
  6.2 0.7 pad_maximum_fusion
  6.9 0.7 concatenate.7
  7.7 0.6 convert_element_type.24.refs_4_
  8.3 0.8 reshape.324
  9.1 0.6 pad.21.refs_7_
  9.8 1.4 pad.22.refs_8_.refs_19_
  11.3 0.7 pad.23.refs_9_
  12.0 1.1 reshape.321
  13.1 0.8 pad.19
  13.9 1.1 reshape.323
  15.0 0.8 pad.20.refs_6_
  15.8 258.2 %shard_map.264 = (bf16[4,2,4,32,3072]{4,3,2,1,0:T(8,128)(2,1)}, bf16[4,2,4,32,1024]{4,3,2,1,0:T(8,128)(2,1)}, bf16[4,2,4,32,4096]{4,3,2,1,0:T(8,128)(2,1)}, bf16...) custom-call(bf16[2,32,3072]{2,1,0:T(8,128)(2,1)} %refs_0_.1, ...), custom_call_target="tpu_custom_call" | custom-call | tf_op jit(solution)/shard_map/pallas_call | solution.py:1512
  274.0 1.0 slice.28
  275.0 0.8 reshape.326
  275.9 242.7 %shard_map.265 = (f32[200,1024]{1,0:T(8,128)}, f32[2,32,3072]{2,1,0:T(8,128)}, f32[2,32,1024]{2,1,0:T(8,128)}, f32[2,32,4096]{2,1,0:T(8,128)}, f32[2,128,1024]{2...) custom-call(bf16[4,2,4,32,3072]{4,3,2,1,0:T(8,128)(2,1)} %get-tuple-element.41.refs_0_, ...), custom_call_target="tpu_custom_call" | custom-call | tf_op jit(solution)/shard_map/pallas_call | solution.py:2136
  518.6 1.4 slice.39
  520.0 1.3 slice.42
  521.3 1.3 fusion.5
  522.6 1.4 fusion.6
  524.0 0.9 slice.32
  525.0 0.7 reshape.329
  525.7 2.1 copy.47
  527.8 2.1 copy.48
  529.9 1.7 copy.49
  531.5 1.0 copy.50
  532.5 1.0 copy.51
  (21 shorter events, 1.3 us)
Async XLA Ops:
  4.9 10.8 %copy-start.2 = (s32[2]{0:T(128)}, s32[2]{0:T(128)S(1)}, u32[]{:S(2)}) copy-start(s32[2]{0:T(128)S(1)} %get-tuple-element.79.refs_13_.refs_21_) | copy-start | bytes 28
  5.0 10.8 %copy-start.3 = (s32[2]{0:T(128)}, s32[2]{0:T(128)S(1)}, u32[]{:S(2)}) copy-start(s32[2]{0:T(128)S(1)} %get-tuple-element.78.refs_11_) | copy-start | bytes 28
  518.6 12.9 %copy-start.1 = (f32[2,32,4096]{2,1,0:T(8,128)S(1)}, f32[2,32,4096]{2,1,0:T(8,128)}, u32[]{:S(2)}) copy-start(f32[2,32,4096]{2,1,0:T(8,128)} %get-tuple-element.104) | copy-start | bytes 3145732
  518.6 13.9 %copy-start = (f32[2,128,1024]{2,1,0:T(8,128)S(1)}, f32[2,128,1024]{2,1,0:T(8,128)}, u32[]{:S(2)}) copy-start(f32[2,128,1024]{2,1,0:T(8,128)} %get-tuple-element.106) | copy-start | bytes 3145732

commit v3 on v2

--- a/solution.py
+++ b/solution.py
@@ -903,8 +903,8 @@
 
 
 ROWS = 112
-GAP = 2
-AHEAD = 4
+GAP, F_GAP = 2, 1
+EARLY = {12: 1, 20: 9}
 F_BUDGET, B_BUDGET = 5.0, 5.0
 KEYS = 128
 GROUP = 4
@@ -912,10 +912,6 @@
 LOW = jnp.bfloat16
 WHOLE = jnp.float32
 NEVER = -1e30
-
-
-def names(words, refs):
-    return types.SimpleNamespace(**dict(zip(words, refs, strict=True)))
 
 
 class Queue:
@@ -1010,20 +1006,34 @@
 
 
 class Gather:
-    def __init__(self, place, chunks, blocks, fulls, sems):
+    def __init__(self, place, chunks, early, blocks, fulls, sems):
         self.place, self.chunks, self.blocks, self.fulls = place, chunks, blocks, fulls
         (self.z_send, self.z_recv, self.r_send, self.r_recv, self.c_send, self.c_recv, self.own_sem) = sems
         self.half, self.cut = place.half, place.depths // 2
-
-    def view(self, i, depth, peer):
+        self.early = early
+        self.late = [i for i in range(len(chunks)) if i not in early]
+        self.begun = 0
+        self.gone = len(self.late) - 1 + F_GAP * self.half
+        assert place.depths == 2 * self.half
+
+    def whole_at(self, i):
+        if i in self.early:
+            return max(self.whole_at(i - 1), self.early[i] + 2 * self.half + 2 * self.place.depths - 1)
+        return self.late.index(i) + F_GAP * self.half
+
+    def full(self, i):
         array, layer, columns = self.chunks[i]
-        return self.fulls[layer * len(self.blocks) + array].at[
-            depth, self.place.core, peer, :, columns
-        ]
-
-    def block(self, i):
+        return self.fulls[layer * len(self.blocks) + array]
+
+    def view(self, i, depth, peer, rows=slice(None)):
+        return self.full(i).at[depth, self.place.core, peer, rows, self.chunks[i][2]]
+
+    def plane(self, i, depth):
+        return self.full(i).at[depth, self.place.core, :, :, self.chunks[i][2]]
+
+    def block(self, i, rows=slice(None)):
         array, layer, columns = self.chunks[i]
-        return self.blocks[array].at[layer, :, columns]
+        return self.blocks[array].at[layer, rows, columns]
 
     def own(self, i):
         place = self.place
@@ -1033,71 +1043,110 @@
 
     def deep(self, i, step):
         place = self.place
+        if i in self.early:
+            source = target = self.plane(i, place.depth)
+        else:
+            source, target = self.block(i), self.view(i, place.depth, place.peer)
         return remote(
-            self.block(i),
-            self.view(i, place.depth, place.peer),
+            source,
+            target,
             self.z_send.at[i, step - 1],
             self.z_recv.at[i, step - 1],
             place.deep(step),
         )
 
-    def part(self, step, way):
-        if step < self.half:
-            return slice(None)
-        return slice(0, self.cut) if way == 0 else slice(self.cut, self.place.depths)
-
     def ring(self, i, step, way):
+        place = self.place
         turn = 1 if way == 0 else -1
-        here = self.view(i, self.part(step, way), self.place.around(-turn * (step - 1)))
+        peer = place.around(-turn * (step - 1))
+        if i in self.early:
+            rows = slice(None)
+            if step == self.half:
+                cut = self.full(i).shape[3] // 2
+                rows = slice(0, cut) if way == 0 else slice(cut, 2 * cut)
+            target = self.view(i, place.depth, peer, rows)
+            source = self.block(i, rows) if step == 1 else target
+        else:
+            depths = slice(None)
+            if step == self.half:
+                depths = slice(0, self.cut) if way == 0 else slice(self.cut, place.depths)
+            source = target = self.view(i, depths, peer)
         return remote(
-            here,
-            here,
+            source,
+            target,
             self.r_send.at[i, step - 1, way],
             self.r_recv.at[i, step - 1, way],
-            self.place.neighbour(turn),
+            place.neighbour(turn),
         )
 
     def across(self, i, slot):
-        step = (slot + 1) // 2
-        turn = 1 if slot % 2 else -1
-        here = self.view(i, slice(None), self.place.around(-turn * step))
-        return remote(
-            here, here, self.c_send.at[i, slot], self.c_recv.at[i, slot], self.place.sibling()
-        )
+        place = self.place
+        if i in self.early:
+            here = self.plane(i, place.at_depth(-slot))
+        else:
+            step = (slot + 1) // 2
+            turn = 1 if slot % 2 else -1
+            here = self.view(i, slice(None), place.around(-turn * step))
+        return remote(here, here, self.c_send.at[i, slot], self.c_recv.at[i, slot], place.sibling())
 
     def begin(self, i):
         for step in range(1, self.place.depths):
             self.deep(i, step).start()
         self.own(i).start()
 
+    def start_ring(self, i):
+        self.ring(i, 1, 0).start()
+        self.ring(i, 1, 1).start()
+
     def first(self, i):
         self.own(i).wait()
         for step in range(1, self.place.depths):
             self.deep(i, step).wait_recv()
-        self.ring(i, 1, 0).start()
-        self.ring(i, 1, 1).start()
+        self.start_ring(i)
         self.across(i, 0).start()
 
     def later(self, i, step):
         self.ring(i, step, 0).wait_recv()
         self.ring(i, step, 1).wait_recv()
+        early = i in self.early
         if step < self.half:
             self.ring(i, step + 1, 0).start()
             self.ring(i, step + 1, 1).start()
-            self.across(i, 2 * step - 1).start()
-            self.across(i, 2 * step).start()
+            if not early:
+                self.across(i, 2 * step - 1).start()
+                self.across(i, 2 * step).start()
+        elif early:
+            self.own(i).wait()
+            self.across(i, 0).start()
         else:
             self.across(i, 2 * step - 1).start()
 
+    def spread_planes(self, i):
+        for step in range(1, self.place.depths):
+            self.deep(i, step).wait_recv()
+            self.across(i, step).start()
+
     def tick(self, tick):
-        total = len(self.chunks)
-        if tick + AHEAD < total:
-            self.begin(tick + AHEAD)
-        if tick < total:
-            self.first(tick)
+        late = self.late
+        for i, start in self.early.items():
+            if tick == start:
+                self.own(i).start()
+                self.start_ring(i)
+            step, odd = divmod(tick - start, 2)
+            if 1 <= step <= self.half and not odd:
+                self.later(i, step)
+            if 0 <= step - self.half < self.place.depths - 1 and not odd:
+                self.deep(i, step - self.half + 1).start()
+            if tick == self.whole_at(i):
+                self.spread_planes(i)
+        while self.begun < min(len(late), tick + 1 + min(2 + (tick + 1) // 2, 6)):
+            self.begin(late[self.begun])
+            self.begun += 1
+        if tick < len(late):
+            self.first(late[tick])
         for step in range(1, self.half + 1):
-            if 0 <= tick - step * GAP < total:
-                self.later(tick - step * GAP, step)
+            if 0 <= tick - step * F_GAP < len(late):
+                self.later(late[tick - step * F_GAP], step)
 
     def await_across(self, i):
         for slot in range(2 * self.half):
@@ -1114,29 +1163,23 @@
                     self.ring(i, step, way).wait_send()
 
 
-F_IN = (
-    "w0", "w1", "w2", "w3", "small", "x0", "grads", "tables", "index", "mask", "forward_send", "forward_take",
-    "backward_send", "backward_take",
-)
-F_OUT = (
-    "f0", "f1", "f2", "f3", "f4", "f5", "f6", "f7", "moved_grad", "result", "left0", "left1", "left2",
-    "left3", "low_x", "middle", "qkv", "probs", "slope", "vec32",
-)
-F_SCRATCH = (
-    "small_full", "bias", "x", "x0w", "normed", "att", "normed_two", "act", "mid", "q_s", "p_s", "slope_s", "wide_a",
-    "wide_b", "total", "sib_a", "sib_b", "turned", "left_a", "left_b", "g_out", "g_in", "x_out", "x_in",
-    "y_out", "y_in", "vec64", "vec128", "z_send", "z_recv", "r_send", "r_recv", "c_send", "c_recv", "own_sem",
-    "s_send", "s_recv", "s_own", "load", "save", "swap_send", "swap_recv", "eg_send", "eg_recv", "ex_send",
-    "ex_recv", "ey_send", "ey_recv",
-)
-
-
 def forward_kernel(chunks, depths, peers, *refs):
-    r = names(F_IN + F_OUT + F_SCRATCH, refs)
+    r = types.SimpleNamespace()
+    (
+        r.w0, r.w1, r.w2, r.w3, r.small, r.x0, r.grads, r.tables, r.index, r.mask, r.forward_send,
+        r.forward_take, r.backward_send, r.backward_take, r.f0, r.f1, r.f2, r.f3, r.f4, r.f5, r.f6, r.f7,
+        r.moved_grad, r.result, r.left0, r.left1, r.left2, r.left3, r.low_x, r.middle, r.qkv, r.probs,
+        r.slope, r.vec32, r.small_full, r.bias, r.x, r.x0w, r.normed, r.att, r.normed_two, r.act, r.mid,
+        r.q_s, r.p_s, r.slope_s, r.wide_a, r.wide_b, r.total, r.sib_a, r.sib_b, r.turned, r.left_a, r.left_b,
+        r.g_out, r.g_in, r.x_out, r.x_in, r.y_out, r.y_in, r.vec64, r.vec128, r.z_send, r.z_recv, r.r_send,
+        r.r_recv, r.c_send, r.c_recv, r.own_sem, r.s_send, r.s_recv, r.s_own, r.load, r.save, r.swap_send,
+        r.swap_recv, r.eg_send, r.eg_recv, r.ex_send, r.ex_recv, r.ey_send, r.ey_recv,
+    ) = refs
     place = Place(depths, peers)
     gather = Gather(
         place,
         chunks,
+        EARLY,
         (r.w0, r.w1, r.w2, r.w3),
         (r.f0, r.f1, r.f2, r.f3, r.f4, r.f5, r.f6, r.f7),
         (r.z_send, r.z_recv, r.r_send, r.r_recv, r.c_send, r.c_recv, r.own_sem),
@@ -1231,6 +1274,13 @@
     def vec(k):
         return r.vec32[k : k + 1, :]
 
+    def pad_windows(source):
+        flat = r.mid.at[1]
+        flat[0 : windows * WIN, :] = source[...].astype(WHOLE)
+        r.total[...] = jnp.zeros(r.total.shape, WHOLE)
+        for w in range(windows):
+            r.total[w * ROWS : w * ROWS + WIN, :] = flat[w * WIN : (w + 1) * WIN, :]
+
     def norm(source, target, layer, k):
         gain, shift = vec(2 * layer + k), vec(4 + 2 * layer + k)
 
@@ -1244,7 +1294,8 @@
     def enter(layer):
         x = r.x.at[layer]
         if layer == 0:
-            x[...] = r.x0[...]
+            pad_windows(r.x0)
+            x[...] = r.total[...].astype(LOW)
         else:
             for part in range(4):
                 ex.await_part(part)
@@ -1369,40 +1420,43 @@
             spill(r.left_a.at[layer, array], (r.left0, r.left1, r.left2)[array].at[layer])
 
     place.greet()
-    gather.begin(0)
+    for i in range(2):
+        gather.begin(gather.late[i])
+        gather.begun += 1
+    pad_windows(r.grads)
+    for w in range(windows):
+        r.x0w[w] = r.total[w * ROWS : (w + 1) * ROWS, :].astype(LOW)
+    eg.give(0, r.x0w, r.forward_send)
     spread.start()
-    eg.give(0, r.grads, r.forward_send)
-    for i in range(1, AHEAD):
-        gather.begin(i)
-
-    whole_at = GAP * place.half + 1
-    lag = whole_at + 1
+
+    def at(layer, part):
+        return gather.whole_at(layer * per_layer + part) + 2
+
     queue.add(0, 5, bias_rows, 0, 7)
     queue.add(0, 5, bias_rows, 7, ROWS // 8)
     queue.add(2, 1, unpack)
     for layer in range(2):
         base = layer * per_layer
-        late = base + lag
-        queue.add(2 if layer == 0 else late + 1, 2, enter, layer)
+        queue.add(2 if layer == 0 else at(0, 11) + 1, 2, enter, layer)
         for part in range(3):
-            queue.add(late + part, 1.5, project, layer, base + part)
+            queue.add(at(layer, part), 1.5, project, layer, base + part)
         for w in range(windows):
-            queue.add(late + 2, 5, attend, layer, w)
-        queue.add(late + 3, 1.5, branch, layer, base + 3)
-        queue.add(late + 3, 1.5, second_norm, layer)
+            queue.add(at(layer, 2), 5, attend, layer, w)
+        queue.add(at(layer, 3), 1.5, branch, layer, base + 3)
+        queue.add(at(layer, 3), 1.5, second_norm, layer)
         for part in range(4):
-            queue.add(late + 4 + part, 3.5, widen, layer, base + 4 + part)
+            queue.add(at(layer, 4 + part), 3.5, widen, layer, base + 4 + part)
             if part < 3:
-                queue.add(late + 4 + part, 1, turn, layer, part)
+                queue.add(at(layer, 4 + part), 1, turn, layer, part)
         for part in range(4):
-            queue.add(late + 8 + part, 1.5, narrow, layer, base + 8 + part)
-        queue.add(late + 12, 4, turn, layer, 3)
-
-    last = total - 1 + lag
+            queue.add(at(layer, 8 + part), 1.5, narrow, layer, base + 8 + part)
+        queue.add(at(layer, 11) + 1, 4, turn, layer, 3)
+
+    last = gather.gone + 2
     state = types.SimpleNamespace(tick=0)
 
     def pump():
-        while len(loaded) < total and len(loaded) <= state.tick - whole_at:
+        while len(loaded) < total and gather.whole_at(len(loaded)) < state.tick:
             i = len(loaded)
             same = [j for j in range(i) if (chunks[j][0] == 3) == (chunks[i][0] == 3)]
             if len(same) > 1 and same[-2] not in used:
@@ -1423,7 +1477,9 @@
     for part in range(4):
         ey.await_part(part)
     for w in range(windows):
-        r.result[w] = r.y_in[r.backward_take[w]]
+        tile = r.y_in[r.backward_take[w]].astype(WHOLE)
+        r.total[w * WIN : (w + 1) * WIN, :] = tile[:WIN]
+    r.result[...] = r.total[0 : windows * WIN, :].astype(LOW)
     eg.finish(1)
     ex.finish(4)
     ey.finish(4)
@@ -1439,7 +1495,7 @@
     count = depths * 2 * peers
     width = x0.shape[-1]
     hidden = blocks[2].shape[-1]
-    tall = x0.shape[0]
+    tall = 2 * ROWS
     half = peers // 2
     chunks = []
     for layer in range(2):
@@ -1456,7 +1512,7 @@
     tiles = (2, ROWS, width)
     left = (2, peers, depths * unit, 512)
     outs = [shape((depths, 2, peers) + b.shape[1:], LOW) for _ in range(2) for b in blocks]
-    outs += [shape(tiles, LOW), shape(tiles, LOW)]
+    outs += [shape(tiles, LOW), shape(x0.shape, LOW)]
     outs += [shape(left, LOW)] * 3 + [shape((2, 4) + left[1:], LOW)]
     outs += [
         shape((2, tall, width), LOW),
@@ -1521,7 +1577,8 @@
     )(*blocks, small, x0, grads, tables, index, mask, *moves)
 
 
-SLOTS = 6
+SLOTS, Z_SLOTS, Z_WAIT = 6, 9, 3
+DEEP = {3: (1, 7), 7: (6, 13), 15: (14, 20)}
 
 
 class Reduce:
@@ -1549,7 +1606,7 @@
         )
 
     def deep(self, i, step):
-        slot = i % SLOTS
+        slot = i % Z_SLOTS
         return remote(
             self.z_out.at[slot, self.place.at_depth(step)],
             self.z_in.at[slot, step - 1],
@@ -1562,6 +1619,8 @@
         for way in range(2):
             for step in range(1, self.half + 1):
                 self.ring(i, step, way).wait_send()
+
+    def deep_sent(self, i):
         for step in range(1, self.place.depths):
             self.deep(i, step).wait_send()
 
@@ -1569,7 +1628,7 @@
         if i >= SLOTS:
             self.sent(i - SLOTS)
         slot = i % SLOTS
-        found = self.product(i, self.place.around(self.half)).astype(LOW)
+        found = self.product(self.plan[i], self.place.around(self.half)).astype(LOW)
         for way in range(2):
             self.half_send[slot, way] = found[: self.cut] if way == 0 else found[self.cut :]
             self.ring(i, 1, way).start()
@@ -1579,7 +1638,7 @@
         cut = self.cut
         for way in range(2):
             turn = 1 if way == 0 else -1
-            found = self.product(i, self.place.around(turn * (self.half - step + 1)))
+            found = self.product(self.plan[i], self.place.around(turn * (self.half - step + 1)))
             self.ring(i, step - 1, way).wait_recv()
             target = self.full_send.at[slot, step - 2, way]
             if step == 2:
@@ -1595,66 +1654,157 @@
 
     def plane(self, i):
         slot, rows = i % SLOTS, self.rows
-        found = self.product(i, self.place.peer)
+        z_slot = i % Z_SLOTS
+        if i >= Z_SLOTS:
+            self.deep_sent(i - Z_SLOTS)
+        found = self.product(self.plan[i], self.place.peer)
         for way in range(2):
             self.ring(i, self.half, way).wait_recv()
             found += self.full_recv[slot, self.half - 2, way].astype(WHOLE)
         for depth in range(self.place.depths):
             piece = found[depth * rows : (depth + 1) * rows]
-            self.z_out[slot, depth] = piece.astype(LOW)
+            self.z_out[z_slot, depth] = piece.astype(LOW)
 
             @pl.when(depth == self.place.depth)
             def _():
-                self.own_part[slot] = piece
+                self.own_part[z_slot] = piece
 
         for step in range(1, self.place.depths):
             self.deep(i, step).start()
 
     def finish(self, i):
-        slot = i % SLOTS
+        slot = i % Z_SLOTS
         found = self.own_part[slot]
         for step in range(1, self.place.depths):
             self.deep(i, step).wait_recv()
             found += self.z_in[slot, step - 1].astype(WHOLE)
-        self.keep(i, found)
-
-
-B_IN = (
-    "f0", "f1", "f2", "f3", "f4", "f5", "f6", "f7", "moved_grad", "left0", "left1", "left2", "left3", "low_x",
-    "middle", "qkv", "probs", "slope", "vec32", "index", "backward_send", "backward_take",
-)
-B_OUT = (
-    "patches_grad", "g_qkv", "g_proj", "g_up", "g_down", "small_all", "own",
-)
-B_SCRATCH = (
-    "half_send", "half_recv", "full_send", "full_recv", "z_out", "z_in", "own_part", "left_a", "left_b",
-    "right0", "right1", "right2", "right3", "wide_a", "wide_b", "slope_s", "p_s", "q_s", "mid", "x", "grad",
-    "att_grad", "total", "g_mid", "score_sum", "tiles", "e_out", "e_in", "small_mine", "small_in",
-    "small_sum", "r_send", "r_recv", "z_send", "z_recv", "swap_send", "swap_recv", "credit", "load", "state",
-    "e_send", "e_recv", "a_send", "a_recv", "a_own", "b_send", "b_recv", "b_own",
-)
+        self.keep(self.plan[i], found)
+
+
 SMALL_ROWS = 96
 
 
-def backward_kernel(plan, depths, peers, *refs):
-    r = names(B_IN + B_OUT + B_SCRATCH, refs)
+class DeepFirst:
+    def __init__(self, reduce, bufs, sems):
+        self.reduce, self.place = reduce, reduce.place
+        (self.out, self.into, self.kept, self.half_send, self.half_recv, self.full_send, self.full_recv) = bufs
+        self.z_send, self.z_recv, self.r_send, self.r_recv = sems
+        self.rows = self.kept.shape[2]
+        self.cut = self.rows // 2
+
+    def deep(self, k, step):
+        return remote(
+            self.out.at[k, self.place.at_depth(step)],
+            self.into.at[k, step - 1],
+            self.z_send.at[k, step - 1],
+            self.z_recv.at[k, step - 1],
+            self.place.deep(step),
+        )
+
+    def ring(self, k, step, way):
+        if step == 1:
+            source, target = self.half_send.at[k, way], self.half_recv.at[k, way]
+        else:
+            source = self.full_send.at[k, step - 2, way]
+            target = self.full_recv.at[k, step - 2, way]
+        return remote(
+            source,
+            target,
+            self.r_send.at[k, step - 1, way],
+            self.r_recv.at[k, step - 1, way],
+            self.place.neighbour(1 if way == 0 else -1),
+        )
+
+    def start(self, k, entry):
+        rows = self.rows
+        for peer in range(self.place.peers):
+            found = self.reduce.product(entry, peer)
+            for depth in range(self.place.depths):
+                piece = found[depth * rows : (depth + 1) * rows]
+                self.out[k, depth, peer * rows : (peer + 1) * rows] = piece.astype(LOW)
+
+                @pl.when(depth == self.place.depth)
+                def _():
+                    self.kept[k, peer] = piece
+
+    def turn(self, k):
+        place, rows = self.place, self.rows
+        for step in range(1, place.depths):
+            self.deep(k, step).wait_recv()
+        for peer in range(place.peers):
+            found = self.kept[k, peer]
+            for step in range(1, place.depths):
+                found += self.into[k, step - 1, peer * rows : (peer + 1) * rows].astype(WHOLE)
+            self.kept[k, peer] = found
+        found = self.kept[k, place.around(place.half)].astype(LOW)
+        for way in range(2):
+            self.half_send[k, way] = found[: self.cut] if way == 0 else found[self.cut :]
+            self.ring(k, 1, way).start()
+
+    def next_step(self, k, step):
+        place, cut = self.place, self.cut
+        for way in range(2):
+            turn = 1 if way == 0 else -1
+            found = self.kept[k, place.around(turn * (place.half - step + 1))]
+            self.ring(k, step - 1, way).wait_recv()
+            if step == 2:
+                came = self.half_recv[k, way].astype(WHOLE)
+                low = found[:cut] + came if way == 0 else found[:cut]
+                high = found[cut:] if way == 0 else found[cut:] + came
+                found = jnp.concatenate([low, high], axis=0)
+            else:
+                found += self.full_recv[k, step - 3, way].astype(WHOLE)
+            self.full_send[k, step - 2, way] = found.astype(LOW)
+            self.ring(k, step, way).start()
+
+    def finish(self, k, entry):
+        place = self.place
+        found = self.kept[k, place.peer]
+        for way in range(2):
+            self.ring(k, place.half, way).wait_recv()
+            found += self.full_recv[k, place.half - 2, way].astype(WHOLE)
+        self.reduce.keep(entry, found)
+
+    def sent(self, k):
+        for way in range(2):
+            for step in range(1, self.place.half + 1):
+                self.ring(k, step, way).wait_send()
+        for step in range(1, self.place.depths):
+            self.deep(k, step).wait_send()
+
+
+def backward_kernel(everything, depths, peers, *refs):
+    r = types.SimpleNamespace()
+    (
+        r.f0, r.f1, r.f2, r.f3, r.f4, r.f5, r.f6, r.f7, r.moved_grad, r.left0, r.left1, r.left2, r.left3,
+        r.low_x, r.middle, r.qkv, r.probs, r.slope, r.vec32, r.index, r.backward_send, r.backward_take,
+        r.patches_grad, r.g_qkv, r.g_proj, r.g_up, r.g_down, r.o_gain, r.o_shift, r.o_qv, r.o_proj, r.o_up, r.o_down, r.o_table, r.small_all, r.half_send, r.half_recv,
+        r.full_send, r.full_recv, r.z_out, r.z_in, r.own_part, r.left_a, r.left_b, r.right0, r.right1,
+        r.right2, r.right3, r.wide_a, r.wide_b, r.slope_s, r.p_s, r.q_s, r.mid, r.x, r.grad, r.att_grad,
+        r.total, r.g_mid, r.score_sum, r.tiles, r.e_out, r.e_in, r.small_mine, r.small_in, r.small_sum,
+        r.r_send, r.r_recv, r.z_send, r.z_recv, r.swap_send, r.swap_recv, r.credit, r.load, r.state, r.e_send,
+        r.e_recv, r.a_send, r.a_recv, r.a_own, r.b_send, r.b_recv, r.b_own,
+        r.d_out, r.d_in, r.d_kept, r.d_half_send, r.d_half_recv, r.d_full_send, r.d_full_recv,
+        r.dz_send, r.dz_recv, r.dr_send, r.dr_recv,
+    ) = refs
     place = Place(depths, peers)
     fulls = (r.f0, r.f1, r.f2, r.f3, r.f4, r.f5, r.f6, r.f7)
     rights = (r.right0, r.right1, r.right2, r.right3)
     outs = (r.g_qkv, r.g_proj, r.g_up, r.g_down)
     windows, tall = 2, 2 * ROWS
+    plan = [entry for i, entry in enumerate(everything) if i not in DEEP]
     total = len(plan)
     queue = Queue(B_BUDGET)
     done, used, loaded = set(), set(), []
     unit = r.z_out.shape[2]
 
-    def product(i, peer):
-        layer, array, part, start = plan[i]
+    def product(entry, peer):
+        layer, array, part, start = entry
         left = r.left_b[layer, part, peer] if array == 3 else r.left_a[layer, array, peer]
         return dot(left, rights[array][:, start : start + WIDE])
 
-    def keep(i, found):
-        layer, array, part, start = plan[i]
+    def keep(entry, found):
+        layer, array, part, start = entry
         outs[array][layer, part * unit : (part + 1) * unit, start : start + WIDE] = found
 
     reduce = Reduce(
@@ -1664,6 +1814,11 @@
         keep,
         (r.half_send, r.half_recv, r.full_send, r.full_recv, r.z_out, r.z_in, r.own_part),
         (r.r_send, r.r_recv, r.z_send, r.z_recv),
+    )
+    deep_first = DeepFirst(
+        reduce,
+        (r.d_out, r.d_in, r.d_kept, r.d_half_send, r.d_half_recv, r.d_full_send, r.d_full_recv),
+        (r.dz_send, r.dz_recv, r.dr_send, r.dr_recv),
     )
     exchange = Exchange(place, r.e_out, r.e_in, r.e_send, r.e_recv, 1)
 
@@ -1731,13 +1886,11 @@
         ones = jnp.ones((8, tall), LOW)
         put(layer, row, dot(ones, value)[:1])
 
-    states = (("slope_s", "slope"), ("p_s", "probs"), ("q_s", "qkv"), ("mid", "middle"), ("x", "low_x"))
+    states = ((r.slope_s, r.slope), (r.p_s, r.probs), (r.q_s, r.qkv), (r.mid, r.middle), (r.x, r.low_x))
 
     def state_copy(layer, k):
         here, there = states[k]
-        return pltpu.make_async_copy(
-            getattr(r, there).at[layer], getattr(r, here), r.state.at[layer, k]
-        )
+        return pltpu.make_async_copy(there.at[layer], here, r.state.at[layer, k])
 
     def left_copies(layer):
         sources = (r.left0, r.left1, r.left2)
@@ -1861,10 +2014,10 @@
                 weighed = probs * prob_grad[:, one]
                 pieces.append(weighed - probs * jnp.sum(weighed, axis=1, keepdims=True))
             score_grad = jnp.concatenate(pieces, axis=1).astype(LOW)
-            if w == 0:
-                r.score_sum[g] = score_grad.astype(WHOLE)
-            else:
-                r.score_sum[g] += score_grad.astype(WHOLE)
+            for head in range(GROUP):
+                lines = pl.ds(pl.multiple_of((head * 8 + g) * ROWS, 8), ROWS)
+                one = score_grad[:, head * KEYS : (head + 1) * KEYS].astype(WHOLE)
+                r.score_sum[lines, :] = one if w == 0 else r.score_sum[lines, :] + one
             by_query = dot(score_grad, per_head(k)) * SCALE
             by_key = fold(dot(score_grad, q, (0, 0))) * SCALE
             by_value = fold(dot(low, out_grad, (0, 0)))
@@ -1905,17 +2058,19 @@
         buckets = lax.broadcasted_iota(jnp.int32, (384, KEYS), 0)
 
         def step(i, found):
-            line = r.index[pl.ds(i, 1), :]
-            hot = jnp.where(buckets == line, 1.0, 0.0).astype(LOW)
-            value = r.score_sum[:, pl.ds(i, 1), :].reshape(8, GROUP * KEYS)
-            value = jnp.concatenate(
-                [value[:, head * KEYS : (head + 1) * KEYS] for head in range(GROUP)], axis=0
-            )
+            start = pl.multiple_of(i * 8, 8)
+            lines = r.index[pl.ds(start, 8), :]
+            values, hots = [], []
+            for row in range(8):
+                hots.append(jnp.where(buckets == lines[row : row + 1], 1.0, 0.0).astype(LOW))
+                values.append(r.score_sum[pl.ds(start + row, HEADS, stride=ROWS), :])
+            value = jnp.concatenate(values, axis=1)
             high = value.astype(LOW)
             rest = (value - high.astype(WHOLE)).astype(LOW)
-            return found + dot(jnp.concatenate([high, rest], axis=0), hot, (1, 1))
-
-        found = lax.fori_loop(0, 100, step, jnp.zeros((64, 384), WHOLE))
+            both = jnp.concatenate([high, rest], axis=0)
+            return found + dot(both, jnp.concatenate(hots, axis=1), (1, 1))
+
+        found = lax.fori_loop(0, 13, step, jnp.zeros((64, 384), WHOLE))
         found = found[:32] + found[32:]
         base = 2 * SMALL_ROWS + layer * SMALL_ROWS
         for k in range(3):
@@ -1952,13 +2107,35 @@
         spread.start()
 
     def own_vectors():
-        starts = ((0, 4), (8, 4), (16, 4), (24, 4), (32, 2), (48, 4), (56, 1), (88, 4))
+        places = (
+            (0, 4, r.o_gain, 0),
+            (8, 4, r.o_gain, 1),
+            (16, 4, r.o_shift, 0),
+            (24, 4, r.o_shift, 1),
+            (32, 2, r.o_qv, None),
+            (48, 4, r.o_proj, None),
+            (56, 1, r.o_up, None),
+            (88, 4, r.o_down, None),
+        )
         for layer in range(2):
-            for k, (row, each) in enumerate(starts):
+            for row, each, target, k in places:
                 line = layer * SMALL_ROWS + row + lax.div(place.index, each)
                 found = r.small_all[lax.div(line, 16), pl.ds(lax.rem(line, 16), 1), :]
                 back = lax.rem(each - lax.rem(place.index, each), each) * (128 // each)
-                r.own[8 * layer + k : 8 * layer + k + 1, :] = pltpu.roll(found, back, 1)
+                found = pltpu.roll(found, back, 1)[:, : 128 // each]
+                if k is None:
+                    target[layer : layer + 1, :] = found
+                else:
+                    target[layer, k : k + 1, :] = found
+            first = (2 + layer) * SMALL_ROWS // 16
+            parts = [
+                r.small_all[first + 2 * k : first + 2 * k + 2].reshape(HEADS, 128) for k in range(3)
+            ]
+            rows = jnp.concatenate(parts, axis=1)
+            order = [rows[h % GROUP * 8 + h // GROUP :][:1] for h in range(HEADS)]
+            order.append(jnp.zeros((128 - HEADS, 384), WHOLE))
+            turned = jnp.concatenate(order, axis=0).T
+            r.o_table[layer] = turned[: r.o_table.shape[1], :HEADS]
 
     def note(work, *what):
         work(*what)
@@ -2006,8 +2183,8 @@
 
     needs = {3: ("take_grad",), 2: ("hidden_grad",), 1: ("middle_grad",), 0: ("attend_back",)}
 
-    def wanted(i):
-        layer, array, part, start = plan[i]
+    def wanted(entry):
+        layer, array, part, start = entry
         what = needs[array] + (layer,)
         if array == 2:
             what += (start // 1024,)
@@ -2017,20 +2194,40 @@
 
     received, lefts_in = set(), set()
     half = place.half
-    for tick in range(total + GAP * (half + 1)):
+
+    def prepare(entry):
+        layer, array, part, start = entry
+        while wanted(entry) not in done:
+            queue.step(pump)
+        if layer not in lefts_in:
+            lefts_in.add(layer)
+            for copy in left_copies(layer):
+                copy.wait()
+        key = (layer, array, start // 1024)
+        if key not in received:
+            received.add(key)
+            swap(*key).wait_recv()
+
+    for tick in range(total + GAP * half + Z_WAIT):
         if tick < total:
-            layer, array, part, start = plan[tick]
-            while wanted(tick) not in done:
-                queue.step(pump)
-            if layer not in lefts_in:
-                lefts_in.add(layer)
-                for copy in left_copies(layer):
-                    copy.wait()
-            key = (layer, array, start // 1024)
-            if key not in received:
-                received.add(key)
-                swap(*key).wait_recv()
+            prepare(plan[tick])
             reduce.first(tick)
+        for k, (i, (begin, middle)) in enumerate(DEEP.items()):
+            assert place.depths == 4 and half == 2
+            entry, slot = everything[i], k % 2
+            if tick == begin:
+                prepare(entry)
+                if k >= 2:
+                    deep_first.sent(slot)
+                deep_first.start(slot, entry)
+            if tick in (begin, begin + 2, begin + 4):
+                deep_first.deep(slot, (tick - begin) // 2 + 1).start()
+            if tick == middle:
+                deep_first.turn(slot)
+            if tick == middle + 3:
+                deep_first.next_step(slot, 2)
+            if tick == middle + 6:
+                deep_first.finish(slot, entry)
         for step in range(2, half + 1):
             i = tick - GAP * (step - 1)
             if 0 <= i < total:
@@ -2042,7 +2239,7 @@
                 if i == last:
                     free(array)
                     done.add((array, "freed"))
-        i = tick - GAP * (half + 1)
+        i = tick - GAP * half - Z_WAIT
         if 0 <= i < total:
             reduce.finish(i)
         queue.run(tick, pump)
@@ -2059,9 +2256,13 @@
             swap(0, array, part).wait_send()
     for i in range(total - SLOTS, total):
         reduce.sent(i)
-
-
-def backward_all(fulls, state, index, moves, depths, peers):
+    for i in range(total - Z_SLOTS, total):
+        reduce.deep_sent(i)
+    for k in range(2):
+        deep_first.sent(k)
+
+
+def backward_all(fulls, state, index, moves, depths, peers, buckets):
     moved_grad, left0, left1, left2, left3, low_x, middle, qkv, probs, slope, vec32 = state
     count = depths * 2 * peers
     tall, width = low_x.shape[1:]
@@ -2085,17 +2286,23 @@
         shape((2, unit, width), WHOLE),
         shape((2, unit, hidden), WHOLE),
         shape((2, 4 * unit, width), WHOLE),
-        shape((count, 16, 128), WHOLE),
-        shape((16, 128), WHOLE),
+        shape((2, 2, unit), WHOLE),
+        shape((2, 2, unit), WHOLE),
+        shape((2, 2 * unit), WHOLE),
+        shape((2, unit), WHOLE),
+        shape((2, 4 * unit), WHOLE),
+        shape((2, unit), WHOLE),
+        shape((2, buckets, HEADS), WHOLE),
     ]
     scratch = [
+        vmem((count, 16, 128), WHOLE),
         vmem((SLOTS, 2, flat // 2, WIDE), LOW),
         vmem((SLOTS, 2, flat // 2, WIDE), LOW),
         vmem((SLOTS, half - 1, 2, flat, WIDE), LOW),
         vmem((SLOTS, half - 1, 2, flat, WIDE), LOW),
-        vmem((SLOTS, depths, unit, WIDE), LOW),
-        vmem((SLOTS, depths - 1, unit, WIDE), LOW),
-        vmem((SLOTS, unit, WIDE), WHOLE),
+        vmem((Z_SLOTS, depths, unit, WIDE), LOW),
+        vmem((Z_SLOTS, depths - 1, unit, WIDE), LOW),
+        vmem((Z_SLOTS, unit, WIDE), WHOLE),
         vmem((2, 3) + left0.shape[1:], LOW),
         vmem(left3.shape, LOW),
         vmem((512, 3 * width), LOW),
@@ -2113,7 +2320,7 @@
         vmem((tall, width), LOW),
         vmem((tall, width), WHOLE),
         vmem((tall, width), WHOLE),
-        vmem((8, ROWS, GROUP * KEYS), WHOLE),
+        vmem((HEADS * ROWS, KEYS), WHOLE),
         vmem((2, ROWS, width), LOW),
         vmem((peers, ROWS, width), LOW),
         vmem((peers, ROWS, width), LOW),
@@ -2122,8 +2329,8 @@
         vmem((16, 128), WHOLE),
         dma((SLOTS, half, 2)),
         dma((SLOTS, half, 2)),
-        dma((SLOTS, depths - 1)),
-        dma((SLOTS, depths - 1)),
+        dma((Z_SLOTS, depths - 1)),
+        dma((Z_SLOTS, depths - 1)),
         dma((4, 4)),
         dma((4, 4)),
         pltpu.SemaphoreType.REGULAR((4,)),
@@ -2132,17 +2339,58 @@
         dma((1, peers - 1)),
         dma((1, peers - 1)),
         *[dma(())] * 6,
+        vmem((2, depths, peers * unit, WIDE), LOW),
+        vmem((2, depths - 1, peers * unit, WIDE), LOW),
+        vmem((2, peers, unit, WIDE), WHOLE),
+        vmem((2, 2, unit // 2, WIDE), LOW),
+        vmem((2, 2, unit // 2, WIDE), LOW),
+        vmem((2, half - 1, 2, unit, WIDE), LOW),
+        vmem((2, half - 1, 2, unit, WIDE), LOW),
+        dma((2, depths - 1)),
+        dma((2, depths - 1)),
+        dma((2, half, 2)),
+        dma((2, half, 2)),
     ]
     return pl.pallas_call(
         functools.partial(backward_kernel, plan, depths, peers),
         out_shape=outs,
         in_specs=[ANY] * 8 + [VMEM] + [ANY] * 9 + [VMEM] * 2 + [smem] * 2,
-        out_specs=[VMEM] * 7,
+        out_specs=[VMEM] * 12,
         scratch_shapes=scratch,
         compiler_params=pltpu.CompilerParams(
             collective_id=4, has_side_effects=True, vmem_limit_bytes=63 * 2**20
         ),
     )(*fulls, *state, index, *moves)
+
+
+def copy_kernel(count, *refs):
+    sources, targets, held = refs[:count], refs[count : 2 * count], refs[2 * count : 3 * count]
+    came, went = refs[3 * count :]
+    loads = [pltpu.make_async_copy(sources[k], held[k], came.at[k]) for k in range(count)]
+    stores = [pltpu.make_async_copy(held[k], targets[k], went.at[k]) for k in range(count)]
+    for copy in loads:
+        copy.start()
+    for load, store in zip(loads, stores):
+        load.wait()
+        store.start()
+    for copy in stores:
+        copy.wait()
+
+
+def copy_out(arrays):
+    count = len(arrays)
+    return pl.pallas_call(
+        functools.partial(copy_kernel, count),
+        out_shape=[jax.ShapeDtypeStruct(a.shape, a.dtype) for a in arrays],
+        in_specs=[ANY] * count,
+        out_specs=[ANY] * count,
+        scratch_shapes=[
+            *[pltpu.VMEM(a.shape, a.dtype) for a in arrays],
+            pltpu.SemaphoreType.DMA((count,)),
+            pltpu.SemaphoreType.DMA((count,)),
+        ],
+        compiler_params=pltpu.CompilerParams(vmem_limit_bytes=63 * 2**20),
+    )(*arrays)
 
 
 def whole_shards(
@@ -2214,14 +2462,11 @@
         axis=0,
     ).astype(jnp.float32)
 
-    def padded(rows):
-        return jnp.pad(rows.reshape(windows, WIN, width), ((0, 0), (0, ROWS - WIN), (0, 0)))
-
     found = forward_all(
         (qkv_weight, proj_weight, up_weight, down_weight),
         small,
-        padded(patches).reshape(windows * ROWS, width),
-        padded(out_grad),
+        patches,
+        out_grad,
         tables,
         index,
         mask,
@@ -2230,23 +2475,24 @@
         peer_count,
     )
     fulls, moved_grad, result, state = found[:8], found[8], found[9], found[10:]
-    grad_patches, grad_qkv, grad_proj, grad_up, grad_down, small_all, own = backward_all(
-        fulls, (moved_grad, *state), index, moves[2:], depths, peer_count
-    )
-
-    def trimmed(rows):
-        return rows.reshape(windows, ROWS, width)[:, :WIN].reshape(windows * WIN, width)
-
-    flat = small_all.reshape(-1)
-    per_layer = SMALL_ROWS * 128
-    own = own.reshape(2, 8, 128)
-    gain_grad, shift_grad = own[:, 0:2, :each], own[:, 2:4, :each]
-    qv_grad, proj_b_grad = own[:, 4, : 2 * each], own[:, 5, :each]
-    up_b_grad, down_b_grad = own[:, 6], own[:, 7, :each]
-    table = flat[2 * per_layer : 4 * per_layer].reshape(2, 3, GROUP, HEADS // GROUP, 128)
-    table = table.transpose(0, 1, 4, 3, 2).reshape(2, 3 * 128, HEADS)[:, : rel_table.shape[1]]
-    return (
-        trimmed(result),
+    (
+        grad_patches,
+        grad_qkv,
+        grad_proj,
+        grad_up,
+        grad_down,
+        gain_grad,
+        shift_grad,
+        qv_grad,
+        proj_b_grad,
+        up_b_grad,
+        down_b_grad,
+        table,
+    ) = backward_all(
+        fulls, (moved_grad, *state), index, moves[2:], depths, peer_count, rel_table.shape[1]
+    )
+    results = (
+        result,
         grad_patches,
         gain_grad,
         shift_grad,
@@ -2260,6 +2506,7 @@
         grad_down,
         down_b_grad,
     )
+    return tuple(copy_out(results))
 
 
 def solution(mesh):

time: 541 us -> 495 us (0.915)
  Pallas kernels: 501 us -> 474 us
  local copies, waits for them, and re-layouts: 27.1 us -> 8.38 us
    pallas_call x1, Pallas kernels: 243 us -> 227 us  [backward_all(): pl.pallas_call(functools.partial(backward_kernel, plan, depths, peers), o...]
    pallas_call x1, Pallas kernels: 258 us -> 243 us  [forward_all(): pl.pallas_call(functools.partial(forward_kernel, chunks, depths, peers),...]
    unnamed x13 -> x4, local copies, waits for them, and re-layouts: 7.81 us -> 0.01 us
    slice x6 -> x0, local copies, waits for them, and re-layouts: 7.3 us -> none  [the longest x2 2.6 us: whole_shards(): up_b_grad, down_b_grad = (own[:, 6], own[:, 7, :each])]
where the time goes in v3:
time: 495 us; the launch traced here: 488 us
  Pallas kernels  474 us (96%)
  local copies, waits for them, and re-layouts  8.38 us (2%)
    pallas_call x1, Pallas kernels, forward_all(): pl.pallas_call(functools.partial(forward_kernel, chunks, depths, peers),...  243 us
    pallas_call x1, Pallas kernels, backward_all(): pl.pallas_call(functools.partial(backward_kernel, plan, depths, peers), o...  227 us

profile of v3, /device:TPU:0, one launch (start us, length us, event | category | flops | bytes accessed | tf_op | source)
XLA Modules:
  0.0 488.1 jit_solution(7502937504848275033)
XLA Ops:
  0.7 0.8 reshape.293
  1.4 0.8 reshape.294
  2.2 0.7 reshape.296
  2.9 0.8 select_reduce_fusion.2
  3.8 0.8 select_reduce_fusion.1
  4.6 0.1 select_reduce_fusion
  4.7 0.2 select_reduce_fusion.4
  4.9 0.0 copy-start
  5.0 0.0 copy-start.1
  5.0 0.6 fusion.1.refs_12_.refs_20_
  5.6 0.6 fusion.refs_10_
  6.2 0.7 pad_maximum_fusion
  6.8 0.1 reshape.295
  6.9 0.7 concatenate.7
  7.6 0.1 multiply_add_fusion
  7.7 0.6 convert_element_type.21.refs_4_
  8.3 0.8 reshape.297
  9.1 0.6 pad.12.refs_7_
  9.8 1.4 pad.13.refs_8_.refs_19_
  11.2 0.1 compare_select_fusion
  11.3 0.7 pad.14.refs_9_
  12.0 0.0 copy-done
  12.0 0.0 copy-done.1
  12.0 242.9 %shard_map.264 = (bf16[4,2,4,32,3072]{4,3,2,1,0:T(8,128)(2,1)}, bf16[4,2,4,32,1024]{4,3,2,1,0:T(8,128)(2,1)}, bf16[4,2,4,32,4096]{4,3,2,1,0:T(8,128)(2,1)}, bf16...) custom-call(bf16[2,32,3072]{2,1,0:T(8,128)(2,1)} %refs_0_.1, ...), custom_call_target="tpu_custom_call" | custom-call | tf_op jit(solution)/shard_map/pallas_call | solution.py:1568
  254.9 226.8 %shard_map.265 = (f32[200,1024]{1,0:T(8,128)}, f32[2,32,3072]{2,1,0:T(8,128)}, f32[2,32,1024]{2,1,0:T(8,128)}, f32[2,32,4096]{2,1,0:T(8,128)}, f32[2,128,1024]{2...) custom-call(bf16[4,2,4,32,3072]{4,3,2,1,0:T(8,128)(2,1)} %get-tuple-, ...), custom_call_target="tpu_custom_call" | custom-call | tf_op jit(solution)/shard_map/pallas_call | solution.py:2354
  481.7 4.5 shard_map.266
  486.2 1.8 copy.33
  (6 shorter events, 0.1 us)
Async XLA Ops:
  4.9 7.0 %copy-start = (s32[2]{0:T(128)}, s32[2]{0:T(128)S(1)}, u32[]{:S(2)}) copy-start(s32[2]{0:T(128)S(1)} %get-tuple-element.111.refs_13_.refs_21_) | copy-start | bytes 28
  5.0 7.0 %copy-start.1 = (s32[2]{0:T(128)}, s32[2]{0:T(128)S(1)}, u32[]{:S(2)}) copy-start(s32[2]{0:T(128)S(1)} %get-tuple-element.110.refs_11_) | copy-start | bytes 28

commit v4 on v3

--- a/solution.py
+++ b/solution.py
@@ -904,7 +904,7 @@
 
 ROWS = 112
 GAP, F_GAP = 2, 1
-EARLY = {12: 1, 20: 9}
+EARLY = {11: 1, 17: 6, 22: 10}
 F_BUDGET, B_BUDGET = 5.0, 5.0
 KEYS = 128
 GROUP = 4
@@ -1008,17 +1008,17 @@
 class Gather:
     def __init__(self, place, chunks, early, blocks, fulls, sems):
         self.place, self.chunks, self.blocks, self.fulls = place, chunks, blocks, fulls
-        (self.z_send, self.z_recv, self.r_send, self.r_recv, self.c_send, self.c_recv, self.own_sem) = sems
+        (self.z_send, self.z_recv, self.r_send, self.r_recv, self.c_send, self.c_recv, self.own_sem, self.relay_send) = sems
         self.half, self.cut = place.half, place.depths // 2
         self.early = early
         self.late = [i for i in range(len(chunks)) if i not in early]
         self.begun = 0
         self.gone = len(self.late) - 1 + F_GAP * self.half
-        assert place.depths == 2 * self.half
+        assert place.depths == 2 * self.half == 4
 
     def whole_at(self, i):
         if i in self.early:
-            return max(self.whole_at(i - 1), self.early[i] + 2 * self.half + 2 * self.place.depths - 1)
+            return max(self.whole_at(i - 1), self.early[i] + 2 * self.half + 8)
         return self.late.index(i) + F_GAP * self.half
 
     def full(self, i):
@@ -1054,6 +1054,35 @@
             self.z_recv.at[i, step - 1],
             place.deep(step),
         )
+
+    def unless_far(self, i, step, work):
+        place = self.place
+        far = {1: place.depths - 1, place.depths - 1: 0}
+        if i in self.early and step in far:
+            pl.when(place.depth != far[step])(work)
+        else:
+            work()
+
+    def relay(self, i):
+        place = self.place
+        end = 3 * (place.depth - 1)
+        here = self.plane(i, 3 - end)
+        return remote(
+            here,
+            here,
+            self.relay_send.at[i],
+            self.z_recv.at[i, 2 * (place.depth - 1)],
+            (end * 2 + place.core, place.peer),
+        )
+
+    def if_between(self, work):
+        depth = self.place.depth
+        pl.when(jnp.logical_and(depth > 0, depth < self.place.depths - 1))(work)
+
+    def pass_on(self, i):
+        self.deep(i, 2).wait_recv()
+        self.if_between(lambda: self.relay(i).start())
+        self.across(i, 2).start()
 
     def ring(self, i, step, way):
         place = self.place
@@ -1122,7 +1151,7 @@
             self.across(i, 2 * step - 1).start()
 
     def spread_planes(self, i):
-        for step in range(1, self.place.depths):
+        for step in (1, 3):
             self.deep(i, step).wait_recv()
             self.across(i, step).start()
 
@@ -1136,7 +1165,10 @@
             if 1 <= step <= self.half and not odd:
                 self.later(i, step)
             if 0 <= step - self.half < self.place.depths - 1 and not odd:
-                self.deep(i, step - self.half + 1).start()
+                deep = (2, 1, 3)[step - self.half]
+                self.unless_far(i, deep, self.deep(i, deep).start)
+            if tick == start + 2 * self.half + 3:
+                self.pass_on(i)
             if tick == self.whole_at(i):
                 self.spread_planes(i)
         while self.begun < min(len(late), tick + 1 + min(2 + (tick + 1) // 2, 6)):
@@ -1157,7 +1189,9 @@
             for slot in range(2 * self.half):
                 self.across(i, slot).wait_send()
             for step in range(1, self.place.depths):
-                self.deep(i, step).wait_send()
+                self.unless_far(i, step, self.deep(i, step).wait_send)
+            if i in self.early:
+                self.if_between(lambda i=i: self.relay(i).wait_send())
             for step in range(1, self.half + 1):
                 for way in range(2):
                     self.ring(i, step, way).wait_send()
@@ -1166,13 +1200,13 @@
 def forward_kernel(chunks, depths, peers, *refs):
     r = types.SimpleNamespace()
     (
-        r.w0, r.w1, r.w2, r.w3, r.small, r.x0, r.grads, r.tables, r.index, r.mask, r.forward_send,
+        r.w0, r.w1, r.w2, r.w3, r.gain, r.shift, r.qv, r.proj_b, r.up_b, r.down_b, r.x0, r.grads, r.table, r.bias_index, r.region, r.forward_send,
         r.forward_take, r.backward_send, r.backward_take, r.f0, r.f1, r.f2, r.f3, r.f4, r.f5, r.f6, r.f7,
         r.moved_grad, r.result, r.left0, r.left1, r.left2, r.left3, r.low_x, r.middle, r.qkv, r.probs,
-        r.slope, r.vec32, r.small_full, r.bias, r.x, r.x0w, r.normed, r.att, r.normed_two, r.act, r.mid,
-        r.q_s, r.p_s, r.slope_s, r.wide_a, r.wide_b, r.total, r.sib_a, r.sib_b, r.turned, r.left_a, r.left_b,
+        r.slope, r.vec32, r.small_full, r.small, r.tables, r.index, r.mask, r.bias, r.x, r.x0w, r.normed, r.att, r.normed_two, r.act, r.mid,
+        r.q_s, r.p_s, r.slope_s, r.wide_a, r.wide_b, r.total, r.sib_a, r.sib_b, r.turned, r.wide_t, r.left_a, r.left_b,
         r.g_out, r.g_in, r.x_out, r.x_in, r.y_out, r.y_in, r.vec64, r.vec128, r.z_send, r.z_recv, r.r_send,
-        r.r_recv, r.c_send, r.c_recv, r.own_sem, r.s_send, r.s_recv, r.s_own, r.load, r.save, r.swap_send,
+        r.r_recv, r.c_send, r.c_recv, r.own_sem, r.relay_send, r.s_send, r.s_recv, r.s_own, r.load, r.save, r.swap_send,
         r.swap_recv, r.eg_send, r.eg_recv, r.ex_send, r.ex_recv, r.ey_send, r.ey_recv,
     ) = refs
     place = Place(depths, peers)
@@ -1182,7 +1216,7 @@
         EARLY,
         (r.w0, r.w1, r.w2, r.w3),
         (r.f0, r.f1, r.f2, r.f3, r.f4, r.f5, r.f6, r.f7),
-        (r.z_send, r.z_recv, r.r_send, r.r_recv, r.c_send, r.c_recv, r.own_sem),
+        (r.z_send, r.z_recv, r.r_send, r.r_recv, r.c_send, r.c_recv, r.own_sem, r.relay_send),
     )
     spread = Spread(place, r.small, r.small_full, r.s_send, r.s_recv, r.s_own)
     eg = Exchange(place, r.g_out, r.g_in, r.eg_send, r.eg_recv, 1)
@@ -1252,6 +1286,44 @@
             r.vec128[member : member + 1, :] = jnp.concatenate(
                 [line[d : d + 1] for d in range(count)], axis=1
             )
+
+    def pack():
+        r.small[...] = jnp.zeros(r.small.shape, WHOLE)
+        gain, shift = r.gain[...].astype(WHOLE), r.shift[...].astype(WHOLE)
+        proj_b, down_b = r.proj_b[...].astype(WHOLE), r.down_b[...].astype(WHOLE)
+        qv, up_b = r.qv[...].astype(WHOLE), r.up_b[...].astype(WHOLE)
+        each = proj_b.shape[1]
+        for layer in range(2):
+            for k in range(2):
+                columns = slice((2 * layer + k) * each, (2 * layer + k + 1) * each)
+                r.small[0:1, columns] = gain[layer, k : k + 1]
+                r.small[1:2, columns] = shift[layer, k : k + 1]
+            r.small[2:3, layer * each : (layer + 1) * each] = proj_b[layer : layer + 1]
+            r.small[2:3, (2 + layer) * each : (3 + layer) * each] = down_b[layer : layer + 1]
+            r.small[3:4, 2 * layer * each : 2 * (layer + 1) * each] = qv[layer : layer + 1]
+            r.small[4 + layer : 5 + layer, :] = up_b[layer : layer + 1]
+
+    def make_tables():
+        count = r.table.shape[1]
+        r.index[...] = jnp.full(r.index.shape, count, jnp.int32)
+        r.index[:WIN, :WIN] = r.bias_index[...]
+        for layer in range(2):
+            r.wide_t[...] = jnp.full(r.wide_t.shape, NEVER, WHOLE)
+            r.wide_t[:count, :HEADS] = r.table[layer].astype(WHOLE)
+            turned = r.wide_t[...].T
+            order = [turned[k % 8 * GROUP + k // 8 :][:1] for k in range(HEADS)]
+            r.tables[layer * HEADS : (layer + 1) * HEADS, :] = jnp.concatenate(order, axis=0).astype(LOW)
+
+        def label(axis, region):
+            place = lax.broadcasted_iota(jnp.int32, (ROWS, KEYS), axis)
+            row = lax.shift_right_logical(place * 6554, 16)
+            right = jnp.where(place - 10 * row >= 5, 1, 0)
+            lower = jnp.where(row >= 5, 1, 0)
+            return lax.rem(region, 2) * right + 2 * lax.div(region, 2) * lower
+
+        for w in range(windows):
+            same = label(0, r.region[w]) == label(1, r.region[w])
+            r.mask[w] = jnp.where(same, 0.0, masked_score)
 
     def bias_rows(start, stop):
         buckets = lax.broadcasted_iota(jnp.int32, (384, KEYS), 0)
@@ -1419,10 +1491,10 @@
         else:
             spill(r.left_a.at[layer, array], (r.left0, r.left1, r.left2)[array].at[layer])
 
+    pack()
     place.greet()
-    for i in range(2):
-        gather.begin(gather.late[i])
-        gather.begun += 1
+    gather.begin(gather.late[0])
+    gather.begun = 1
     pad_windows(r.grads)
     for w in range(windows):
         r.x0w[w] = r.total[w * ROWS : (w + 1) * ROWS, :].astype(LOW)
@@ -1430,8 +1502,9 @@
     spread.start()
 
     def at(layer, part):
-        return gather.whole_at(layer * per_layer + part) + 2
-
+        return gather.whole_at(layer * per_layer + part) + 1
+
+    queue.add(0, 1, make_tables)
     queue.add(0, 5, bias_rows, 0, 7)
     queue.add(0, 5, bias_rows, 7, ROWS // 8)
     queue.add(2, 1, unpack)
@@ -1452,11 +1525,11 @@
             queue.add(at(layer, 8 + part), 1.5, narrow, layer, base + 8 + part)
         queue.add(at(layer, 11) + 1, 4, turn, layer, 3)
 
-    last = gather.gone + 2
+    last = gather.gone + 1
     state = types.SimpleNamespace(tick=0)
 
     def pump():
-        while len(loaded) < total and gather.whole_at(len(loaded)) < state.tick:
+        while len(loaded) < total and gather.whole_at(len(loaded)) <= state.tick:
             i = len(loaded)
             same = [j for j in range(i) if (chunks[j][0] == 3) == (chunks[i][0] == 3)]
             if len(same) > 1 and same[-2] not in used:
@@ -1491,7 +1564,7 @@
         copy.wait()
 
 
-def forward_all(blocks, small, x0, grads, tables, index, mask, moves, depths, peers):
+def forward_all(blocks, vectors, x0, grads, table, bias_index, region, moves, depths, peers):
     count = depths * 2 * peers
     width = x0.shape[-1]
     hidden = blocks[2].shape[-1]
@@ -1524,7 +1597,11 @@
     ]
     exchange = (peers,) + tiles[1:]
     scratch = [
-        vmem((count,) + small.shape, WHOLE),
+        vmem((count, 8, 128), WHOLE),
+        vmem((8, 128), WHOLE),
+        vmem((2 * HEADS, 384), LOW),
+        vmem((ROWS, KEYS), jnp.int32),
+        vmem((2, ROWS, KEYS), WHOLE),
         vmem((2, 8, ROWS, GROUP * KEYS), WHOLE),
         vmem((2, tall, width), LOW),
         vmem(tiles, LOW),
@@ -1542,6 +1619,7 @@
         vmem((3, 2, tall, width), LOW),
         vmem((2, tall, hidden), LOW),
         vmem((depths, 128, 512), WHOLE),
+        vmem((384, 128), WHOLE),
         vmem((2, 3) + left[1:], LOW),
         vmem((2, 4) + left[1:], LOW),
         *[vmem(exchange, LOW)] * 6,
@@ -1553,6 +1631,7 @@
         dma((total, half, 2)),
         dma((total, 2 * half)),
         dma((total, 2 * half)),
+        dma((total,)),
         dma((total,)),
         dma(()),
         dma(()),
@@ -1568,13 +1647,13 @@
     return pl.pallas_call(
         functools.partial(forward_kernel, chunks, depths, peers),
         out_shape=outs,
-        in_specs=[ANY] * 4 + [VMEM] * 6 + [smem] * 4,
+        in_specs=[ANY] * 4 + [VMEM] * 10 + [smem] * 5,
         out_specs=[ANY] * 8 + [VMEM] * 2 + [ANY] * 9 + [VMEM],
         scratch_shapes=scratch,
         compiler_params=pltpu.CompilerParams(
             collective_id=3, has_side_effects=True, vmem_limit_bytes=63 * 2**20
         ),
-    )(*blocks, small, x0, grads, tables, index, mask, *moves)
+    )(*blocks, *vectors, x0, grads, table, bias_index, region, *moves)
 
 
 SLOTS, Z_SLOTS, Z_WAIT = 6, 9, 3
@@ -1777,11 +1856,11 @@
     r = types.SimpleNamespace()
     (
         r.f0, r.f1, r.f2, r.f3, r.f4, r.f5, r.f6, r.f7, r.moved_grad, r.left0, r.left1, r.left2, r.left3,
-        r.low_x, r.middle, r.qkv, r.probs, r.slope, r.vec32, r.index, r.backward_send, r.backward_take,
+        r.low_x, r.middle, r.qkv, r.probs, r.slope, r.vec32, r.bias_index, r.backward_send, r.backward_take,
         r.patches_grad, r.g_qkv, r.g_proj, r.g_up, r.g_down, r.o_gain, r.o_shift, r.o_qv, r.o_proj, r.o_up, r.o_down, r.o_table, r.small_all, r.half_send, r.half_recv,
         r.full_send, r.full_recv, r.z_out, r.z_in, r.own_part, r.left_a, r.left_b, r.right0, r.right1,
         r.right2, r.right3, r.wide_a, r.wide_b, r.slope_s, r.p_s, r.q_s, r.mid, r.x, r.grad, r.att_grad,
-        r.total, r.g_mid, r.score_sum, r.tiles, r.e_out, r.e_in, r.small_mine, r.small_in, r.small_sum,
+        r.total, r.g_mid, r.score_sum, r.tiles, r.e_out, r.e_in, r.index, r.small_mine, r.small_in, r.small_sum,
         r.r_send, r.r_recv, r.z_send, r.z_recv, r.swap_send, r.swap_recv, r.credit, r.load, r.state, r.e_send,
         r.e_recv, r.a_send, r.a_recv, r.a_own, r.b_send, r.b_recv, r.b_own,
         r.d_out, r.d_in, r.d_kept, r.d_half_send, r.d_half_recv, r.d_full_send, r.d_full_recv,
@@ -2153,6 +2232,8 @@
         zero = jnp.zeros((256 - tall, right.shape[1]), LOW)
         right[tall:256, :] = zero
         right[256 + tall : 512, :] = zero
+    r.index[...] = jnp.full(r.index.shape, r.o_table.shape[1], jnp.int32)
+    r.index[:WIN, :WIN] = r.bias_index[...]
     r.small_mine[...] = jnp.zeros(r.small_mine.shape, WHOLE)
     pump()
     place.greet()
@@ -2324,6 +2405,7 @@
         vmem((2, ROWS, width), LOW),
         vmem((peers, ROWS, width), LOW),
         vmem((peers, ROWS, width), LOW),
+        vmem((ROWS, KEYS), jnp.int32),
         vmem((count * 16, 128), WHOLE),
         vmem((count, 16, 128), WHOLE),
         vmem((16, 128), WHOLE),
@@ -2440,36 +2522,15 @@
         return jnp.sum(jnp.where(peers[None, :] == spots[:, None], numbers[None, :], 0), axis=1)
 
     moves = (window_for(backward_take), forward_take, window_for(forward_take), backward_take)
-    mask = region_mask(look_up(region_slot, own_slots))[:, 0]
-    mask = jnp.pad(mask, ((0, 0), (0, ROWS - WIN), (0, KEYS - WIN)))
-    index = jnp.pad(
-        bias_index, ((0, ROWS - WIN), (0, KEYS - WIN)), constant_values=rel_table.shape[1]
-    )
-    tables = rel_table.reshape(2, -1, HEADS // GROUP, GROUP).transpose(0, 3, 2, 1)
-    tables = tables.reshape(2 * HEADS, -1)
-    tables = jnp.pad(tables, ((0, 0), (0, 384 - tables.shape[1])), constant_values=NEVER)
-
-    each = width // (outer_count * peer_count)
-    small = jnp.concatenate(
-        [
-            norm_gain.reshape(1, 4 * each),
-            norm_shift.reshape(1, 4 * each),
-            jnp.concatenate([proj_bias, down_bias], axis=0).reshape(1, 4 * each),
-            qv_bias.reshape(1, 4 * each),
-            up_bias,
-            jnp.zeros((2, 4 * each), LOW),
-        ],
-        axis=0,
-    ).astype(jnp.float32)
-
+    region = look_up(region_slot, own_slots)
     found = forward_all(
         (qkv_weight, proj_weight, up_weight, down_weight),
-        small,
+        (norm_gain, norm_shift, qv_bias, proj_bias, up_bias, down_bias),
         patches,
         out_grad,
-        tables,
-        index,
-        mask,
+        rel_table,
+        bias_index,
+        region,
         moves,
         depths,
         peer_count,
@@ -2489,7 +2550,7 @@
         down_b_grad,
         table,
     ) = backward_all(
-        fulls, (moved_grad, *state), index, moves[2:], depths, peer_count, rel_table.shape[1]
+        fulls, (moved_grad, *state), bias_index, moves[2:], depths, peer_count, rel_table.shape[1]
     )
     results = (
         result,

time: 495 us -> 484 us (0.978)
  Pallas kernels: 474 us -> 469 us
  local copies, waits for them, and re-layouts: 8.38 us -> 3.39 us
where the time goes in v4:
time: 484 us; the launch traced here: 477 us
  Pallas kernels  469 us (97%)
    pallas_call x1, Pallas kernels, forward_all(): pl.pallas_call(functools.partial(forward_kernel, chunks, depths, peers),...  239 us
    pallas_call x1, Pallas kernels, backward_all(): pl.pallas_call(functools.partial(backward_kernel, plan, depths, peers), o...  225 us

profile of v4, /device:TPU:0, one launch (start us, length us, event | category | flops | bytes accessed | tf_op | source)
XLA Modules:
  0.0 476.7 jit_solution(7933592629862511873)
XLA Ops:
  0.7 0.8 select_reduce_fusion.2
  1.5 0.8 select_reduce_fusion.1
  2.3 0.1 select_reduce_fusion
  2.4 0.7 select_reduce_fusion.4
  3.1 0.0 copy-start
  3.2 0.0 copy-start.1
  3.2 0.6 fusion.1.refs_17_.refs_20_
  3.8 0.6 fusion.refs_15_
  4.4 1.6 copy.32.refs_12_
  6.0 0.0 copy-done
  6.0 0.0 copy-done.1
  6.0 239.2 %shard_map.264 = (bf16[4,2,4,32,3072]{4,3,2,1,0:T(8,128)(2,1)}, bf16[4,2,4,32,1024]{4,3,2,1,0:T(8,128)(2,1)}, bf16[4,2,4,32,4096]{4,3,2,1,0:T(8,128)(2,1)}, bf16...) custom-call(bf16[2,32,3072]{2,1,0:T(8,128)(2,1)} %refs_0_.1, ...), custom_call_target="tpu_custom_call" | custom-call | tf_op jit(solution)/shard_map/pallas_call | solution.py:1647
  245.2 225.1 %shard_map.265 = (f32[200,1024]{1,0:T(8,128)}, f32[2,32,3072]{2,1,0:T(8,128)}, f32[2,32,1024]{2,1,0:T(8,128)}, f32[2,32,4096]{2,1,0:T(8,128)}, f32[2,128,1024]{2...) custom-call(bf16[4,2,4,32,3072]{4,3,2,1,0:T(8,128)(2,1)} %get-tuple-, ...), custom_call_target="tpu_custom_call" | custom-call | tf_op jit(solution)/shard_map/pallas_call | solution.py:2436
  470.2 4.5 shard_map.266
  474.7 1.8 copy.33
  (2 shorter events, 0.0 us)
Async XLA Ops:
  3.1 2.8 copy-start
  3.2 2.8 copy-start.1

commit v5 on v4

--- a/solution.py
+++ b/solution.py
@@ -1304,13 +1304,13 @@
             r.small[4 + layer : 5 + layer, :] = up_b[layer : layer + 1]
 
     def make_tables():
-        count = r.table.shape[1]
+        count = r.table.shape[2]
         r.index[...] = jnp.full(r.index.shape, count, jnp.int32)
         r.index[:WIN, :WIN] = r.bias_index[...]
         for layer in range(2):
             r.wide_t[...] = jnp.full(r.wide_t.shape, NEVER, WHOLE)
-            r.wide_t[:count, :HEADS] = r.table[layer].astype(WHOLE)
-            turned = r.wide_t[...].T
+            r.wide_t[:, :count] = r.table[layer].astype(WHOLE)
+            turned = r.wide_t[...]
             order = [turned[k % 8 * GROUP + k // 8 :][:1] for k in range(HEADS)]
             r.tables[layer * HEADS : (layer + 1) * HEADS, :] = jnp.concatenate(order, axis=0).astype(LOW)
 
@@ -1619,7 +1619,7 @@
         vmem((3, 2, tall, width), LOW),
         vmem((2, tall, hidden), LOW),
         vmem((depths, 128, 512), WHOLE),
-        vmem((384, 128), WHOLE),
+        vmem((HEADS, 384), WHOLE),
         vmem((2, 3) + left[1:], LOW),
         vmem((2, 4) + left[1:], LOW),
         *[vmem(exchange, LOW)] * 6,
@@ -2212,9 +2212,7 @@
             ]
             rows = jnp.concatenate(parts, axis=1)
             order = [rows[h % GROUP * 8 + h // GROUP :][:1] for h in range(HEADS)]
-            order.append(jnp.zeros((128 - HEADS, 384), WHOLE))
-            turned = jnp.concatenate(order, axis=0).T
-            r.o_table[layer] = turned[: r.o_table.shape[1], :HEADS]
+            r.o_table[layer] = jnp.concatenate(order, axis=0)[:, : r.o_table.shape[2]]
 
     def note(work, *what):
         work(*what)
@@ -2232,7 +2230,7 @@
         zero = jnp.zeros((256 - tall, right.shape[1]), LOW)
         right[tall:256, :] = zero
         right[256 + tall : 512, :] = zero
-    r.index[...] = jnp.full(r.index.shape, r.o_table.shape[1], jnp.int32)
+    r.index[...] = jnp.full(r.index.shape, r.o_table.shape[2], jnp.int32)
     r.index[:WIN, :WIN] = r.bias_index[...]
     r.small_mine[...] = jnp.zeros(r.small_mine.shape, WHOLE)
     pump()
@@ -2373,7 +2371,7 @@
         shape((2, unit), WHOLE),
         shape((2, 4 * unit), WHOLE),
         shape((2, unit), WHOLE),
-        shape((2, buckets, HEADS), WHOLE),
+        shape((2, HEADS, buckets), WHOLE),
     ]
     scratch = [
         vmem((count, 16, 128), WHOLE),
@@ -2528,7 +2526,7 @@
         (norm_gain, norm_shift, qv_bias, proj_bias, up_bias, down_bias),
         patches,
         out_grad,
-        rel_table,
+        rel_table.transpose(0, 2, 1),
         bias_index,
         region,
         moves,
@@ -2567,7 +2565,9 @@
         grad_down,
         down_b_grad,
     )
-    return tuple(copy_out(results))
+    results = list(copy_out(results))
+    results[6] = results[6].transpose(0, 2, 1)
+    return tuple(results)
 
 
 def solution(mesh):

time: 484 us -> 480 us (level)
  no operation moved by 1% of the time
where the time goes in v5:
time: 480 us; the launch traced here: 473 us
  Pallas kernels  468 us (98%)
    pallas_call x1, Pallas kernels, forward_all(): pl.pallas_call(functools.partial(forward_kernel, chunks, depths, peers),...  239 us
    pallas_call x1, Pallas kernels, backward_all(): pl.pallas_call(functools.partial(backward_kernel, plan, depths, peers), o...  225 us

profile of v5, /device:TPU:0, one launch (start us, length us, event | category | flops | bytes accessed | tf_op | source)
XLA Modules:
  0.0 472.7 jit_solution(18139586011429389132)
XLA Ops:
  0.7 0.8 select_reduce_fusion.2
  1.5 0.8 select_reduce_fusion.1
  2.3 0.1 select_reduce_fusion
  2.4 0.7 select_reduce_fusion.4
  3.1 0.0 copy-start
  3.2 0.0 copy-start.1
  3.2 0.6 fusion.1.refs_17_.refs_20_
  3.8 0.6 fusion.refs_15_
  4.4 0.0 copy-done
  4.4 0.0 copy-done.1
  4.4 239.1 %shard_map.264 = (bf16[4,2,4,32,3072]{4,3,2,1,0:T(8,128)(2,1)}, bf16[4,2,4,32,1024]{4,3,2,1,0:T(8,128)(2,1)}, bf16[4,2,4,32,4096]{4,3,2,1,0:T(8,128)(2,1)}, bf16...) custom-call(bf16[2,32,3072]{2,1,0:T(8,128)(2,1)} %refs_0_.1, ...), custom_call_target="tpu_custom_call" | custom-call | tf_op jit(solution)/shard_map/pallas_call | solution.py:1647
  243.5 224.8 %shard_map.265 = (f32[200,1024]{1,0:T(8,128)}, f32[2,32,3072]{2,1,0:T(8,128)}, f32[2,32,1024]{2,1,0:T(8,128)}, f32[2,32,4096]{2,1,0:T(8,128)}, f32[2,128,1024]{2...) custom-call(bf16[4,2,4,32,3072]{4,3,2,1,0:T(8,128)(2,1)} %get-tuple-, ...), custom_call_target="tpu_custom_call" | custom-call | tf_op jit(solution)/shard_map/pallas_call | solution.py:2434
  468.3 4.2 shard_map.266
  (2 shorter events, 0.0 us)
Async XLA Ops:
  3.1 1.2 copy-start
  3.2 1.2 copy-start.1
